TPU v7x, 32 devices: a whole 2x2x4 slice. The times are simulated.
32 devices in a mesh: blk: 4 (over z), str: 8 (over y, x, core).
Axes of the slice: x: 2, y: 2, z: 4, core: 2. Of those that a mesh axis runs over, the one named last changes fastest.
Arguments:
- civec: bfloat16 [2048, 1024], P(('blk', 'str')), may hold values from -6 to 6
- beta_index: int32 [2, 50, 1024], replicated, may hold values from 0 to 1023
- beta_sign: int32 [2, 50, 1024], replicated, may hold values from -1 to 1
- alpha_index: int32 [2, 50, 2048], replicated, may hold values from 0 to 511
- alpha_sign: int32 [2, 50, 2048], replicated, may hold values from -1 to 1
- integrals: bfloat16 [2, 50, 50], replicated, may hold values from -0.078125 to 0.078125
- beta_operator: bfloat16 [1024, 1024], replicated, may hold values from -0.1875 to 0.1875
- alpha_operator: bfloat16 [2048, 512], P(('blk', 'str')), may hold values from -0.25 to 0.25
Outputs:
- sigma_out: float32 [2048, 1024], P(('blk', 'str'))
All inputs are finite; a program needn't handle non-finite values.
Results may differ from a plain program's by a relative error of at most 0.0013.
Values may be sent and summed in bfloat16 or wider, within the bound.
No kernel may reach another device: no remote copies, remote signals or barrier semaphores. Data moves between devices by JAX's collectives and lax.ppermute only.
A program may use at most 128 MiB of HBM per device.

v0:
```python
import jax
import jax.numpy as jnp
from jax import lax
from jax.sharding import PartitionSpec as P


def swapped(block, axis, distance):
    count = lax.axis_size(axis)
    route = []
    for low in range(count):
        high = low | 1 << distance
        if high != low and high < count:
            route += [(low, high), (high, low)]
    return lax.ppermute(block, axis, route)


def couple_rows(images, row_index, row_sign):
    row_count = row_index.shape[1]
    row_width = 256
    positions = jnp.arange(images.shape[1], dtype=jnp.int32)
    starts = jnp.arange(row_count // row_width, dtype=jnp.int32) * row_width
    sign_values = row_sign.astype(jnp.bfloat16)

    def row_block(start):
        block_index = lax.dynamic_slice_in_dim(row_index, start, row_width, 1)
        block_sign = lax.dynamic_slice_in_dim(sign_values, start, row_width, 1)
        selector = jnp.where(
            block_index[:, :, None] == positions[None, None, :],
            block_sign[:, :, None],
            jnp.zeros((), jnp.bfloat16),
        )
        return jnp.einsum("par,prc->ac", selector, images, preferred_element_type=jnp.float32)

    blocks = lax.map(row_block, starts)
    return blocks.reshape(row_count, images.shape[2])


def beta_images(rows, index_one, sign_one, integral_one):
    beta_count = rows.shape[1]
    col_width = 128
    starts = jnp.arange(beta_count // col_width, dtype=jnp.int32) * col_width
    positions = jnp.arange(beta_count, dtype=jnp.int32)

    def column_block(start):
        column_index = lax.dynamic_slice_in_dim(index_one, start, col_width, 1)
        column_sign = lax.dynamic_slice_in_dim(sign_one, start, col_width, 1)
        selector = jnp.where(
            positions[None, :, None] == column_index[:, None, :],
            column_sign[:, None, :],
            jnp.zeros((), jnp.bfloat16),
        )
        coupled = jnp.einsum(
            "ac,pcw->paw", rows, selector, preferred_element_type=jnp.float32
        ).astype(jnp.bfloat16)
        return jnp.einsum(
            "qp,paw->qaw", integral_one, coupled, preferred_element_type=jnp.float32
        ).astype(jnp.bfloat16)

    blocks = lax.map(column_block, starts)
    pair_count, row_count = (blocks.shape[1], blocks.shape[2])
    return blocks.transpose(1, 2, 0, 3).reshape(pair_count, row_count, beta_count)


def row_lists(alpha_index, alpha_sign, symmetry, start, count):
    first = jnp.asarray(start, jnp.int32)
    return (
        lax.dynamic_slice_in_dim(alpha_index[symmetry], first, count, 1),
        lax.dynamic_slice_in_dim(alpha_sign[symmetry], first, count, 1),
    )


def local(
    civec, beta_index, beta_sign, alpha_index, alpha_sign, integrals, beta_operator, alpha_operator
):
    classes = integrals.shape[0]
    pair_count = integrals.shape[1]
    local_rows, beta_count = civec.shape
    block_rows = local_rows * lax.axis_size("str")
    block_place = lax.axis_index("blk")
    sign_columns = beta_sign.astype(jnp.bfloat16)
    images = jnp.stack(
        [
            beta_images(civec, beta_index[symmetry], sign_columns[symmetry], integrals[symmetry])
            for symmetry in range(classes)
        ]
    )
    stacked = images.reshape(classes * pair_count, local_rows, beta_count)
    received = lax.all_to_all(stacked, "str", split_axis=2, concat_axis=1, tiled=True)
    received = received.reshape(classes, pair_count, received.shape[1], received.shape[2])
    block_sigma = jnp.zeros((received.shape[2], received.shape[3]), jnp.float32)
    for symmetry in range(classes):
        partner_place = jnp.bitwise_xor(block_place, 1 << symmetry)
        far_index, far_sign = row_lists(
            alpha_index, alpha_sign, symmetry, partner_place * block_rows, block_rows
        )
        partner_term = couple_rows(received[symmetry], far_index, far_sign)
        block_sigma = block_sigma + swapped(partner_term, "blk", symmetry)
    returned = lax.all_to_all(block_sigma, "str", split_axis=0, concat_axis=1, tiled=True)
    sigma_out = returned + jnp.dot(civec, beta_operator, preferred_element_type=jnp.float32)
    return sigma_out + jnp.dot(
        alpha_operator,
        lax.all_gather(civec, "str", axis=0, tiled=True),
        preferred_element_type=jnp.float32,
    )


def solution(mesh):
    placed = (P(("blk", "str"), None), P(), P(), P(), P(), P(), P(), P(("blk", "str"), None))
    return jax.shard_map(
        local, mesh=mesh, in_specs=placed, out_specs=P(("blk", "str"), None), check_vma=False
    )
```

profile of v0, /device:TPU:0, one launch (start us, length us, event | category | flops | bytes accessed | tf_op | source)
XLA Modules:
  0.0 518.0 jit_solution(8867375041171246759)
XLA Ops:
  10.3 3.9 broadcast.26.clone.1
  14.2 56.2 %while.44 = (s32[]{:T(128)}, bf16[8,50,64,128]{3,1,2,0:T(8,128)(2,1)}, s32[8]{0:T(128)S(1)}, s32[50,1024]{1,0:T(8,128)S(1)}, bf16[50,1024]{1,0:T(8,128)(2,1)S(1)...) while((s32[]{:T(128)}, ...), condition=%wide.region_1.2_spmd.clone, body=%wide.region_0.1_spmd.clone.sunk | while | flops 893747200 | bytes 2807843 | solution.py:59
  17.1 2.5 fusion.108
  24.1 2.5 fusion.108
  26.5 1.7 fusion.109
  31.1 2.5 fusion.108
  33.6 1.7 fusion.109
  38.1 2.5 fusion.108
  45.2 2.5 fusion.108
  52.2 2.5 fusion.108
  54.6 1.7 fusion.109
  59.2 2.5 fusion.108
  66.2 2.5 fusion.108
  70.4 10.1 %copy.69 = bf16[50,64,8,128]{3,2,1,0:T(8,128)(2,1)} copy(bf16[50,64,8,128]{3,0,1,2:T(8,128)(2,1)} %bitcast.5) | data formatting | bytes 13107200 | tf_op jit(solution)/shard_map/transpose | solution.py:61
  80.5 11.0 %stack_reshape.6 = bf16[1,50,64,1024]{3,2,1,0:T(8,128)(2,1)} reshape(bf16[50,64,8,128]{3,2,1,0:T(8,128)(2,1)} %copy.69) | data formatting | bytes 13107200 | tf_op jit(solution)/shard_map/stack;reshape | solution.py:81
  91.5 3.9 broadcast.26.clone
  95.4 56.2 %while.45 = (s32[]{:T(128)}, bf16[8,50,64,128]{3,1,2,0:T(8,128)(2,1)}, s32[8]{0:T(128)S(1)}, s32[50,1024]{1,0:T(8,128)S(1)}, bf16[50,1024]{1,0:T(8,128)(2,1)S(1)...) while((s32[]{:T(128)}, ...), condition=%wide.region_3.4_spmd.clone, body=%wide.region_2.3_spmd.clone.sunk | while | flops 893747200 | bytes 2807843 | solution.py:59
  98.2 2.5 fusion.114
  105.2 2.5 fusion.114
  107.7 1.7 fusion.115
  112.3 2.5 fusion.114
  114.7 1.7 fusion.115
  119.3 2.5 fusion.114
  126.3 2.5 fusion.114
  133.3 2.5 fusion.114
  140.3 2.5 fusion.114
  147.4 2.5 fusion.114
  151.5 10.0 %copy.72 = bf16[50,64,8,128]{3,2,1,0:T(8,128)(2,1)} copy(bf16[50,64,8,128]{3,0,1,2:T(8,128)(2,1)} %bitcast.9) | data formatting | bytes 13107200 | tf_op jit(solution)/shard_map/transpose | solution.py:61
  161.6 11.0 %stack_reshape.7 = bf16[1,50,64,1024]{3,2,1,0:T(8,128)(2,1)} reshape(bf16[50,64,8,128]{3,2,1,0:T(8,128)(2,1)} %copy.72) | data formatting | bytes 13107200 | tf_op jit(solution)/shard_map/stack;reshape | solution.py:81
  172.5 10.8 %pad_maximum_fusion = bf16[2,50,64,1024]{3,2,1,0:T(8,128)(2,1)} fusion(bf16[1,50,64,1024]{3,2,1,0:T(8,128)(2,1)} %stack_reshape.7, bf16[1,50,64,1024]{3,2,1,0:T(8,128)(2,1)} %stack_reshape.6), kind=kLoop, calls=%fused_computation.60 | loop fusion | flops 6553600 | bytes 26214400 | tf_op jit(solution)/shard_map/stack | solution.py:81
  183.3 24.1 %copy.73 = bf16[100,64,1024]{0,1,2:T(8,128)(2,1)} copy(bf16[100,64,1024]{2,1,0:T(8,128)(2,1)} %bitcast.123) | data formatting | bytes 26214400 | tf_op jit(solution)/shard_map/reshape | solution.py:87
  207.5 5.9 %all-to-all-start = ((bf16[100,64,1024]{0,1,2:T(8,128)(2,1)}), bf16[100,64,1024]{0,1,2:T(8,128)(2,1)}, u32[]{:S(2)}, u32[]{:S(2)}) async-start(bf16[100,64,1024]{0,1,2:T(8,128)(2,1)} %copy.73), calls=%async_computation | async-start | bytes 33554432 | tf_op jit(solution)/shard_map/all_to_all | solution.py:88
  214.9 2.2 fusion.74
  217.2 185.0 %all-to-all-done = bf16[100,64,1024]{0,1,2:T(8,128)(2,1)} async-done(((bf16[100,64,1024]{0,1,2:T(8,128)(2,1)}), bf16[100,64,1024]{0,1,2:T(8,128)(2,1)}, u32[]{:S(2)}, u32[]{:S(2)}) %all-to-all-start) | async-done | bytes 13107232 | tf_op jit(solution)/shard_map/all_to_all | solution.py:88
  402.2 28.2 %copy.80 = bf16[100,64,8,128]{3,2,1,0:T(8,128)(2,1)} copy(bf16[100,64,8,128]{0,1,3,2:T(8,128)(2,1)} %bitcast.11) | data formatting | bytes 26214400 | tf_op jit(solution)/shard_map/all_to_all | solution.py:88
  430.4 8.5 %fusion.73 = (bf16[50,8,64,128]{3,1,2,0:T(8,128)(2,1)S(1)}, bf16[50,8,64,128]{3,1,2,0:T(8,128)(2,1)}) fusion(bf16[100,8,64,128]{3,1,2,0:T(8,128)(2,1)} %bitcast.122), kind=kLoop, calls=%fused_computation.82 | loop fusion | bytes 26214400 | tf_op jit(solution)/shard_map/slice | solution.py:96
  438.9 4.7 copy.78
  443.7 18.4 %while.47 = (s32[]{:T(128)}, f32[2,256,128]{2,1,0:T(8,128)S(1)}, s32[2]{0:T(128)S(1)}, s32[50,512]{1,0:T(8,128)S(1)}, bf16[50,512]{1,0:T(8,128)(2,1)S(1)}, /*ind...) while((s32[]{:T(128)}, f32[2,256,128]{2,1,0:T(8,128)S(1)}, s32[2]{0:T(128)S(1)}, ...), condition=%wide.region_7.8_spmd.clone, body=%wide.region_6.7_spmd.clone.sunk | while | flops 1690828800 | bytes 6924439 | solution.py:34
  446.1 6.7 %fusion.121 = f32[2,256,128]{2,1,0:T(8,128)S(1)} fusion(f32[2,256,128]{2,1,0:T(8,128)S(1)} %get-tuple-element.556, s32[]{:T(128)} %get-tuple-element.555, bf16[50,512,128]{2,1,0:T(8,128)(2,1)} %get-tuple-element.569, s32[50,256]{1,0:T(8,128)S(1)} %constant_dynamic-slice_fusion.26, bf16[50,256]{1,0:T(8,128)(2,1)S(1)} %constant_dynamic-slice_fusion.27), kind=kOutput, calls=%fused_computation.56.clone.1 | convolution fusion | flops 1690828800 | bytes 6770692 | tf_op jit(solution)/shard_map/while/body/eval_jaxpr/par,prc->ac/dot_general | solution.py:32
  455.4 6.7 %fusion.121 = f32[2,256,128]{2,1,0:T(8,128)S(1)} fusion(f32[2,256,128]{2,1,0:T(8,128)S(1)} %get-tuple-element.556, s32[]{:T(128)} %get-tuple-element.555, bf16[50,512,128]{2,1,0:T(8,128)(2,1)} %get-tuple-element.569, s32[50,256]{1,0:T(8,128)S(1)} %constant_dynamic-slice_fusion.26, bf16[50,256]{1,0:T(8,128)(2,1)S(1)} %constant_dynamic-slice_fusion.27), kind=kOutput, calls=%fused_computation.56.clone.1 | convolution fusion | flops 1690828800 | bytes 6770692 | tf_op jit(solution)/shard_map/while/body/eval_jaxpr/par,prc->ac/dot_general | solution.py:32
  462.1 3.5 collective-permute-start.1
  465.6 7.6 %copy.75 = bf16[50,8,64,128]{3,2,1,0:T(8,128)(2,1)} copy(bf16[50,8,64,128]{3,1,2,0:T(8,128)(2,1)} %get-tuple-element.280) | data formatting | bytes 13107200 | tf_op jit(solution)/shard_map/slice | solution.py:96
  473.2 19.2 %while.46 = (s32[]{:T(128)}, f32[2,256,128]{2,1,0:T(8,128)S(1)}, s32[2]{0:T(128)S(1)}, s32[50,512]{1,0:T(8,128)S(1)}, bf16[50,512]{1,0:T(8,128)(2,1)S(1)}, /*ind...) while((s32[]{:T(128)}, f32[2,256,128]{2,1,0:T(8,128)S(1)}, s32[2]{0:T(128)S(1)}, ...), condition=%wide.region_5.6_spmd.clone, body=%wide.region_4.5_spmd.clone.sunk | while | flops 1690828800 | bytes 6924439 | solution.py:34
  476.1 6.7 %fusion.118 = f32[2,256,128]{2,1,0:T(8,128)S(1)} fusion(f32[2,256,128]{2,1,0:T(8,128)S(1)} %get-tuple-element.529, s32[]{:T(128)} %get-tuple-element.528, bf16[50,512,128]{2,1,0:T(8,128)(2,1)} %get-tuple-element.542, s32[50,256]{1,0:T(8,128)S(1)} %constant_dynamic-slice_fusion.24, bf16[50,256]{1,0:T(8,128)(2,1)S(1)} %constant_dynamic-slice_fusion.25), kind=kOutput, calls=%fused_computation.45.clone.1 | convolution fusion | flops 1690828800 | bytes 6770692 | tf_op jit(solution)/shard_map/while/body/eval_jaxpr/par,prc->ac/dot_general | solution.py:32
  485.7 6.7 %fusion.118 = f32[2,256,128]{2,1,0:T(8,128)S(1)} fusion(f32[2,256,128]{2,1,0:T(8,128)S(1)} %get-tuple-element.529, s32[]{:T(128)} %get-tuple-element.528, bf16[50,512,128]{2,1,0:T(8,128)(2,1)} %get-tuple-element.542, s32[50,256]{1,0:T(8,128)S(1)} %constant_dynamic-slice_fusion.24, bf16[50,256]{1,0:T(8,128)(2,1)S(1)} %constant_dynamic-slice_fusion.25), kind=kOutput, calls=%fused_computation.45.clone.1 | convolution fusion | flops 1690828800 | bytes 6770692 | tf_op jit(solution)/shard_map/while/body/eval_jaxpr/par,prc->ac/dot_general | solution.py:32
  494.1 4.8 collective-permute-done
  499.6 3.4 all-to-all-start.1
  504.6 5.3 %all-to-all-done.1 = f32[8,64,128]{2,1,0:T(8,128)S(1)} async-done(((f32[8,64,128]{2,1,0:T(8,128)}), f32[8,64,128]{2,1,0:T(8,128)S(1)}, u32[]{:S(2)}, u32[]{:S(2)}) %all-to-all-start.1) | async-done | bytes 262176 | tf_op jit(solution)/shard_map/all_to_all | solution.py:98
  (106 shorter events, 45.4 us)
Async XLA Ops:
  6.5 503.4 %copy-start = (bf16[1024,1024]{1,0:T(8,128)(2,1)S(1)}, bf16[1024,1024]{1,0:T(8,128)(2,1)}, u32[]{:S(2)}) copy-start(bf16[1024,1024]{1,0:T(8,128)(2,1)} %param.22) | copy-start | bytes 6291460
  6.5 7.7 %copy-start.2 = (bf16[64,1024]{1,0:T(8,128)(2,1)S(1)}, bf16[64,1024]{1,0:T(8,128)(2,1)}, u32[]{:S(2)}) copy-start(bf16[64,1024]{1,0:T(8,128)(2,1)} %param.16) | copy-start | bytes 393220
  151.5 21.0 %copy-start.3 = (bf16[64,1024]{1,0:T(8,128)(2,1)}, bf16[64,1024]{1,0:T(8,128)(2,1)S(1)}, u32[]{:S(2)}) copy-start(bf16[64,1024]{1,0:T(8,128)(2,1)S(1)} %get-tuple-element.579) | copy-start | bytes 393220
  207.5 6.6 %copy-start.1 = (s32[2,50,2048]{2,0,1:T(2,128)S(1)}, s32[2,50,2048]{2,0,1:T(2,128)}, u32[]{:S(2)}) copy-start(s32[2,50,2048]{2,0,1:T(2,128)} %param.19) | copy-start | bytes 2457604
  207.5 194.7 %all-to-all-start = ((bf16[100,64,1024]{0,1,2:T(8,128)(2,1)}), bf16[100,64,1024]{0,1,2:T(8,128)(2,1)}, u32[]{:S(2)}, u32[]{:S(2)}) async-start(bf16[100,64,1024]{0,1,2:T(8,128)(2,1)} %copy.73), calls=%async_computation | async-start | bytes 33554432 | tf_op jit(solution)/shard_map/all_to_all | solution.py:88
  213.4 289.7 %all-gather.2.cloned.1.call-start = ((), (), s32[]{:S(2)}) async-start(), calls=%async_computation.2 | async-start | bytes 1179648 | tf_op jit(solution)/shard_map/all_gather | solution.py:102
  462.1 32.0 %collective-permute-start.1 = (f32[512,128]{1,0:T(8,128)S(1)}, f32[512,128]{1,0:T(8,128)S(1)}, u32[]{:S(2)}, u32[]{:S(2)}) collective-permute-start(f32[512,128]{1,0:T(8,128)S(1)} %bitcast.129), channel_id=1, source_target_pairs={{0,16},{16,0},{8,24},{24,8},{1,17},{17,1},{9,25},{25,9},{2,18},{18... | collective-permute-start | bytes 786440 | tf_op jit(solution)/shard_map/ppermute | solution.py:14
  473.2 36.7 %copy-start.4 = (bf16[64,1024]{1,0:T(8,128)(2,1)S(1)}, bf16[64,1024]{1,0:T(8,128)(2,1)}, u32[]{:S(2)}) copy-start(bf16[64,1024]{1,0:T(8,128)(2,1)} %copy-done.3) | copy-start | bytes 393220
  492.4 6.4 %collective-permute-start = (f32[512,128]{1,0:T(8,128)S(1)}, f32[512,128]{1,0:T(8,128)S(1)}, u32[]{:S(2)}, u32[]{:S(2)}) collective-permute-start(f32[512,128]{1,0:T(8,128)S(1)} %bitcast.128), channel_id=1, source_target_pairs={{0,8},{8,0},{16,24},{24,16},{1,9},{9,1},{17,25},{25,17},{2,10},{10... | collective-permute-start | bytes 786440 | tf_op jit(solution)/shard_map/ppermute | solution.py:14
  499.6 10.3 %all-to-all-start.1 = ((f32[8,64,128]{2,1,0:T(8,128)}), f32[8,64,128]{2,1,0:T(8,128)S(1)}, u32[]{:S(2)}, u32[]{:S(2)}) async-start(f32[8,64,128]{2,1,0:T(8,128)} %bitcast.19), calls=%async_computation.1 | async-start | bytes 524288 | tf_op jit(solution)/shard_map/all_to_all | solution.py:98
Sparse Core Ops, SparseCore 0:
  216.1 100.5 all-gather.1
where the time goes:
time: 521 us; the launch traced here: 518 us
  waiting for transfers between devices  196 us (38%)
  local copies, waits for them, and re-layouts  145 us (28%)
  matrix products  96.3 us (18%)
  loops' own time  40.2 us (8%)
  starting transfers between devices  14.4 us (3%)
  between operations  13.6 us (3%)
  other arithmetic  12.7 us (2%)
    all_to_all x1, waiting for transfers between devices, local(): lax.all_to_all(stacked, 'str', split_axis=2, concat_axis=1, tiled=True)  185 us
    dot_general x16, matrix products, column_block(): jnp.einsum('ac,pcw->paw', rows, selector, preferred_element_type=jnp.floa...  39.3 us
    another operation x2, loops' own time, beta_images(): blocks = lax.map(column_block, starts)  32.6 us
    all_to_all x1, local copies, waits for them, and re-layouts, local(): lax.all_to_all(stacked, 'str', split_axis=2, concat_axis=1, tiled=True)  28.2 us
    dot_general x16, matrix products, column_block(): jnp.einsum('qp,paw->qaw', integral_one, coupled, preferred_element_type=j...  27.3 us
    dot_general x4, matrix products, row_block(): jnp.einsum('par,prc->ac', selector, images, preferred_element_type=jnp.fl...  27 us
    reshape x1, local copies, waits for them, and re-layouts, local(): stacked = images.reshape(classes * pair_count, local_rows, beta_count)  24.1 us
    another operation x2, local copies, waits for them, and re-layouts, local(): jnp.stack([beta_images(civec, beta_index[symmetry], sign_columns[symmetry...  22 us
  transfers between devices with their start and end apart: 5, of which 3 were waited for; matrix products, arithmetic and copies ran while one was open for 16% of the time, Pallas kernels for 0%

commit v1 on v0

v1 whole, which is shorter than its diff:
```python
import functools

import jax
import jax.numpy as jnp
from jax import lax
from jax.experimental import pallas as pl
from jax.experimental.pallas import tpu as pltpu
from jax.sharding import PartitionSpec as P

QUAD = 4
STEP = 4 * QUAD
VMEM_LIMIT = 56 * 1024 * 1024


def whole():
    return pl.BlockSpec(memory_space=pltpu.VMEM)


def mixed_kernel(count, place_ref, *refs):
    pieces = refs[:count]
    onehot_ref, kron_ref, index_ref, sign_ref = refs[count : count + 4]
    outs = refs[count + 4 : 2 * count + 4]
    turned, images, total, ordered = refs[2 * count + 4 :]
    step = pl.program_id(0)
    block_rows = turned.shape[1]
    local_rows = pieces[0].shape[0]
    halves = images.shape[0]
    group = kron_ref.shape[0]

    @pl.when(step == 0)
    def _():
        for at in range(0, count, 2):
            both = jnp.concatenate([pieces[at][...], pieces[at + 1][...]], axis=0)
            turned[:, at * local_rows : (at + 2) * local_rows] = both.T

    coupled = jnp.dot(onehot_ref[...], turned[...], preferred_element_type=jnp.float32)
    coupled = coupled.astype(jnp.bfloat16)
    low = lax.broadcasted_iota(jnp.int32, (halves, 8, block_rows), 1) < QUAD
    evens, odds = [], []
    for pair in range(2):
        first, second = [
            jnp.dot(
                kron_ref[...],
                coupled[at * group : (at + 1) * group],
                preferred_element_type=jnp.float32,
            ).reshape(halves, 8, block_rows)
            for at in (2 * pair, 2 * pair + 1)
        ]
        evens.append(jnp.where(low, first, pltpu.roll(second, QUAD, 1)))
        odds.append(jnp.where(low, pltpu.roll(first, QUAD, 1), second))
    rows = pl.ds(pl.multiple_of(step * STEP, STEP), STEP)
    images[:, 0, rows, :] = jnp.concatenate(evens, axis=1).astype(jnp.bfloat16)
    images[:, 1, rows, :] = jnp.concatenate(odds, axis=1).astype(jnp.bfloat16)

    @pl.when(step == pl.num_programs(0) - 1)
    def _():
        total[...] = jnp.zeros_like(total)
        position = lax.broadcasted_iota(jnp.int32, (block_rows, block_rows), 0)

        def body(half, carry):
            terms = []
            for side in range(2):
                pair = 2 * half + side
                selector = jnp.where(
                    position == index_ref[pl.ds(pair, 1), :], sign_ref[pl.ds(pair, 1), :], 0.0
                ).astype(jnp.bfloat16)
                terms.append(
                    jnp.dot(images[half, side], selector, preferred_element_type=jnp.float32)
                )
            total[...] += terms[0] + terms[1]
            return carry

        lax.fori_loop(0, halves, body, 0)
        ordered[...] = total[...].T
        for at in range(count):
            start = pl.multiple_of((place_ref[0] ^ at) * local_rows, local_rows)
            outs[at][...] = ordered[pl.ds(start, local_rows), :]


def mixed_pieces(place, pieces, onehot, kron, index, sign, window):
    count = len(pieces)
    local_rows, beta_count = pieces[0].shape
    pair_count, block_rows = index.shape
    steps = window // STEP
    rows = pair_count * STEP
    flops = 2 * window * pair_count * block_rows * (beta_count + pair_count * QUAD + block_rows)
    return pl.pallas_call(
        functools.partial(mixed_kernel, count),
        out_shape=[jax.ShapeDtypeStruct((local_rows, window), jnp.float32)] * count,
        grid_spec=pltpu.PrefetchScalarGridSpec(
            num_scalar_prefetch=1,
            grid=(steps,),
            in_specs=[whole()] * count
            + [pl.BlockSpec((rows, beta_count), lambda i, place_ref: (i, 0))]
            + [whole()] * 3,
            out_specs=[whole()] * count,
            scratch_shapes=[
                pltpu.VMEM((beta_count, block_rows), jnp.bfloat16),
                pltpu.VMEM((pair_count // 2, 2, window, block_rows), jnp.bfloat16),
                pltpu.VMEM((window, block_rows), jnp.float32),
                pltpu.VMEM((block_rows, window), jnp.float32),
            ],
        ),
        compiler_params=pltpu.CompilerParams(
            dimension_semantics=("arbitrary",), vmem_limit_bytes=VMEM_LIMIT
        ),
        cost_estimate=pl.CostEstimate(
            flops=flops, bytes_accessed=2 * onehot.size, transcendentals=0
        ),
        name="mixed",
    )(place, *pieces, onehot, kron, index, sign)


def plain_kernel(count, place_ref, *refs):
    pieces = refs[:count]
    alpha_ref, beta_ref, out_ref, block = refs[count:]
    local_rows = pieces[0].shape[0]
    for at in range(count):
        start = pl.multiple_of((place_ref[0] ^ at) * local_rows, local_rows)
        block[pl.ds(start, local_rows), :] = pieces[at][...]
    out_ref[...] = jnp.dot(
        alpha_ref[...], block[...], preferred_element_type=jnp.float32
    ) + jnp.dot(pieces[0][...], beta_ref[...], preferred_element_type=jnp.float32)


def plain_terms(place, pieces, alpha_operator, beta_operator):
    count = len(pieces)
    local_rows, beta_count = pieces[0].shape
    block_rows = alpha_operator.shape[1]
    return pl.pallas_call(
        functools.partial(plain_kernel, count),
        out_shape=jax.ShapeDtypeStruct((local_rows, beta_count), jnp.float32),
        in_specs=[pl.BlockSpec(memory_space=pltpu.SMEM)] + [whole()] * (count + 2),
        out_specs=whole(),
        scratch_shapes=[pltpu.VMEM((block_rows, beta_count), jnp.bfloat16)],
        compiler_params=pltpu.CompilerParams(vmem_limit_bytes=VMEM_LIMIT),
        cost_estimate=pl.CostEstimate(
            flops=2 * local_rows * beta_count * (beta_count + block_rows),
            bytes_accessed=2 * beta_count * (beta_count + block_rows),
            transcendentals=0,
        ),
        name="plain",
    )(place, *pieces, alpha_operator, beta_operator)


def add_kernel(count, classes, place_ref, base_ref, *refs):
    terms, out_ref = refs[:count], refs[count]
    window = terms[0].shape[1]
    chunk = place_ref[0] // classes
    for at in range(0, count, classes):
        start = pl.multiple_of((chunk ^ (at // classes)) * window, window)
        columns = pl.ds(start, window)
        value = base_ref[:, columns]
        for other in range(classes):
            value = value + terms[at + other][...]
        out_ref[:, columns] = value


def add_terms(place, base, terms, classes):
    count = len(terms)
    return pl.pallas_call(
        functools.partial(add_kernel, count, classes),
        out_shape=jax.ShapeDtypeStruct(base.shape, jnp.float32),
        in_specs=[pl.BlockSpec(memory_space=pltpu.SMEM)] + [whole()] * (count + 1),
        out_specs=whole(),
        compiler_params=pltpu.CompilerParams(vmem_limit_bytes=VMEM_LIMIT),
        name="add",
    )(place, base, *terms)


def local(
    civec, beta_index, beta_sign, alpha_index, alpha_sign, integrals, beta_operator, alpha_operator
):
    classes, pair_count = integrals.shape[:2]
    local_rows, beta_count = civec.shape
    count = lax.axis_size("str")
    blocks = lax.axis_size("blk")
    block_rows = local_rows * count
    window = beta_count * classes // count
    quads = window // QUAD
    block_at, place = lax.axis_index("blk"), lax.axis_index("str")
    symmetry, chunk = place % classes, place // classes
    scalar_place = place.astype(jnp.int32).reshape(1)

    def near(array, distance):
        route = [
            (blk * count + at, blk * count + (at ^ distance))
            for blk in range(blocks)
            for at in range(count)
        ]
        return lax.ppermute(array, ("blk", "str"), route)

    def far(array, distance):
        route = [
            (blk * count + at, (blk ^ (1 << at % classes)) * count + (at ^ distance))
            for blk in range(blocks)
            for at in range(count)
        ]
        return lax.ppermute(array, ("blk", "str"), route)

    straight = [civec] + [near(civec, at) for at in range(2, count, 2)]
    crossed = [near(piece, 1) for piece in straight]
    pieces = [piece for two in zip(straight, crossed) for piece in two]

    def one_class(array, start, width):
        return lax.dynamic_slice(array, (symmetry, 0, start), (1, array.shape[1], width))[0]

    def by_quad(array):
        part = one_class(array, chunk * window, window).reshape(pair_count, quads, QUAD)
        return part.transpose(1, 0, 2).reshape(pair_count * window, 1)

    positions = jnp.arange(beta_count, dtype=jnp.int32)[None, :]
    onehot = jnp.where(by_quad(beta_index) == positions, by_quad(beta_sign), 0).astype(jnp.bfloat16)
    same = jnp.eye(QUAD, dtype=jnp.bfloat16)
    own_integrals = lax.dynamic_index_in_dim(integrals, symmetry, 0, keepdims=False)
    kron = (own_integrals[:, None, :, None] * same[None, :, None, :]).reshape(
        pair_count * QUAD, pair_count * QUAD
    )
    partner = jnp.bitwise_xor(block_at, 1 << symmetry)
    index = one_class(alpha_index, partner * block_rows, block_rows)
    index = jnp.bitwise_xor(index // local_rows, place) * local_rows + index % local_rows
    sign = one_class(alpha_sign, partner * block_rows, block_rows).astype(jnp.float32)

    sent = mixed_pieces(scalar_place, pieces, onehot, kron, index, sign, window)
    terms = [far(sent[at], at) for at in range(count)]
    base = plain_terms(scalar_place, pieces, alpha_operator, beta_operator)
    return add_terms(scalar_place, base, terms, classes)


def solution(mesh):
    placed = (P(("blk", "str"), None), P(), P(), P(), P(), P(), P(), P(("blk", "str"), None))
    return jax.shard_map(
        local, mesh=mesh, in_specs=placed, out_specs=P(("blk", "str"), None), check_vma=False
    )
```

time: 521 us -> 87.3 us (0.17)
  waiting for transfers between devices: 196 us -> 3.27 us
  local copies, waits for them, and re-layouts: 145 us -> 9.14 us
  matrix products: 96.3 us -> 0 us
  Pallas kernels: 0 us -> 41.4 us
  loops' own time: 40.2 us -> 0 us
  between operations: 13.6 us -> 0.17 us
    all_to_all x2 -> x0, waiting for transfers between devices: 190 us -> none  [the longest x1 185 us: local(): lax.all_to_all(stacked, 'str', split_axis=2, concat_axis=1, tiled=True)]
    dot_general x38 -> x0, matrix products: 96.3 us -> none  [the longest x16 39.3 us: column_block(): jnp.einsum('ac,pcw->paw', rows, selector, preferred_element_type=jnp.floa...]
    pallas_call x0 -> x3, Pallas kernels: none -> 41.4 us  [the longest x1 36.1 us: mixed_pieces(): pl.pallas_call(functools.partial(mixed_kernel, count), out_shape=[jax.Sha...]
    another operation x4 -> x0, loops' own time: 40.2 us -> none  [the longest x2 32.6 us: beta_images(): blocks = lax.map(column_block, starts)]
    another operation x6 -> x0, local copies, waits for them, and re-layouts: 29.8 us -> none  [the longest x2 22 us: local(): jnp.stack([beta_images(civec, beta_index[symmetry], sign_columns[symmetry...]
    all_to_all x1 -> x0, local copies, waits for them, and re-layouts: 28.2 us -> none  [local(): lax.all_to_all(stacked, 'str', split_axis=2, concat_axis=1, tiled=True)]
    slice x7 -> x0, local copies, waits for them, and re-layouts: 26.2 us -> none  [the longest x3 20.9 us: local(): partner_term = couple_rows(received[symmetry], far_index, far_sign)]
    reshape x1 -> x0, local copies, waits for them, and re-layouts: 24.1 us -> none  [local(): stacked = images.reshape(classes * pair_count, local_rows, beta_count)]
  transfers between devices with their start and end apart: 5 -> 15, of which waited for: 3 -> 4; matrix products, arithmetic and copies ran while one was open for 16% -> 25% of each run, Pallas kernels for 0% -> 4%
where the time goes in v1:
time: 87.3 us; the launch traced here: 86.8 us
  Pallas kernels  41.4 us (47%)
  starting transfers between devices  18.5 us (21%)
  other arithmetic  14.3 us (16%)
  local copies, waits for them, and re-layouts  9.14 us (10%)
  waiting for transfers between devices  3.27 us (4%)
    pallas_call x1, Pallas kernels, mixed_pieces(): pl.pallas_call(functools.partial(mixed_kernel, count), out_shape=[jax.Sha...  36.1 us
    ppermute x8, starting transfers between devices, far(): return lax.ppermute(array, ('blk', 'str'), route)  12.9 us
    convert_element_type x1, other arithmetic, local(): jnp.where(by_quad(beta_index) == positions, by_quad(beta_sign), 0)  12.4 us
    ppermute x7, starting transfers between devices, near(): return lax.ppermute(array, ('blk', 'str'), route)  5.54 us
    pallas_call x1, Pallas kernels, plain_terms(): pl.pallas_call(functools.partial(plain_kernel, count), out_shape=jax.Shap...  3.43 us
    ppermute x8, waiting for transfers between devices, far(): return lax.ppermute(array, ('blk', 'str'), route)  3.02 us
    dynamic_slice x4, local copies, waits for them, and re-layouts, one_class(): lax.dynamic_slice(array, (symmetry, 0, start), (1, array.shape[1], width))  2.97 us
    mul x1, local copies, waits for them, and re-layouts, local(): own_integrals[:, None, :, None] * same[None, :, None, :]  2.2 us
  transfers between devices with their start and end apart: 15, of which 4 were waited for; matrix products, arithmetic and copies ran while one was open for 25% of the time, Pallas kernels for 4%

profile of v1, /device:TPU:0, one launch (start us, length us, event | category | flops | bytes accessed | tf_op | source)
XLA Modules:
  0.0 86.8 jit_solution(16891750428151981377)
XLA Ops:
  0.0 3.9 %collective-permute-start.5 = (bf16[64,1024]{1,0:T(8,128)(2,1)}, bf16[64,1024]{1,0:T(8,128)(2,1)S(1)}, u32[]{:S(2)}, u32[]{:S(2)}) collective-permute-start(bf16[64,1024]{1,0:T(8,128)(2,1)} %refs_0_.3), channel_id=1, source_target_pairs={{0,6},{1,7},{2,4},{3,5},{4,2},{5,3},{6,0},{7,1},{8,14},{9,15},{10,... | collective-permute-start | bytes 393224 | tf_op jit(solution)/shard_map/ppermute | solution.py:191
  3.9 0.5 collective-permute-start.3
  4.4 0.1 collective-permute-start.1
  4.5 0.0 collective-permute-start
  4.6 1.2 %constant_dynamic-slice_fusion.3 = (s32[1,50,256]{2,0,1:T(1,128)S(1)}, s32[1,50,256]{2,0,1:T(1,128)S(1)}) fusion(s32[2,50,1024]{2,0,1:T(2,128)} %param.10, s32[]{:T(128)S(6)} %select_n.43, s32[]{:T(128)S(6)} %select_n.45, s32[2,50,1024]{2,0,1:T(2,128)} %param.9), kind=kLoop, calls=%fused_computation.25 | loop fusion | bytes 204808 | tf_op jit(solution)/shard_map/dynamic_slice | solution.py:206
  5.8 0.1 copy.12
  6.0 0.1 copy.10
  6.1 0.8 copy.11
  6.8 0.6 eq.26
  7.4 0.8 copy.13
  8.1 0.6 broadcast_in_dim.17
  8.7 0.4 broadcast_multiply_fusion
  9.1 2.2 %mul.36.refs_9_ = bf16[200,200]{1,0:T(8,128)(2,1)} reshape(bf16[50,4,50,4]{3,2,1,0:T(8,128)(2,1)S(1)} %broadcast_multiply_fusion) | data formatting | bytes 160000 | tf_op jit(solution)/shard_map/mul | solution.py:216
  11.3 12.4 %select_convert_fusion.refs_8_ = bf16[12800,1024]{1,0:T(8,128)(2,1)} fusion(s32[12800]{0:T(1024)S(1)} %broadcast_in_dim.17, s32[12800]{0:T(1024)S(1)} %eq.26), kind=kLoop, calls=%fused_computation | loop fusion | flops 39321600 | bytes 26316800 | tf_op jit(solution)/shard_map/convert_element_type | solution.py:213
  23.8 1.5 %constant_dynamic-slice_fusion = (s32[1,50,512]{2,0,1:T(1,128)S(1)}, s32[1,50,512]{2,0,1:T(1,128)S(1)}) fusion(s32[2,50,2048]{2,0,1:T(2,128)} %param.12, s32[]{:T(128)S(6)} %select_n.43, s32[]{:T(128)S(6)} %select_n.47, s32[2,50,2048]{2,0,1:T(2,128)} %param.11), kind=kLoop, calls=%fused_computation.22 | loop fusion | bytes 409608 | tf_op jit(solution)/shard_map/dynamic_slice | solution.py:206
  25.3 0.7 fusion.3.refs_11_
  25.9 0.0 collective-permute-done.5.refs_6_
  25.9 0.5 collective-permute-start.6
  26.4 0.0 collective-permute-done.3.refs_4_
  26.5 0.1 collective-permute-start.4
  26.5 0.0 collective-permute-done.1.refs_2_
  26.5 0.4 collective-permute-start.2
  27.0 0.8 fusion.2.refs_10_
  27.7 0.0 collective-permute-done.refs_1_
  27.7 0.0 collective-permute-done.6.refs_7_
  27.7 0.1 collective-permute-done.4.refs_5_
  27.8 0.2 collective-permute-done.2.refs_3_
  28.0 0.4 copy-done.4
  28.4 0.0 copy-done.5
  28.4 0.0 copy-done.6
  28.5 0.2 copy-done.7
  28.6 36.1 %mixed.1 = (f32[64,256]{1,0:T(8,128)}, f32[64,256]{1,0:T(8,128)}, f32[64,256]{1,0:T(8,128)}, f32[64,256]{1,0:T(8,128)}, f32[64,256]{1,0:T(8,128)}, /*index=5*/f3...) custom-call(s32[1]{0:T(128)} %bitcast.place_ref, bf16[64,1024]{1,0:T(8,128)(2,1)} %refs_0_.3, ...), custom_call_target="tpu_custom_call" | custom-call | flops 22754099200 | bytes 26214400 | tf_op jit(solution)/shard_map/mixed/pallas_call | solution.py:87
  64.7 2.0 %collective-permute-start.7 = (f32[64,256]{1,0:T(8,128)}, f32[64,256]{1,0:T(8,128)S(1)}, u32[]{:S(2)}, u32[]{:S(2)}) collective-permute-start(f32[64,256]{1,0:T(8,128)} %get-tuple-element.13), channel_id=1, source_target_pairs={{0,8},{1,17},{2,10},{3,19},{4,12},{5,21},{6,14},{7,23},{8,0},{9,25... | collective-permute-start | bytes 196616 | tf_op jit(solution)/shard_map/ppermute | solution.py:199
  66.8 2.2 %collective-permute-start.8 = (f32[64,256]{1,0:T(8,128)}, f32[64,256]{1,0:T(8,128)S(1)}, u32[]{:S(2)}, u32[]{:S(2)}) collective-permute-start(f32[64,256]{1,0:T(8,128)} %get-tuple-element.14), channel_id=1, source_target_pairs={{0,9},{1,16},{2,11},{3,18},{4,13},{5,20},{6,15},{7,22},{8,1},{9,24... | collective-permute-start | bytes 196616 | tf_op jit(solution)/shard_map/ppermute | solution.py:199
  69.0 1.4 %collective-permute-start.9 = (f32[64,256]{1,0:T(8,128)}, f32[64,256]{1,0:T(8,128)S(1)}, u32[]{:S(2)}, u32[]{:S(2)}) collective-permute-start(f32[64,256]{1,0:T(8,128)} %get-tuple-element.15), channel_id=1, source_target_pairs={{0,10},{1,19},{2,8},{3,17},{4,14},{5,23},{6,12},{7,21},{8,2},{9,27... | collective-permute-start | bytes 196616 | tf_op jit(solution)/shard_map/ppermute | solution.py:199
  70.4 0.0 collective-permute-start.10
  70.5 2.6 %collective-permute-start.11 = (f32[64,256]{1,0:T(8,128)}, f32[64,256]{1,0:T(8,128)S(1)}, u32[]{:S(2)}, u32[]{:S(2)}) collective-permute-start(f32[64,256]{1,0:T(8,128)} %get-tuple-element.17), channel_id=1, source_target_pairs={{0,12},{1,21},{2,14},{3,23},{4,8},{5,17},{6,10},{7,19},{8,4},{9,29... | collective-permute-start | bytes 196616 | tf_op jit(solution)/shard_map/ppermute | solution.py:199
  73.0 0.0 collective-permute-done.7.refs_0_
  73.0 2.2 %collective-permute-start.12 = (f32[64,256]{1,0:T(8,128)}, f32[64,256]{1,0:T(8,128)S(1)}, u32[]{:S(2)}, u32[]{:S(2)}) collective-permute-start(f32[64,256]{1,0:T(8,128)} %get-tuple-element.18), channel_id=1, source_target_pairs={{0,13},{1,20},{2,15},{3,22},{4,9},{5,16},{6,11},{7,18},{8,5},{9,28... | collective-permute-start | bytes 196616 | tf_op jit(solution)/shard_map/ppermute | solution.py:199
  75.2 0.0 collective-permute-done.8.refs_1_
  75.2 2.3 %collective-permute-start.13 = (f32[64,256]{1,0:T(8,128)}, f32[64,256]{1,0:T(8,128)S(1)}, u32[]{:S(2)}, u32[]{:S(2)}) collective-permute-start(f32[64,256]{1,0:T(8,128)} %get-tuple-element.19), channel_id=1, source_target_pairs={{0,14},{1,23},{2,12},{3,21},{4,10},{5,19},{6,8},{7,17},{8,6},{9,31... | collective-permute-start | bytes 196616 | tf_op jit(solution)/shard_map/ppermute | solution.py:199
  77.5 0.2 collective-permute-start.14
  77.7 3.4 %plain.1.base_ref = f32[64,1024]{1,0:T(8,128)} custom-call(s32[1]{0:T(128)} %bitcast.place_ref, bf16[64,1024]{1,0:T(8,128)(2,1)} %refs_0_.3, bf16[64,1024]{1,0:T(8,128)(2,1)} %copy-done.4, bf16[64,1024]{1,0:T(8,128)(2,1)} %copy-done.3, bf16[64,1024]{1,0:T(8,128)(2,1)} %copy-done.7, bf16[64,1024]{1,0:T(8,128)(2,1)} %copy-done.2, bf16[64,1024]{1,0:T(8,128)(2,1)} %copy-done.6, ...), custom_call_target="tpu_custom_call" | custom-call | flops 201326592 | bytes 3145728 | tf_op jit(solution)/shard_map/plain/pallas_call | solution.py:130
  81.2 0.0 collective-permute-done.11.refs_4_
  81.2 0.6 collective-permute-done.13.refs_6_
  81.8 2.4 %collective-permute-done.14.refs_7_ = f32[64,256]{1,0:T(8,128)S(1)} collective-permute-done((f32[64,256]{1,0:T(8,128)}, f32[64,256]{1,0:T(8,128)S(1)}, u32[]{:S(2)}, u32[]{:S(2)}) %collective-permute-start.14) | collective-permute-done | bytes 65568 | tf_op jit(solution)/shard_map/ppermute | solution.py:199
  84.3 0.6 copy-done.15
  84.9 1.9 %add.42 = f32[64,1024]{1,0:T(8,128)} custom-call(s32[1]{0:T(128)} %bitcast.place_ref, f32[64,1024]{1,0:T(8,128)} %plain.1.base_ref, f32[64,256]{1,0:T(8,128)} %copy-done.8, f32[64,256]{1,0:T(8,128)} %copy-done.9, f32[64,256]{1,0:T(8,128)} %copy-done.10, f32[64,256]{1,0:T(8,128)} %copy-done.11, f32[64,256]{1,0:T(8,128)} %copy-done.12, f32[64,256]{1,0:T(8,128)} %copy-done.13, ...), custom_call_target="tpu_custom_call" | custom-call | tf_op jit(solution)/shard_map/add/pallas_call | solution.py:161
  (33 shorter events, 0.1 us)
Async XLA Ops:
  0.0 4.5 %copy-start = (bf16[2,50,50]{2,0,1:T(2,128)(2,1)S(1)}, bf16[2,50,50]{2,0,1:T(2,128)(2,1)}, u32[]{:S(2)}) copy-start(bf16[2,50,50]{2,0,1:T(2,128)(2,1)} %param.13) | copy-start | bytes 30004
  0.0 25.9 %collective-permute-start.5 = (bf16[64,1024]{1,0:T(8,128)(2,1)}, bf16[64,1024]{1,0:T(8,128)(2,1)S(1)}, u32[]{:S(2)}, u32[]{:S(2)}) collective-permute-start(bf16[64,1024]{1,0:T(8,128)(2,1)} %refs_0_.3), channel_id=1, source_target_pairs={{0,6},{1,7},{2,4},{3,5},{4,2},{5,3},{6,0},{7,1},{8,14},{9,15},{10,... | collective-permute-start | bytes 393224 | tf_op jit(solution)/shard_map/ppermute | solution.py:191
  3.9 22.6 %collective-permute-start.3 = (bf16[64,1024]{1,0:T(8,128)(2,1)}, bf16[64,1024]{1,0:T(8,128)(2,1)S(1)}, u32[]{:S(2)}, u32[]{:S(2)}) collective-permute-start(bf16[64,1024]{1,0:T(8,128)(2,1)} %refs_0_.3), channel_id=1, source_target_pairs={{0,4},{1,5},{2,6},{3,7},{4,0},{5,1},{6,2},{7,3},{8,12},{9,13},{10,... | collective-permute-start | bytes 393224 | tf_op jit(solution)/shard_map/ppermute | solution.py:191
  4.4 22.1 %collective-permute-start.1 = (bf16[64,1024]{1,0:T(8,128)(2,1)}, bf16[64,1024]{1,0:T(8,128)(2,1)S(1)}, u32[]{:S(2)}, u32[]{:S(2)}) collective-permute-start(bf16[64,1024]{1,0:T(8,128)(2,1)} %refs_0_.3), channel_id=1, source_target_pairs={{0,2},{1,3},{2,0},{3,1},{4,6},{5,7},{6,4},{7,5},{8,10},{9,11},{10,... | collective-permute-start | bytes 393224 | tf_op jit(solution)/shard_map/ppermute | solution.py:191
  4.5 23.2 %collective-permute-start = (bf16[64,1024]{1,0:T(8,128)(2,1)}, bf16[64,1024]{1,0:T(8,128)(2,1)S(1)}, u32[]{:S(2)}, u32[]{:S(2)}) collective-permute-start(bf16[64,1024]{1,0:T(8,128)(2,1)} %refs_0_.3), channel_id=1, source_target_pairs={{0,1},{1,0},{2,3},{3,2},{4,5},{5,4},{6,7},{7,6},{8,9},{9,8},{10,11... | collective-permute-start | bytes 393224 | tf_op jit(solution)/shard_map/ppermute | solution.py:191
  25.9 2.1 %copy-start.1 = (bf16[64,1024]{1,0:T(8,128)(2,1)}, bf16[64,1024]{1,0:T(8,128)(2,1)S(1)}, u32[]{:S(2)}) copy-start(bf16[64,1024]{1,0:T(8,128)(2,1)S(1)} %collective-permute-done.5.refs_6_) | copy-start | bytes 393220
  25.9 1.8 %collective-permute-start.6 = (bf16[64,1024]{1,0:T(8,128)(2,1)S(1)}, bf16[64,1024]{1,0:T(8,128)(2,1)S(1)}, u32[]{:S(2)}, u32[]{:S(2)}) collective-permute-start(bf16[64,1024]{1,0:T(8,128)(2,1)S(1)} %collective-permute-done.5.refs_6_), channel_id=1, source_target_pairs={{0,1},{1,0},{2,3},{3,2},{4,5},{5,4},{6,7},{7,6},{8,9},{9,8},{10,11... | collective-permute-start | bytes 393224 | tf_op jit(solution)/shard_map/ppermute | solution.py:191
  26.5 1.5 %copy-start.2 = (bf16[64,1024]{1,0:T(8,128)(2,1)}, bf16[64,1024]{1,0:T(8,128)(2,1)S(1)}, u32[]{:S(2)}) copy-start(bf16[64,1024]{1,0:T(8,128)(2,1)S(1)} %collective-permute-done.3.refs_4_) | copy-start | bytes 393220
  26.5 1.3 %collective-permute-start.4 = (bf16[64,1024]{1,0:T(8,128)(2,1)S(1)}, bf16[64,1024]{1,0:T(8,128)(2,1)S(1)}, u32[]{:S(2)}, u32[]{:S(2)}) collective-permute-start(bf16[64,1024]{1,0:T(8,128)(2,1)S(1)} %collective-permute-done.3.refs_4_), channel_id=1, source_target_pairs={{0,1},{1,0},{2,3},{3,2},{4,5},{5,4},{6,7},{7,6},{8,9},{9,8},{10,11... | collective-permute-start | bytes 393224 | tf_op jit(solution)/shard_map/ppermute | solution.py:191
  26.5 1.5 %copy-start.3 = (bf16[64,1024]{1,0:T(8,128)(2,1)}, bf16[64,1024]{1,0:T(8,128)(2,1)S(1)}, u32[]{:S(2)}) copy-start(bf16[64,1024]{1,0:T(8,128)(2,1)S(1)} %collective-permute-done.1.refs_2_) | copy-start | bytes 393220
  26.5 1.4 %collective-permute-start.2 = (bf16[64,1024]{1,0:T(8,128)(2,1)S(1)}, bf16[64,1024]{1,0:T(8,128)(2,1)S(1)}, u32[]{:S(2)}, u32[]{:S(2)}) collective-permute-start(bf16[64,1024]{1,0:T(8,128)(2,1)S(1)} %collective-permute-done.1.refs_2_), channel_id=1, source_target_pairs={{0,1},{1,0},{2,3},{3,2},{4,5},{5,4},{6,7},{7,6},{8,9},{9,8},{10,11... | collective-permute-start | bytes 393224 | tf_op jit(solution)/shard_map/ppermute | solution.py:191
  27.7 0.7 copy-start.4
  27.7 0.7 copy-start.5
  27.8 0.7 copy-start.6
  28.0 0.6 copy-start.7
  64.7 8.3 %collective-permute-start.7 = (f32[64,256]{1,0:T(8,128)}, f32[64,256]{1,0:T(8,128)S(1)}, u32[]{:S(2)}, u32[]{:S(2)}) collective-permute-start(f32[64,256]{1,0:T(8,128)} %get-tuple-element.13), channel_id=1, source_target_pairs={{0,8},{1,17},{2,10},{3,19},{4,12},{5,21},{6,14},{7,23},{8,0},{9,25... | collective-permute-start | bytes 196616 | tf_op jit(solution)/shard_map/ppermute | solution.py:199
  66.8 8.4 %collective-permute-start.8 = (f32[64,256]{1,0:T(8,128)}, f32[64,256]{1,0:T(8,128)S(1)}, u32[]{:S(2)}, u32[]{:S(2)}) collective-permute-start(f32[64,256]{1,0:T(8,128)} %get-tuple-element.14), channel_id=1, source_target_pairs={{0,9},{1,16},{2,11},{3,18},{4,13},{5,20},{6,15},{7,22},{8,1},{9,24... | collective-permute-start | bytes 196616 | tf_op jit(solution)/shard_map/ppermute | solution.py:199
  69.0 8.5 %collective-permute-start.9 = (f32[64,256]{1,0:T(8,128)}, f32[64,256]{1,0:T(8,128)S(1)}, u32[]{:S(2)}, u32[]{:S(2)}) collective-permute-start(f32[64,256]{1,0:T(8,128)} %get-tuple-element.15), channel_id=1, source_target_pairs={{0,10},{1,19},{2,8},{3,17},{4,14},{5,23},{6,12},{7,21},{8,2},{9,27... | collective-permute-start | bytes 196616 | tf_op jit(solution)/shard_map/ppermute | solution.py:199
  70.4 10.7 %collective-permute-start.10 = (f32[64,256]{1,0:T(8,128)}, f32[64,256]{1,0:T(8,128)S(1)}, u32[]{:S(2)}, u32[]{:S(2)}) collective-permute-start(f32[64,256]{1,0:T(8,128)} %get-tuple-element.16), channel_id=1, source_target_pairs={{0,11},{1,18},{2,9},{3,16},{4,15},{5,22},{6,13},{7,20},{8,3},{9,26... | collective-permute-start | bytes 196616 | tf_op jit(solution)/shard_map/ppermute | solution.py:199
  70.5 10.7 %collective-permute-start.11 = (f32[64,256]{1,0:T(8,128)}, f32[64,256]{1,0:T(8,128)S(1)}, u32[]{:S(2)}, u32[]{:S(2)}) collective-permute-start(f32[64,256]{1,0:T(8,128)} %get-tuple-element.17), channel_id=1, source_target_pairs={{0,12},{1,21},{2,14},{3,23},{4,8},{5,17},{6,10},{7,19},{8,4},{9,29... | collective-permute-start | bytes 196616 | tf_op jit(solution)/shard_map/ppermute | solution.py:199
  73.0 11.2 %copy-start.8 = (f32[64,256]{1,0:T(8,128)}, f32[64,256]{1,0:T(8,128)S(1)}, u32[]{:S(2)}) copy-start(f32[64,256]{1,0:T(8,128)S(1)} %collective-permute-done.7.refs_0_) | copy-start | bytes 196612
  73.0 8.2 %collective-permute-start.12 = (f32[64,256]{1,0:T(8,128)}, f32[64,256]{1,0:T(8,128)S(1)}, u32[]{:S(2)}, u32[]{:S(2)}) collective-permute-start(f32[64,256]{1,0:T(8,128)} %get-tuple-element.18), channel_id=1, source_target_pairs={{0,13},{1,20},{2,15},{3,22},{4,9},{5,16},{6,11},{7,18},{8,5},{9,28... | collective-permute-start | bytes 196616 | tf_op jit(solution)/shard_map/ppermute | solution.py:199
  75.2 9.0 %copy-start.9 = (f32[64,256]{1,0:T(8,128)}, f32[64,256]{1,0:T(8,128)S(1)}, u32[]{:S(2)}) copy-start(f32[64,256]{1,0:T(8,128)S(1)} %collective-permute-done.8.refs_1_) | copy-start | bytes 196612
  75.2 6.6 %collective-permute-start.13 = (f32[64,256]{1,0:T(8,128)}, f32[64,256]{1,0:T(8,128)S(1)}, u32[]{:S(2)}, u32[]{:S(2)}) collective-permute-start(f32[64,256]{1,0:T(8,128)} %get-tuple-element.19), channel_id=1, source_target_pairs={{0,14},{1,23},{2,12},{3,21},{4,10},{5,19},{6,8},{7,17},{8,6},{9,31... | collective-permute-start | bytes 196616 | tf_op jit(solution)/shard_map/ppermute | solution.py:199
  77.5 6.7 %copy-start.10 = (f32[64,256]{1,0:T(8,128)}, f32[64,256]{1,0:T(8,128)S(1)}, u32[]{:S(2)}) copy-start(f32[64,256]{1,0:T(8,128)S(1)} %collective-permute-done.9.refs_2_) | copy-start | bytes 196612
  77.5 6.7 %collective-permute-start.14 = (f32[64,256]{1,0:T(8,128)}, f32[64,256]{1,0:T(8,128)S(1)}, u32[]{:S(2)}, u32[]{:S(2)}) collective-permute-start(f32[64,256]{1,0:T(8,128)} %get-tuple-element.20), channel_id=1, source_target_pairs={{0,15},{1,22},{2,13},{3,20},{4,11},{5,18},{6,9},{7,16},{8,7},{9,30... | collective-permute-start | bytes 196616 | tf_op jit(solution)/shard_map/ppermute | solution.py:199
  81.2 3.1 %copy-start.11 = (f32[64,256]{1,0:T(8,128)}, f32[64,256]{1,0:T(8,128)S(1)}, u32[]{:S(2)}) copy-start(f32[64,256]{1,0:T(8,128)S(1)} %collective-permute-done.10.refs_3_) | copy-start | bytes 196612
  81.2 3.1 %copy-start.12 = (f32[64,256]{1,0:T(8,128)}, f32[64,256]{1,0:T(8,128)S(1)}, u32[]{:S(2)}) copy-start(f32[64,256]{1,0:T(8,128)S(1)} %collective-permute-done.11.refs_4_) | copy-start | bytes 196612
  81.2 3.1 %copy-start.13 = (f32[64,256]{1,0:T(8,128)}, f32[64,256]{1,0:T(8,128)S(1)}, u32[]{:S(2)}) copy-start(f32[64,256]{1,0:T(8,128)S(1)} %collective-permute-done.12.refs_5_) | copy-start | bytes 196612
  81.8 2.5 %copy-start.14 = (f32[64,256]{1,0:T(8,128)}, f32[64,256]{1,0:T(8,128)S(1)}, u32[]{:S(2)}) copy-start(f32[64,256]{1,0:T(8,128)S(1)} %collective-permute-done.13.refs_6_) | copy-start | bytes 196612
  84.3 0.6 copy-start.15

commit v2 on v1

--- a/solution.py
+++ b/solution.py
@@ -8,7 +8,6 @@
 from jax.sharding import PartitionSpec as P
 
 QUAD = 4
-STEP = 4 * QUAD
 VMEM_LIMIT = 56 * 1024 * 1024
 
 
@@ -16,16 +15,74 @@
     return pl.BlockSpec(memory_space=pltpu.VMEM)
 
 
-def mixed_kernel(count, place_ref, *refs):
+def prepare_kernel(place_ref, index_ref, sign_ref, integral_ref, code_ref, kron_ref):
+    pairs, window = index_ref.shape[1:]
+    codes = index_ref[0] * 4 + sign_ref[0] + 1
+    low = lax.broadcasted_iota(jnp.int32, (128 // 8, 8, 128), 1) < QUAD
+    for start in range(0, window, 128):
+        for half in range(pairs // 2):
+            first, second = [
+                jnp.broadcast_to(codes[pair : pair + 1, start : start + 128], (128, 128))
+                .T.reshape(128 // 8, 8, 128)
+                for pair in (2 * half, 2 * half + 1)
+            ]
+            rows = slice(start // 8, (start + 128) // 8)
+            code_ref[rows, 0, half] = jnp.where(low, first, pltpu.roll(second, QUAD, 1))
+            code_ref[rows, 1, half] = jnp.where(low, pltpu.roll(first, QUAD, 1), second)
+    size = pairs * QUAD
+    spread = (
+        lax.broadcasted_iota(jnp.int32, (size, pairs), 0) // QUAD
+        == lax.broadcasted_iota(jnp.int32, (size, pairs), 1)
+    ).astype(jnp.bfloat16)
+    tall = jnp.dot(spread, integral_ref[0], preferred_element_type=jnp.float32)
+    wide = lax.dot_general(
+        tall.astype(jnp.bfloat16),
+        spread,
+        (((1,), (1,)), ((), ())),
+        preferred_element_type=jnp.float32,
+    )
+    row = lax.broadcasted_iota(jnp.int32, (size, size), 0)
+    column = lax.broadcasted_iota(jnp.int32, (size, size), 1)
+    kron_ref[...] = jnp.where(row % QUAD == column % QUAD, wide, 0.0).astype(jnp.bfloat16)
+
+
+def prepare(place, beta_index, beta_sign, integrals, window):
+    pairs = beta_index.shape[1]
+    size = pairs * QUAD
+    part = pl.BlockSpec((1, pairs, window), lambda i, at: (at[1], 0, at[2]))
+    codes, kron = pl.pallas_call(
+        prepare_kernel,
+        out_shape=[
+            jax.ShapeDtypeStruct((window // 8, 2, pairs // 2, 8, 128), jnp.int32),
+            jax.ShapeDtypeStruct((size, size), jnp.bfloat16),
+        ],
+        grid_spec=pltpu.PrefetchScalarGridSpec(
+            num_scalar_prefetch=1,
+            grid=(1,),
+            in_specs=[part, part, pl.BlockSpec((1, pairs, pairs), lambda i, at: (at[1], 0, 0))],
+            out_specs=[whole(), whole()],
+        ),
+        compiler_params=pltpu.CompilerParams(vmem_limit_bytes=VMEM_LIMIT),
+        cost_estimate=pl.CostEstimate(
+            flops=0, bytes_accessed=4 * window * size * 32, transcendentals=0
+        ),
+        name="prepare",
+    )(place, beta_index, beta_sign, integrals)
+    return codes.reshape(window * pairs, 128), kron
+
+
+def mixed_kernel(count, bundle, place_ref, *refs):
     pieces = refs[:count]
-    onehot_ref, kron_ref, index_ref, sign_ref = refs[count : count + 4]
+    code_ref, kron_ref, index_ref, sign_ref = refs[count : count + 4]
     outs = refs[count + 4 : 2 * count + 4]
-    turned, images, total, ordered = refs[2 * count + 4 :]
+    turned, images, total, ordered, signs = refs[2 * count + 4 :]
     step = pl.program_id(0)
-    block_rows = turned.shape[1]
+    beta_count, block_rows = turned.shape
     local_rows = pieces[0].shape[0]
     halves = images.shape[0]
     group = kron_ref.shape[0]
+    rows = code_ref.shape[0]
+    quads = rows // group
 
     @pl.when(step == 0)
     def _():
@@ -33,11 +90,22 @@
             both = jnp.concatenate([pieces[at][...], pieces[at + 1][...]], axis=0)
             turned[:, at * local_rows : (at + 2) * local_rows] = both.T
 
-    coupled = jnp.dot(onehot_ref[...], turned[...], preferred_element_type=jnp.float32)
+    codes = code_ref[...]
+    target = jnp.right_shift(codes, 2)
+    value = ((codes & 3) - 1).astype(jnp.float32)
+    lane = lax.broadcasted_iota(jnp.int32, (rows, 128), 1)
+    onehot = jnp.concatenate(
+        [
+            jnp.where(lane == target - start, value, 0.0).astype(jnp.bfloat16)
+            for start in range(0, beta_count, 128)
+        ],
+        axis=1,
+    )
+    coupled = jnp.dot(onehot, turned[...], preferred_element_type=jnp.float32)
     coupled = coupled.astype(jnp.bfloat16)
     low = lax.broadcasted_iota(jnp.int32, (halves, 8, block_rows), 1) < QUAD
     evens, odds = [], []
-    for pair in range(2):
+    for pair in range(quads // 2):
         first, second = [
             jnp.dot(
                 kron_ref[...],
@@ -48,67 +116,76 @@
         ]
         evens.append(jnp.where(low, first, pltpu.roll(second, QUAD, 1)))
         odds.append(jnp.where(low, pltpu.roll(first, QUAD, 1), second))
-    rows = pl.ds(pl.multiple_of(step * STEP, STEP), STEP)
-    images[:, 0, rows, :] = jnp.concatenate(evens, axis=1).astype(jnp.bfloat16)
-    images[:, 1, rows, :] = jnp.concatenate(odds, axis=1).astype(jnp.bfloat16)
+    columns = quads * QUAD
+    place = pl.ds(pl.multiple_of(step * columns, columns), columns)
+    images[:, 0, place, :] = jnp.concatenate(evens, axis=1).astype(jnp.bfloat16)
+    images[:, 1, place, :] = jnp.concatenate(odds, axis=1).astype(jnp.bfloat16)
 
     @pl.when(step == pl.num_programs(0) - 1)
     def _():
         total[...] = jnp.zeros_like(total)
+        signs[...] = sign_ref[0].astype(jnp.float32)
         position = lax.broadcasted_iota(jnp.int32, (block_rows, block_rows), 0)
-
-        def body(half, carry):
-            terms = []
-            for side in range(2):
-                pair = 2 * half + side
+        position = jnp.bitwise_xor(position, place_ref[0] * local_rows)
+
+        def body(at, carry):
+            term = None
+            for offset in range(bundle):
+                pair = bundle * at + offset
                 selector = jnp.where(
-                    position == index_ref[pl.ds(pair, 1), :], sign_ref[pl.ds(pair, 1), :], 0.0
+                    position == index_ref[0, pl.ds(pair, 1), :], signs[pl.ds(pair, 1), :], 0.0
                 ).astype(jnp.bfloat16)
-                terms.append(
-                    jnp.dot(images[half, side], selector, preferred_element_type=jnp.float32)
+                part = jnp.dot(
+                    images[lax.div(pair, 2), lax.rem(pair, 2)],
+                    selector,
+                    preferred_element_type=jnp.float32,
                 )
-            total[...] += terms[0] + terms[1]
+                term = part if term is None else term + part
+            total[...] += term
             return carry
 
-        lax.fori_loop(0, halves, body, 0)
+        lax.fori_loop(0, 2 * halves // bundle, body, 0)
         ordered[...] = total[...].T
         for at in range(count):
             start = pl.multiple_of((place_ref[0] ^ at) * local_rows, local_rows)
             outs[at][...] = ordered[pl.ds(start, local_rows), :]
 
 
-def mixed_pieces(place, pieces, onehot, kron, index, sign, window):
+def mixed_pieces(place, pieces, codes, kron, alpha_index, alpha_sign, window):
     count = len(pieces)
     local_rows, beta_count = pieces[0].shape
-    pair_count, block_rows = index.shape
-    steps = window // STEP
-    rows = pair_count * STEP
-    flops = 2 * window * pair_count * block_rows * (beta_count + pair_count * QUAD + block_rows)
+    pairs = alpha_index.shape[1]
+    block_rows = count * local_rows
+    columns = min(64, window)
+    rows = pairs * columns
+    bundle = next(size for size in (10, 5, 2, 1) if pairs % size == 0)
+    flops = 2 * window * pairs * block_rows * (beta_count + pairs * QUAD + block_rows)
+    part = pl.BlockSpec((1, pairs, block_rows), lambda i, at: (at[1], 0, at[3]))
     return pl.pallas_call(
-        functools.partial(mixed_kernel, count),
+        functools.partial(mixed_kernel, count, bundle),
         out_shape=[jax.ShapeDtypeStruct((local_rows, window), jnp.float32)] * count,
         grid_spec=pltpu.PrefetchScalarGridSpec(
             num_scalar_prefetch=1,
-            grid=(steps,),
+            grid=(window // columns,),
             in_specs=[whole()] * count
-            + [pl.BlockSpec((rows, beta_count), lambda i, place_ref: (i, 0))]
-            + [whole()] * 3,
+            + [pl.BlockSpec((rows, 128), lambda i, at: (i, 0)), whole(), part, part],
             out_specs=[whole()] * count,
             scratch_shapes=[
                 pltpu.VMEM((beta_count, block_rows), jnp.bfloat16),
-                pltpu.VMEM((pair_count // 2, 2, window, block_rows), jnp.bfloat16),
+                pltpu.VMEM((pairs // 2, 2, window, block_rows), jnp.bfloat16),
                 pltpu.VMEM((window, block_rows), jnp.float32),
                 pltpu.VMEM((block_rows, window), jnp.float32),
+                pltpu.VMEM((pairs, block_rows), jnp.float32),
             ],
         ),
         compiler_params=pltpu.CompilerParams(
             dimension_semantics=("arbitrary",), vmem_limit_bytes=VMEM_LIMIT
         ),
         cost_estimate=pl.CostEstimate(
-            flops=flops, bytes_accessed=2 * onehot.size, transcendentals=0
+            flops=flops, bytes_accessed=4 * codes.size, transcendentals=0
         ),
         name="mixed",
-    )(place, *pieces, onehot, kron, index, sign)
+    )(place, *pieces, codes, kron, alpha_index, alpha_sign)
 
 
 def plain_kernel(count, place_ref, *refs):
@@ -177,10 +254,10 @@
     blocks = lax.axis_size("blk")
     block_rows = local_rows * count
     window = beta_count * classes // count
-    quads = window // QUAD
     block_at, place = lax.axis_index("blk"), lax.axis_index("str")
-    symmetry, chunk = place % classes, place // classes
-    scalar_place = place.astype(jnp.int32).reshape(1)
+    symmetry = place % classes
+    partner = jnp.bitwise_xor(block_at, 1 << symmetry)
+    place = jnp.stack([place, symmetry, place // classes, partner]).astype(jnp.int32)
 
     def near(array, distance):
         route = [
@@ -202,29 +279,11 @@
     crossed = [near(piece, 1) for piece in straight]
     pieces = [piece for two in zip(straight, crossed) for piece in two]
 
-    def one_class(array, start, width):
-        return lax.dynamic_slice(array, (symmetry, 0, start), (1, array.shape[1], width))[0]
-
-    def by_quad(array):
-        part = one_class(array, chunk * window, window).reshape(pair_count, quads, QUAD)
-        return part.transpose(1, 0, 2).reshape(pair_count * window, 1)
-
-    positions = jnp.arange(beta_count, dtype=jnp.int32)[None, :]
-    onehot = jnp.where(by_quad(beta_index) == positions, by_quad(beta_sign), 0).astype(jnp.bfloat16)
-    same = jnp.eye(QUAD, dtype=jnp.bfloat16)
-    own_integrals = lax.dynamic_index_in_dim(integrals, symmetry, 0, keepdims=False)
-    kron = (own_integrals[:, None, :, None] * same[None, :, None, :]).reshape(
-        pair_count * QUAD, pair_count * QUAD
-    )
-    partner = jnp.bitwise_xor(block_at, 1 << symmetry)
-    index = one_class(alpha_index, partner * block_rows, block_rows)
-    index = jnp.bitwise_xor(index // local_rows, place) * local_rows + index % local_rows
-    sign = one_class(alpha_sign, partner * block_rows, block_rows).astype(jnp.float32)
-
-    sent = mixed_pieces(scalar_place, pieces, onehot, kron, index, sign, window)
+    codes, kron = prepare(place, beta_index, beta_sign, integrals, window)
+    sent = mixed_pieces(place, pieces, codes, kron, alpha_index, alpha_sign, window)
     terms = [far(sent[at], at) for at in range(count)]
-    base = plain_terms(scalar_place, pieces, alpha_operator, beta_operator)
-    return add_terms(scalar_place, base, terms, classes)
+    base = plain_terms(place, pieces, alpha_operator, beta_operator)
+    return add_terms(place, base, terms, classes)
 
 
 def solution(mesh):

time: 87.3 us -> 80.4 us (0.921)
  other arithmetic: 14.3 us -> 0.61 us
  waiting for transfers between devices: 3.27 us -> 8.36 us
  local copies, waits for them, and re-layouts: 9.14 us -> 11.8 us
  starting transfers between devices: 18.5 us -> 17.4 us
    convert_element_type x3 -> x0, other arithmetic: 13.1 us -> none  [the longest x1 12.4 us: local(): jnp.where(by_quad(beta_index) == positions, by_quad(beta_sign), 0)]
    unnamed x33 -> x35, local copies, waits for them, and re-layouts: 1.3 us -> 11.8 us
    ppermute x7, waiting for transfers between devices: 0.25 us -> 6.47 us  [near(): return lax.ppermute(array, ('blk', 'str'), route)]
    dynamic_slice x5 -> x0, local copies, waits for them, and re-layouts: 3.01 us -> none  [the longest x4 2.97 us: one_class(): lax.dynamic_slice(array, (symmetry, 0, start), (1, array.shape[1], width))]
    mul x1 -> x0, local copies, waits for them, and re-layouts: 2.2 us -> none  [local(): own_integrals[:, None, :, None] * same[None, :, None, :]]
    transpose x2 -> x0, local copies, waits for them, and re-layouts: 1.51 us -> none  [by_quad(): return part.transpose(1, 0, 2).reshape(pair_count * window, 1)]
    ppermute x8, waiting for transfers between devices: 3.02 us -> 1.89 us  [far(): return lax.ppermute(array, ('blk', 'str'), route)]
    pallas_call x1 -> x2, Pallas kernels: 36.1 us -> 36.3 us  [the longest x1 30.2 us: mixed_pieces(): pl.pallas_call(functools.partial(mixed_kernel, count, bundle), out_shape=...]
  transfers between devices with their start and end apart: 15 -> 15, of which waited for: 4 -> 3; matrix products, arithmetic and copies ran while one was open for 25% -> 14% of each run, Pallas kernels for 4% -> 12%
where the time goes in v2:
time: 80.4 us; the launch traced here: 79.9 us
  Pallas kernels  41.6 us (52%)
  starting transfers between devices  17.4 us (22%)
  local copies, waits for them, and re-layouts  11.8 us (15%)
  waiting for transfers between devices  8.36 us (10%)
    pallas_call x1, Pallas kernels, mixed_pieces(): pl.pallas_call(functools.partial(mixed_kernel, count, bundle), out_shape=...  30.2 us
    ppermute x8, starting transfers between devices, far(): return lax.ppermute(array, ('blk', 'str'), route)  12.4 us
    unnamed x35, local copies, waits for them, and re-layouts  11.8 us
    ppermute x7, waiting for transfers between devices, near(): return lax.ppermute(array, ('blk', 'str'), route)  6.47 us
    pallas_call x1, Pallas kernels, prepare(): pl.pallas_call(prepare_kernel, out_shape=[jax.ShapeDtypeStruct((window //...  6.03 us
    ppermute x7, starting transfers between devices, near(): return lax.ppermute(array, ('blk', 'str'), route)  4.97 us
    pallas_call x1, Pallas kernels, plain_terms(): pl.pallas_call(functools.partial(plain_kernel, count), out_shape=jax.Shap...  3.46 us
    ppermute x8, waiting for transfers between devices, far(): return lax.ppermute(array, ('blk', 'str'), route)  1.89 us
  transfers between devices with their start and end apart: 15, of which 3 were waited for; matrix products, arithmetic and copies ran while one was open for 14% of the time, Pallas kernels for 12%

profile of v2, /device:TPU:0, one launch (start us, length us, event | category | flops | bytes accessed | tf_op | source)
XLA Modules:
  0.0 79.9 jit_solution(3921049539378024272)
XLA Ops:
  0.0 2.9 %collective-permute-start.1 = (bf16[64,1024]{1,0:T(8,128)(2,1)}, bf16[64,1024]{1,0:T(8,128)(2,1)S(1)}, u32[]{:S(2)}, u32[]{:S(2)}) collective-permute-start(bf16[64,1024]{1,0:T(8,128)(2,1)} %refs_0_.3), channel_id=1, source_target_pairs={{0,2},{1,3},{2,0},{3,1},{4,6},{5,7},{6,4},{7,5},{8,10},{9,11},{10,... | collective-permute-start | bytes 393224 | tf_op jit(solution)/shard_map/ppermute | solution.py:268
  2.9 1.5 %collective-permute-start.3 = (bf16[64,1024]{1,0:T(8,128)(2,1)}, bf16[64,1024]{1,0:T(8,128)(2,1)S(1)}, u32[]{:S(2)}, u32[]{:S(2)}) collective-permute-start(bf16[64,1024]{1,0:T(8,128)(2,1)} %refs_0_.3), channel_id=1, source_target_pairs={{0,4},{1,5},{2,6},{3,7},{4,0},{5,1},{6,2},{7,3},{8,12},{9,13},{10,... | collective-permute-start | bytes 393224 | tf_op jit(solution)/shard_map/ppermute | solution.py:268
  4.5 0.0 collective-permute-start.5
  4.5 0.0 collective-permute-start
  4.5 2.7 %collective-permute-done.1.refs_2_ = bf16[64,1024]{1,0:T(8,128)(2,1)S(1)} collective-permute-done((bf16[64,1024]{1,0:T(8,128)(2,1)}, bf16[64,1024]{1,0:T(8,128)(2,1)S(1)}, u32[]{:S(2)}, u32[]{:S(2)}) %collective-permute-start.1) | collective-permute-done | bytes 131104 | tf_op jit(solution)/shard_map/ppermute | solution.py:268
  7.2 0.0 collective-permute-start.2
  7.2 3.8 %collective-permute-done.3.refs_4_ = bf16[64,1024]{1,0:T(8,128)(2,1)S(1)} collective-permute-done((bf16[64,1024]{1,0:T(8,128)(2,1)}, bf16[64,1024]{1,0:T(8,128)(2,1)S(1)}, u32[]{:S(2)}, u32[]{:S(2)}) %collective-permute-start.3) | collective-permute-done | bytes 131104 | tf_op jit(solution)/shard_map/ppermute | solution.py:268
  10.9 0.0 collective-permute-start.4
  10.9 0.0 collective-permute-done.5.refs_6_
  10.9 0.0 copy-start.2
  10.9 0.5 collective-permute-start.6
  11.4 1.9 %copy.10.sign_ref = s32[2,50,1024]{2,1,0:T(8,128)} copy(s32[2,50,1024]{2,0,1:T(2,128)} %param.10) | data formatting | bytes 819200 | tf_op args[2]
  13.3 2.0 %copy.9.index_ref = s32[2,50,1024]{2,1,0:T(8,128)} copy(s32[2,50,1024]{2,0,1:T(2,128)} %param.9) | data formatting | bytes 819200 | tf_op args[1]
  15.3 1.4 %copy.11.integral_ref = bf16[2,50,50]{2,1,0:T(8,128)(2,1)} copy(bf16[2,50,50]{2,0,1:T(2,128)(2,1)} %param.13) | data formatting | bytes 20000 | tf_op args[5]
  16.7 2.5 %copy.12.refs_10_ = s32[2,50,2048]{2,1,0:T(8,128)} copy(s32[2,50,2048]{2,0,1:T(2,128)} %param.11) | data formatting | bytes 1638400 | tf_op args[3]
  19.2 2.7 %copy.13.refs_11_ = s32[2,50,2048]{2,1,0:T(8,128)} copy(s32[2,50,2048]{2,0,1:T(2,128)} %param.12) | data formatting | bytes 1638400 | tf_op args[4]
  21.9 0.6 pad_add_fusion.place_ref
  22.5 6.0 %prepare.1 = (s32[32,2,25,8,128]{4,3,2,1,0:T(8,128)}, bf16[200,200]{1,0:T(8,128)(2,1)}) custom-call(s32[4]{0:T(128)} %pad_add_fusion.place_ref, s32[2,50,1024]{2,1,0:T(8,128)} %copy.9.index_ref, s32[2,50,1024]{2,1,0:T(8,128)} %copy.10.sign_ref, bf16[2,50,50]{2,1,0:T(8,128)(2,1)} %copy.11.integral_ref), custom_call_target="tpu_custom_call" | custom-call | bytes 6553600 | tf_op jit(solution)/shard_map/prepare/pallas_call | solution.py:53
  28.5 0.0 collective-permute-done.refs_1_
  28.5 0.0 collective-permute-done.2.refs_3_
  28.5 0.0 collective-permute-done.4.refs_5_
  28.5 0.0 copy-start.5
  28.6 0.0 collective-permute-done.6.refs_7_
  28.6 0.6 copy-done.3
  29.2 0.0 copy-done.4
  29.2 0.0 copy-done.5
  29.3 0.0 copy-done.6
  29.3 30.2 %mixed.1 = (f32[64,256]{1,0:T(8,128)}, f32[64,256]{1,0:T(8,128)}, f32[64,256]{1,0:T(8,128)}, f32[64,256]{1,0:T(8,128)}, f32[64,256]{1,0:T(8,128)}, /*index=5*/f3...) custom-call(s32[4]{0:T(128)} %pad_add_fusion.place_ref, bf16[64,1024]{1,0:T(8,128)(2,1)} %refs_0_.3, ...), custom_call_target="tpu_custom_call" | custom-call | flops 22754099200 | bytes 6553600 | tf_op jit(solution)/shard_map/mixed/pallas_call | solution.py:164
  59.6 1.9 %collective-permute-start.10 = (f32[64,256]{1,0:T(8,128)}, f32[64,256]{1,0:T(8,128)S(1)}, u32[]{:S(2)}, u32[]{:S(2)}) collective-permute-start(f32[64,256]{1,0:T(8,128)} %get-tuple-element.20), channel_id=1, source_target_pairs={{0,11},{1,18},{2,9},{3,16},{4,15},{5,22},{6,13},{7,20},{8,3},{9,26... | collective-permute-start | bytes 196616 | tf_op jit(solution)/shard_map/ppermute | solution.py:276
  61.4 0.8 collective-permute-start.11
  62.2 2.4 %collective-permute-start.12 = (f32[64,256]{1,0:T(8,128)}, f32[64,256]{1,0:T(8,128)S(1)}, u32[]{:S(2)}, u32[]{:S(2)}) collective-permute-start(f32[64,256]{1,0:T(8,128)} %get-tuple-element.22), channel_id=1, source_target_pairs={{0,13},{1,20},{2,15},{3,22},{4,9},{5,16},{6,11},{7,18},{8,5},{9,28... | collective-permute-start | bytes 196616 | tf_op jit(solution)/shard_map/ppermute | solution.py:276
  64.6 2.1 %collective-permute-start.13 = (f32[64,256]{1,0:T(8,128)}, f32[64,256]{1,0:T(8,128)S(1)}, u32[]{:S(2)}, u32[]{:S(2)}) collective-permute-start(f32[64,256]{1,0:T(8,128)} %get-tuple-element.23), channel_id=1, source_target_pairs={{0,14},{1,23},{2,12},{3,21},{4,10},{5,19},{6,8},{7,17},{8,6},{9,31... | collective-permute-start | bytes 196616 | tf_op jit(solution)/shard_map/ppermute | solution.py:276
  66.7 1.8 %collective-permute-start.14 = (f32[64,256]{1,0:T(8,128)}, f32[64,256]{1,0:T(8,128)S(1)}, u32[]{:S(2)}, u32[]{:S(2)}) collective-permute-start(f32[64,256]{1,0:T(8,128)} %get-tuple-element.24), channel_id=1, source_target_pairs={{0,15},{1,22},{2,13},{3,20},{4,11},{5,18},{6,9},{7,16},{8,7},{9,30... | collective-permute-start | bytes 196616 | tf_op jit(solution)/shard_map/ppermute | solution.py:276
  68.5 0.0 collective-permute-done.10.refs_3_
  68.6 0.4 collective-permute-start.7
  69.0 0.0 collective-permute-done.11.refs_4_
  69.0 1.8 %collective-permute-start.8 = (f32[64,256]{1,0:T(8,128)}, f32[64,256]{1,0:T(8,128)S(1)}, u32[]{:S(2)}, u32[]{:S(2)}) collective-permute-start(f32[64,256]{1,0:T(8,128)} %get-tuple-element.18), channel_id=1, source_target_pairs={{0,9},{1,16},{2,11},{3,18},{4,13},{5,20},{6,15},{7,22},{8,1},{9,24... | collective-permute-start | bytes 196616 | tf_op jit(solution)/shard_map/ppermute | solution.py:276
  70.8 0.0 collective-permute-done.12.refs_5_
  70.8 1.2 %collective-permute-start.9 = (f32[64,256]{1,0:T(8,128)}, f32[64,256]{1,0:T(8,128)S(1)}, u32[]{:S(2)}, u32[]{:S(2)}) collective-permute-start(f32[64,256]{1,0:T(8,128)} %get-tuple-element.19), channel_id=1, source_target_pairs={{0,10},{1,19},{2,8},{3,17},{4,14},{5,23},{6,12},{7,21},{8,2},{9,27... | collective-permute-start | bytes 196616 | tf_op jit(solution)/shard_map/ppermute | solution.py:276
  72.0 3.5 %plain.1.base_ref = f32[64,1024]{1,0:T(8,128)} custom-call(s32[4]{0:T(128)} %pad_add_fusion.place_ref, bf16[64,1024]{1,0:T(8,128)(2,1)} %refs_0_.3, bf16[64,1024]{1,0:T(8,128)(2,1)} %copy-done.3, bf16[64,1024]{1,0:T(8,128)(2,1)} %copy-done, bf16[64,1024]{1,0:T(8,128)(2,1)} %copy-done.4, bf16[64,1024]{1,0:T(8,128)(2,1)} %copy-done.1, ...), custom_call_target="tpu_custom_call" | custom-call | flops 201326592 | bytes 3145728 | tf_op jit(solution)/shard_map/plain/pallas_call | solution.py:207
  75.4 0.0 collective-permute-done.13.refs_6_
  75.4 0.0 collective-permute-done.14.refs_7_
  75.5 0.0 collective-permute-done.7.refs_0_
  75.5 0.0 copy-start.12
  75.5 0.0 collective-permute-done.8.refs_1_
  75.5 1.8 %collective-permute-done.9.refs_2_ = f32[64,256]{1,0:T(8,128)S(1)} collective-permute-done((f32[64,256]{1,0:T(8,128)}, f32[64,256]{1,0:T(8,128)S(1)}, u32[]{:S(2)}, u32[]{:S(2)}) %collective-permute-start.9) | collective-permute-done | bytes 65568 | tf_op jit(solution)/shard_map/ppermute | solution.py:276
  77.4 0.6 copy-done.14
  78.0 1.9 %add.13 = f32[64,1024]{1,0:T(8,128)} custom-call(s32[4]{0:T(128)} %pad_add_fusion.place_ref, f32[64,1024]{1,0:T(8,128)} %plain.1.base_ref, f32[64,256]{1,0:T(8,128)} %copy-done.12, f32[64,256]{1,0:T(8,128)} %copy-done.13, f32[64,256]{1,0:T(8,128)} %copy-done.14, f32[64,256]{1,0:T(8,128)} %copy-done.7, f32[64,256]{1,0:T(8,128)} %copy-done.8, ...), custom_call_target="tpu_custom_call" | custom-call | tf_op jit(solution)/shard_map/add/pallas_call | solution.py:238
  (22 shorter events, 0.0 us)
Async XLA Ops:
  0.0 7.2 %collective-permute-start.1 = (bf16[64,1024]{1,0:T(8,128)(2,1)}, bf16[64,1024]{1,0:T(8,128)(2,1)S(1)}, u32[]{:S(2)}, u32[]{:S(2)}) collective-permute-start(bf16[64,1024]{1,0:T(8,128)(2,1)} %refs_0_.3), channel_id=1, source_target_pairs={{0,2},{1,3},{2,0},{3,1},{4,6},{5,7},{6,4},{7,5},{8,10},{9,11},{10,... | collective-permute-start | bytes 393224 | tf_op jit(solution)/shard_map/ppermute | solution.py:268
  2.9 8.0 %collective-permute-start.3 = (bf16[64,1024]{1,0:T(8,128)(2,1)}, bf16[64,1024]{1,0:T(8,128)(2,1)S(1)}, u32[]{:S(2)}, u32[]{:S(2)}) collective-permute-start(bf16[64,1024]{1,0:T(8,128)(2,1)} %refs_0_.3), channel_id=1, source_target_pairs={{0,4},{1,5},{2,6},{3,7},{4,0},{5,1},{6,2},{7,3},{8,12},{9,13},{10,... | collective-permute-start | bytes 393224 | tf_op jit(solution)/shard_map/ppermute | solution.py:268
  4.5 6.5 %collective-permute-start.5 = (bf16[64,1024]{1,0:T(8,128)(2,1)}, bf16[64,1024]{1,0:T(8,128)(2,1)S(1)}, u32[]{:S(2)}, u32[]{:S(2)}) collective-permute-start(bf16[64,1024]{1,0:T(8,128)(2,1)} %refs_0_.3), channel_id=1, source_target_pairs={{0,6},{1,7},{2,4},{3,5},{4,2},{5,3},{6,0},{7,1},{8,14},{9,15},{10,... | collective-permute-start | bytes 393224 | tf_op jit(solution)/shard_map/ppermute | solution.py:268
  4.5 24.1 %collective-permute-start = (bf16[64,1024]{1,0:T(8,128)(2,1)}, bf16[64,1024]{1,0:T(8,128)(2,1)S(1)}, u32[]{:S(2)}, u32[]{:S(2)}) collective-permute-start(bf16[64,1024]{1,0:T(8,128)(2,1)} %refs_0_.3), channel_id=1, source_target_pairs={{0,1},{1,0},{2,3},{3,2},{4,5},{5,4},{6,7},{7,6},{8,9},{9,8},{10,11... | collective-permute-start | bytes 393224 | tf_op jit(solution)/shard_map/ppermute | solution.py:268
  7.2 21.4 %copy-start = (bf16[64,1024]{1,0:T(8,128)(2,1)}, bf16[64,1024]{1,0:T(8,128)(2,1)S(1)}, u32[]{:S(2)}) copy-start(bf16[64,1024]{1,0:T(8,128)(2,1)S(1)} %collective-permute-done.1.refs_2_) | copy-start | bytes 393220
  7.2 21.4 %collective-permute-start.2 = (bf16[64,1024]{1,0:T(8,128)(2,1)S(1)}, bf16[64,1024]{1,0:T(8,128)(2,1)S(1)}, u32[]{:S(2)}, u32[]{:S(2)}) collective-permute-start(bf16[64,1024]{1,0:T(8,128)(2,1)S(1)} %collective-permute-done.1.refs_2_), channel_id=1, source_target_pairs={{0,1},{1,0},{2,3},{3,2},{4,5},{5,4},{6,7},{7,6},{8,9},{9,8},{10,11... | collective-permute-start | bytes 393224 | tf_op jit(solution)/shard_map/ppermute | solution.py:268
  10.9 17.7 %copy-start.1 = (bf16[64,1024]{1,0:T(8,128)(2,1)}, bf16[64,1024]{1,0:T(8,128)(2,1)S(1)}, u32[]{:S(2)}) copy-start(bf16[64,1024]{1,0:T(8,128)(2,1)S(1)} %collective-permute-done.3.refs_4_) | copy-start | bytes 393220
  10.9 17.6 %collective-permute-start.4 = (bf16[64,1024]{1,0:T(8,128)(2,1)S(1)}, bf16[64,1024]{1,0:T(8,128)(2,1)S(1)}, u32[]{:S(2)}, u32[]{:S(2)}) collective-permute-start(bf16[64,1024]{1,0:T(8,128)(2,1)S(1)} %collective-permute-done.3.refs_4_), channel_id=1, source_target_pairs={{0,1},{1,0},{2,3},{3,2},{4,5},{5,4},{6,7},{7,6},{8,9},{9,8},{10,11... | collective-permute-start | bytes 393224 | tf_op jit(solution)/shard_map/ppermute | solution.py:268
  10.9 17.7 %copy-start.2 = (bf16[64,1024]{1,0:T(8,128)(2,1)}, bf16[64,1024]{1,0:T(8,128)(2,1)S(1)}, u32[]{:S(2)}) copy-start(bf16[64,1024]{1,0:T(8,128)(2,1)S(1)} %collective-permute-done.5.refs_6_) | copy-start | bytes 393220
  10.9 17.6 %collective-permute-start.6 = (bf16[64,1024]{1,0:T(8,128)(2,1)S(1)}, bf16[64,1024]{1,0:T(8,128)(2,1)S(1)}, u32[]{:S(2)}, u32[]{:S(2)}) collective-permute-start(bf16[64,1024]{1,0:T(8,128)(2,1)S(1)} %collective-permute-done.5.refs_6_), channel_id=1, source_target_pairs={{0,1},{1,0},{2,3},{3,2},{4,5},{5,4},{6,7},{7,6},{8,9},{9,8},{10,11... | collective-permute-start | bytes 393224 | tf_op jit(solution)/shard_map/ppermute | solution.py:268
  28.5 0.7 copy-start.3
  28.5 0.7 copy-start.4
  28.5 0.7 copy-start.5
  28.6 0.7 copy-start.6
  59.6 9.0 %collective-permute-start.10 = (f32[64,256]{1,0:T(8,128)}, f32[64,256]{1,0:T(8,128)S(1)}, u32[]{:S(2)}, u32[]{:S(2)}) collective-permute-start(f32[64,256]{1,0:T(8,128)} %get-tuple-element.20), channel_id=1, source_target_pairs={{0,11},{1,18},{2,9},{3,16},{4,15},{5,22},{6,13},{7,20},{8,3},{9,26... | collective-permute-start | bytes 196616 | tf_op jit(solution)/shard_map/ppermute | solution.py:276
  61.4 7.6 %collective-permute-start.11 = (f32[64,256]{1,0:T(8,128)}, f32[64,256]{1,0:T(8,128)S(1)}, u32[]{:S(2)}, u32[]{:S(2)}) collective-permute-start(f32[64,256]{1,0:T(8,128)} %get-tuple-element.21), channel_id=1, source_target_pairs={{0,12},{1,21},{2,14},{3,23},{4,8},{5,17},{6,10},{7,19},{8,4},{9,29... | collective-permute-start | bytes 196616 | tf_op jit(solution)/shard_map/ppermute | solution.py:276
  62.2 8.6 %collective-permute-start.12 = (f32[64,256]{1,0:T(8,128)}, f32[64,256]{1,0:T(8,128)S(1)}, u32[]{:S(2)}, u32[]{:S(2)}) collective-permute-start(f32[64,256]{1,0:T(8,128)} %get-tuple-element.22), channel_id=1, source_target_pairs={{0,13},{1,20},{2,15},{3,22},{4,9},{5,16},{6,11},{7,18},{8,5},{9,28... | collective-permute-start | bytes 196616 | tf_op jit(solution)/shard_map/ppermute | solution.py:276
  64.6 10.8 %collective-permute-start.13 = (f32[64,256]{1,0:T(8,128)}, f32[64,256]{1,0:T(8,128)S(1)}, u32[]{:S(2)}, u32[]{:S(2)}) collective-permute-start(f32[64,256]{1,0:T(8,128)} %get-tuple-element.23), channel_id=1, source_target_pairs={{0,14},{1,23},{2,12},{3,21},{4,10},{5,19},{6,8},{7,17},{8,6},{9,31... | collective-permute-start | bytes 196616 | tf_op jit(solution)/shard_map/ppermute | solution.py:276
  66.7 8.7 %collective-permute-start.14 = (f32[64,256]{1,0:T(8,128)}, f32[64,256]{1,0:T(8,128)S(1)}, u32[]{:S(2)}, u32[]{:S(2)}) collective-permute-start(f32[64,256]{1,0:T(8,128)} %get-tuple-element.24), channel_id=1, source_target_pairs={{0,15},{1,22},{2,13},{3,20},{4,11},{5,18},{6,9},{7,16},{8,7},{9,30... | collective-permute-start | bytes 196616 | tf_op jit(solution)/shard_map/ppermute | solution.py:276
  68.6 8.8 %copy-start.7 = (f32[64,256]{1,0:T(8,128)}, f32[64,256]{1,0:T(8,128)S(1)}, u32[]{:S(2)}) copy-start(f32[64,256]{1,0:T(8,128)S(1)} %collective-permute-done.10.refs_3_) | copy-start | bytes 196612
  68.6 6.9 %collective-permute-start.7 = (f32[64,256]{1,0:T(8,128)}, f32[64,256]{1,0:T(8,128)S(1)}, u32[]{:S(2)}, u32[]{:S(2)}) collective-permute-start(f32[64,256]{1,0:T(8,128)} %get-tuple-element.17), channel_id=1, source_target_pairs={{0,8},{1,17},{2,10},{3,19},{4,12},{5,21},{6,14},{7,23},{8,0},{9,25... | collective-permute-start | bytes 196616 | tf_op jit(solution)/shard_map/ppermute | solution.py:276
  69.0 8.4 %copy-start.8 = (f32[64,256]{1,0:T(8,128)}, f32[64,256]{1,0:T(8,128)S(1)}, u32[]{:S(2)}) copy-start(f32[64,256]{1,0:T(8,128)S(1)} %collective-permute-done.11.refs_4_) | copy-start | bytes 196612
  69.0 6.5 %collective-permute-start.8 = (f32[64,256]{1,0:T(8,128)}, f32[64,256]{1,0:T(8,128)S(1)}, u32[]{:S(2)}, u32[]{:S(2)}) collective-permute-start(f32[64,256]{1,0:T(8,128)} %get-tuple-element.18), channel_id=1, source_target_pairs={{0,9},{1,16},{2,11},{3,18},{4,13},{5,20},{6,15},{7,22},{8,1},{9,24... | collective-permute-start | bytes 196616 | tf_op jit(solution)/shard_map/ppermute | solution.py:276
  70.8 6.5 %copy-start.9 = (f32[64,256]{1,0:T(8,128)}, f32[64,256]{1,0:T(8,128)S(1)}, u32[]{:S(2)}) copy-start(f32[64,256]{1,0:T(8,128)S(1)} %collective-permute-done.12.refs_5_) | copy-start | bytes 196612
  70.8 6.5 %collective-permute-start.9 = (f32[64,256]{1,0:T(8,128)}, f32[64,256]{1,0:T(8,128)S(1)}, u32[]{:S(2)}, u32[]{:S(2)}) collective-permute-start(f32[64,256]{1,0:T(8,128)} %get-tuple-element.19), channel_id=1, source_target_pairs={{0,10},{1,19},{2,8},{3,17},{4,14},{5,23},{6,12},{7,21},{8,2},{9,27... | collective-permute-start | bytes 196616 | tf_op jit(solution)/shard_map/ppermute | solution.py:276
  75.4 1.9 %copy-start.10 = (f32[64,256]{1,0:T(8,128)}, f32[64,256]{1,0:T(8,128)S(1)}, u32[]{:S(2)}) copy-start(f32[64,256]{1,0:T(8,128)S(1)} %collective-permute-done.13.refs_6_) | copy-start | bytes 196612
  75.5 1.9 %copy-start.11 = (f32[64,256]{1,0:T(8,128)}, f32[64,256]{1,0:T(8,128)S(1)}, u32[]{:S(2)}) copy-start(f32[64,256]{1,0:T(8,128)S(1)} %collective-permute-done.14.refs_7_) | copy-start | bytes 196612
  75.5 1.9 %copy-start.12 = (f32[64,256]{1,0:T(8,128)}, f32[64,256]{1,0:T(8,128)S(1)}, u32[]{:S(2)}) copy-start(f32[64,256]{1,0:T(8,128)S(1)} %collective-permute-done.7.refs_0_) | copy-start | bytes 196612
  75.5 1.9 %copy-start.13 = (f32[64,256]{1,0:T(8,128)}, f32[64,256]{1,0:T(8,128)S(1)}, u32[]{:S(2)}) copy-start(f32[64,256]{1,0:T(8,128)S(1)} %collective-permute-done.8.refs_1_) | copy-start | bytes 196612
  77.4 0.6 copy-start.14

commit v3 on v2

--- a/solution.py
+++ b/solution.py
@@ -15,9 +15,17 @@
     return pl.BlockSpec(memory_space=pltpu.VMEM)
 
 
+def of_class(values, symmetry):
+    picked = values[:, 0, :]
+    for other in range(1, values.shape[1]):
+        picked = jnp.where(symmetry == other, values[:, other, :], picked)
+    return picked
+
+
 def prepare_kernel(place_ref, index_ref, sign_ref, integral_ref, code_ref, kron_ref):
-    pairs, window = index_ref.shape[1:]
-    codes = index_ref[0] * 4 + sign_ref[0] + 1
+    pairs, _, window = index_ref.shape
+    codes = of_class(index_ref[...] * 4 + sign_ref[...] + 1, place_ref[1])
+    integrals = of_class(integral_ref[...].astype(jnp.float32), place_ref[1])
     low = lax.broadcasted_iota(jnp.int32, (128 // 8, 8, 128), 1) < QUAD
     for start in range(0, window, 128):
         for half in range(pairs // 2):
@@ -34,7 +42,7 @@
         lax.broadcasted_iota(jnp.int32, (size, pairs), 0) // QUAD
         == lax.broadcasted_iota(jnp.int32, (size, pairs), 1)
     ).astype(jnp.bfloat16)
-    tall = jnp.dot(spread, integral_ref[0], preferred_element_type=jnp.float32)
+    tall = jnp.dot(spread, integrals.astype(jnp.bfloat16), preferred_element_type=jnp.float32)
     wide = lax.dot_general(
         tall.astype(jnp.bfloat16),
         spread,
@@ -47,9 +55,9 @@
 
 
 def prepare(place, beta_index, beta_sign, integrals, window):
-    pairs = beta_index.shape[1]
+    pairs, classes = beta_index.shape[:2]
     size = pairs * QUAD
-    part = pl.BlockSpec((1, pairs, window), lambda i, at: (at[1], 0, at[2]))
+    part = pl.BlockSpec((pairs, classes, window), lambda i, at: (0, 0, at[2]))
     codes, kron = pl.pallas_call(
         prepare_kernel,
         out_shape=[
@@ -59,7 +67,7 @@
         grid_spec=pltpu.PrefetchScalarGridSpec(
             num_scalar_prefetch=1,
             grid=(1,),
-            in_specs=[part, part, pl.BlockSpec((1, pairs, pairs), lambda i, at: (at[1], 0, 0))],
+            in_specs=[part, part, whole()],
             out_specs=[whole(), whole()],
         ),
         compiler_params=pltpu.CompilerParams(vmem_limit_bytes=VMEM_LIMIT),
@@ -75,7 +83,7 @@
     pieces = refs[:count]
     code_ref, kron_ref, index_ref, sign_ref = refs[count : count + 4]
     outs = refs[count + 4 : 2 * count + 4]
-    turned, images, total, ordered, signs = refs[2 * count + 4 :]
+    turned, images, total, ordered, indices, signs = refs[2 * count + 4 :]
     step = pl.program_id(0)
     beta_count, block_rows = turned.shape
     local_rows = pieces[0].shape[0]
@@ -124,7 +132,8 @@
     @pl.when(step == pl.num_programs(0) - 1)
     def _():
         total[...] = jnp.zeros_like(total)
-        signs[...] = sign_ref[0].astype(jnp.float32)
+        indices[...] = of_class(index_ref[...], place_ref[1])
+        signs[...] = of_class(sign_ref[...], place_ref[1]).astype(jnp.float32)
         position = lax.broadcasted_iota(jnp.int32, (block_rows, block_rows), 0)
         position = jnp.bitwise_xor(position, place_ref[0] * local_rows)
 
@@ -133,7 +142,7 @@
             for offset in range(bundle):
                 pair = bundle * at + offset
                 selector = jnp.where(
-                    position == index_ref[0, pl.ds(pair, 1), :], signs[pl.ds(pair, 1), :], 0.0
+                    position == indices[pl.ds(pair, 1), :], signs[pl.ds(pair, 1), :], 0.0
                 ).astype(jnp.bfloat16)
                 part = jnp.dot(
                     images[lax.div(pair, 2), lax.rem(pair, 2)],
@@ -154,13 +163,13 @@
 def mixed_pieces(place, pieces, codes, kron, alpha_index, alpha_sign, window):
     count = len(pieces)
     local_rows, beta_count = pieces[0].shape
-    pairs = alpha_index.shape[1]
+    pairs, classes = alpha_index.shape[:2]
     block_rows = count * local_rows
     columns = min(64, window)
     rows = pairs * columns
     bundle = next(size for size in (10, 5, 2, 1) if pairs % size == 0)
     flops = 2 * window * pairs * block_rows * (beta_count + pairs * QUAD + block_rows)
-    part = pl.BlockSpec((1, pairs, block_rows), lambda i, at: (at[1], 0, at[3]))
+    part = pl.BlockSpec((pairs, classes, block_rows), lambda i, at: (0, 0, at[3]))
     return pl.pallas_call(
         functools.partial(mixed_kernel, count, bundle),
         out_shape=[jax.ShapeDtypeStruct((local_rows, window), jnp.float32)] * count,
@@ -175,6 +184,7 @@
                 pltpu.VMEM((pairs // 2, 2, window, block_rows), jnp.bfloat16),
                 pltpu.VMEM((window, block_rows), jnp.float32),
                 pltpu.VMEM((block_rows, window), jnp.float32),
+                pltpu.VMEM((pairs, block_rows), jnp.int32),
                 pltpu.VMEM((pairs, block_rows), jnp.float32),
             ],
         ),
@@ -275,12 +285,18 @@
         ]
         return lax.ppermute(array, ("blk", "str"), route)
 
-    straight = [civec] + [near(civec, at) for at in range(2, count, 2)]
+    by_pair = [
+        jnp.transpose(array, (1, 0, 2))
+        for array in (beta_index, beta_sign, integrals, alpha_index, alpha_sign)
+    ]
+    arrived = [near(civec, at) for at in range(2, count, 2)]
+    codes, kron = prepare(place, *by_pair[:3], window)
+    codes, kron, *arrived = lax.optimization_barrier((codes, kron, *arrived))
+    straight = [civec] + arrived
     crossed = [near(piece, 1) for piece in straight]
     pieces = [piece for two in zip(straight, crossed) for piece in two]
 
-    codes, kron = prepare(place, beta_index, beta_sign, integrals, window)
-    sent = mixed_pieces(place, pieces, codes, kron, alpha_index, alpha_sign, window)
+    sent = mixed_pieces(place, pieces, codes, kron, *by_pair[3:], window)
     terms = [far(sent[at], at) for at in range(count)]
     base = plain_terms(place, pieces, alpha_operator, beta_operator)
     return add_terms(place, base, terms, classes)

time: 80.4 us -> 66.7 us (0.83)
  local copies, waits for them, and re-layouts: 11.8 us -> 1.27 us
  waiting for transfers between devices: 8.36 us -> 4.04 us
  starting transfers between devices: 17.4 us -> 18.5 us
    unnamed x35 -> x30, local copies, waits for them, and re-layouts: 11.8 us -> 1.27 us
    ppermute x7, waiting for transfers between devices: 6.47 us -> 1.02 us  [near(): return lax.ppermute(array, ('blk', 'str'), route)]
    ppermute x8, waiting for transfers between devices: 1.89 us -> 3.02 us  [far(): return lax.ppermute(array, ('blk', 'str'), route)]
  transfers between devices with their start and end apart: 15 -> 15, of which waited for: 3 -> 5; matrix products, arithmetic and copies ran while one was open for 14% -> 1% of each run, Pallas kernels for 12% -> 14%
where the time goes in v3:
time: 66.7 us; the launch traced here: 66.5 us
  Pallas kernels  41.9 us (63%)
  starting transfers between devices  18.5 us (28%)
  waiting for transfers between devices  4.04 us (6%)
  local copies, waits for them, and re-layouts  1.27 us (2%)
    pallas_call x1, Pallas kernels, mixed_pieces(): pl.pallas_call(functools.partial(mixed_kernel, count, bundle), out_shape=...  30.4 us
    ppermute x8, starting transfers between devices, far(): return lax.ppermute(array, ('blk', 'str'), route)  13 us
    pallas_call x1, Pallas kernels, prepare(): pl.pallas_call(prepare_kernel, out_shape=[jax.ShapeDtypeStruct((window //...  6.15 us
    ppermute x7, starting transfers between devices, near(): return lax.ppermute(array, ('blk', 'str'), route)  5.55 us
    pallas_call x1, Pallas kernels, plain_terms(): pl.pallas_call(functools.partial(plain_kernel, count), out_shape=jax.Shap...  3.45 us
    ppermute x8, waiting for transfers between devices, far(): return lax.ppermute(array, ('blk', 'str'), route)  3.02 us
    pallas_call x1, Pallas kernels, add_terms(): pl.pallas_call(functools.partial(add_kernel, count, classes), out_shape=j...  1.88 us
  transfers between devices with their start and end apart: 15, of which 5 were waited for; matrix products, arithmetic and copies ran while one was open for 1% of the time, Pallas kernels for 14%

profile of v3, /device:TPU:0, one launch (start us, length us, event | category | flops | bytes accessed | tf_op | source)
XLA Modules:
  0.0 66.5 jit_solution(16373670934990518637)
XLA Ops:
  0.0 3.9 %collective-permute-start.3 = (bf16[64,1024]{1,0:T(8,128)(2,1)}, bf16[64,1024]{1,0:T(8,128)(2,1)S(1)}, u32[]{:S(2)}, u32[]{:S(2)}) collective-permute-start(bf16[64,1024]{1,0:T(8,128)(2,1)} %refs_0_.3), channel_id=1, source_target_pairs={{0,6},{1,7},{2,4},{3,5},{4,2},{5,3},{6,0},{7,1},{8,14},{9,15},{10,... | collective-permute-start | bytes 393224 | tf_op jit(solution)/shard_map/ppermute | solution.py:278
  3.9 0.5 collective-permute-start.2
  4.4 0.1 collective-permute-start.1
  4.5 0.0 collective-permute-start
  4.5 0.6 pad_add_fusion.place_ref
  5.1 6.2 %prepare.1 = (s32[32,2,25,8,128]{4,3,2,1,0:T(8,128)}, bf16[200,200]{1,0:T(8,128)(2,1)}) custom-call(s32[4]{0:T(128)} %pad_add_fusion.place_ref, s32[50,2,1024]{2,1,0:T(2,128)} %bitcast.10, s32[50,2,1024]{2,1,0:T(2,128)} %bitcast.11, bf16[50,2,50]{2,1,0:T(2,128)(2,1)} %bitcast.12), custom_call_target="tpu_custom_call" | custom-call | bytes 6553600 | tf_op jit(solution)/shard_map/prepare/pallas_call | solution.py:61
  11.2 0.0 collective-permute-done.3.refs_6_
  11.2 0.0 collective-permute-done.2.refs_4_
  11.2 0.0 copy-start.1
  11.2 0.0 collective-permute-done.1.refs_2_
  11.3 0.0 copy-start.2
  11.3 0.6 collective-permute-start.4
  11.8 0.1 collective-permute-start.5
  11.9 0.4 collective-permute-start.6
  12.4 0.0 collective-permute-done.refs_1_
  12.4 0.5 collective-permute-done.4.refs_3_
  12.8 0.4 collective-permute-done.5.refs_5_
  13.2 0.2 collective-permute-done.6.refs_7_
  13.4 0.0 copy-done
  13.4 0.0 copy-done.1
  13.4 0.0 copy-done.2
  13.4 0.0 copy-done.3
  13.4 0.1 copy-done.4
  13.5 0.4 copy-done.5
  13.8 0.2 copy-done.6
  14.0 30.4 %mixed.1 = (f32[64,256]{1,0:T(8,128)}, f32[64,256]{1,0:T(8,128)}, f32[64,256]{1,0:T(8,128)}, f32[64,256]{1,0:T(8,128)}, f32[64,256]{1,0:T(8,128)}, /*index=5*/f3...) custom-call(s32[4]{0:T(128)} %pad_add_fusion.place_ref, bf16[64,1024]{1,0:T(8,128)(2,1)} %refs_0_.3, ...), custom_call_target="tpu_custom_call" | custom-call | flops 22754099200 | bytes 6553600 | tf_op jit(solution)/shard_map/mixed/pallas_call | solution.py:173
  44.4 2.1 %collective-permute-start.7 = (f32[64,256]{1,0:T(8,128)}, f32[64,256]{1,0:T(8,128)S(1)}, u32[]{:S(2)}, u32[]{:S(2)}) collective-permute-start(f32[64,256]{1,0:T(8,128)} %get-tuple-element.27), channel_id=1, source_target_pairs={{0,8},{1,17},{2,10},{3,19},{4,12},{5,21},{6,14},{7,23},{8,0},{9,25... | collective-permute-start | bytes 196616 | tf_op jit(solution)/shard_map/ppermute | solution.py:286
  46.5 2.2 %collective-permute-start.8 = (f32[64,256]{1,0:T(8,128)}, f32[64,256]{1,0:T(8,128)S(1)}, u32[]{:S(2)}, u32[]{:S(2)}) collective-permute-start(f32[64,256]{1,0:T(8,128)} %get-tuple-element.28), channel_id=1, source_target_pairs={{0,9},{1,16},{2,11},{3,18},{4,13},{5,20},{6,15},{7,22},{8,1},{9,24... | collective-permute-start | bytes 196616 | tf_op jit(solution)/shard_map/ppermute | solution.py:286
  48.8 1.4 %collective-permute-start.9 = (f32[64,256]{1,0:T(8,128)}, f32[64,256]{1,0:T(8,128)S(1)}, u32[]{:S(2)}, u32[]{:S(2)}) collective-permute-start(f32[64,256]{1,0:T(8,128)} %get-tuple-element.29), channel_id=1, source_target_pairs={{0,10},{1,19},{2,8},{3,17},{4,14},{5,23},{6,12},{7,21},{8,2},{9,27... | collective-permute-start | bytes 196616 | tf_op jit(solution)/shard_map/ppermute | solution.py:286
  50.1 0.1 collective-permute-start.10
  50.2 2.5 %collective-permute-start.11 = (f32[64,256]{1,0:T(8,128)}, f32[64,256]{1,0:T(8,128)S(1)}, u32[]{:S(2)}, u32[]{:S(2)}) collective-permute-start(f32[64,256]{1,0:T(8,128)} %get-tuple-element.31), channel_id=1, source_target_pairs={{0,12},{1,21},{2,14},{3,23},{4,8},{5,17},{6,10},{7,19},{8,4},{9,29... | collective-permute-start | bytes 196616 | tf_op jit(solution)/shard_map/ppermute | solution.py:286
  52.7 0.0 collective-permute-done.7.refs_0_
  52.7 2.2 %collective-permute-start.12 = (f32[64,256]{1,0:T(8,128)}, f32[64,256]{1,0:T(8,128)S(1)}, u32[]{:S(2)}, u32[]{:S(2)}) collective-permute-start(f32[64,256]{1,0:T(8,128)} %get-tuple-element.32), channel_id=1, source_target_pairs={{0,13},{1,20},{2,15},{3,22},{4,9},{5,16},{6,11},{7,18},{8,5},{9,28... | collective-permute-start | bytes 196616 | tf_op jit(solution)/shard_map/ppermute | solution.py:286
  55.0 0.0 collective-permute-done.8.refs_1_
  55.0 2.3 %collective-permute-start.13 = (f32[64,256]{1,0:T(8,128)}, f32[64,256]{1,0:T(8,128)S(1)}, u32[]{:S(2)}, u32[]{:S(2)}) collective-permute-start(f32[64,256]{1,0:T(8,128)} %get-tuple-element.33), channel_id=1, source_target_pairs={{0,14},{1,23},{2,12},{3,21},{4,10},{5,19},{6,8},{7,17},{8,6},{9,31... | collective-permute-start | bytes 196616 | tf_op jit(solution)/shard_map/ppermute | solution.py:286
  57.3 0.0 collective-permute-done.9.refs_2_
  57.3 0.1 collective-permute-start.14
  57.4 3.5 %plain.1.base_ref = f32[64,1024]{1,0:T(8,128)} custom-call(s32[4]{0:T(128)} %pad_add_fusion.place_ref, bf16[64,1024]{1,0:T(8,128)(2,1)} %refs_0_.3, bf16[64,1024]{1,0:T(8,128)(2,1)} %copy-done.3, bf16[64,1024]{1,0:T(8,128)(2,1)} %copy-done.2, bf16[64,1024]{1,0:T(8,128)(2,1)} %copy-done.4, bf16[64,1024]{1,0:T(8,128)(2,1)} %copy-done.1, ...), custom_call_target="tpu_custom_call" | custom-call | flops 201326592 | bytes 3145728 | tf_op jit(solution)/shard_map/plain/pallas_call | solution.py:217
  60.9 0.0 collective-permute-done.10.refs_3_
  60.9 0.0 collective-permute-done.11.refs_4_
  60.9 0.0 copy-start.11
  60.9 0.0 collective-permute-done.12.refs_5_
  60.9 0.0 copy-start.12
  60.9 0.6 collective-permute-done.13.refs_6_
  61.5 2.4 %collective-permute-done.14.refs_7_ = f32[64,256]{1,0:T(8,128)S(1)} collective-permute-done((f32[64,256]{1,0:T(8,128)}, f32[64,256]{1,0:T(8,128)S(1)}, u32[]{:S(2)}, u32[]{:S(2)}) %collective-permute-start.14) | collective-permute-done | bytes 65568 | tf_op jit(solution)/shard_map/ppermute | solution.py:286
  63.9 0.0 copy-done.8
  64.0 0.6 copy-done.14
  64.6 1.9 %add.13 = f32[64,1024]{1,0:T(8,128)} custom-call(s32[4]{0:T(128)} %pad_add_fusion.place_ref, f32[64,1024]{1,0:T(8,128)} %plain.1.base_ref, f32[64,256]{1,0:T(8,128)} %copy-done.7, f32[64,256]{1,0:T(8,128)} %copy-done.8, f32[64,256]{1,0:T(8,128)} %copy-done.9, f32[64,256]{1,0:T(8,128)} %copy-done.10, f32[64,256]{1,0:T(8,128)} %copy-done.11, ...), custom_call_target="tpu_custom_call" | custom-call | tf_op jit(solution)/shard_map/add/pallas_call | solution.py:248
  (17 shorter events, 0.0 us)
Async XLA Ops:
  0.0 11.2 %collective-permute-start.3 = (bf16[64,1024]{1,0:T(8,128)(2,1)}, bf16[64,1024]{1,0:T(8,128)(2,1)S(1)}, u32[]{:S(2)}, u32[]{:S(2)}) collective-permute-start(bf16[64,1024]{1,0:T(8,128)(2,1)} %refs_0_.3), channel_id=1, source_target_pairs={{0,6},{1,7},{2,4},{3,5},{4,2},{5,3},{6,0},{7,1},{8,14},{9,15},{10,... | collective-permute-start | bytes 393224 | tf_op jit(solution)/shard_map/ppermute | solution.py:278
  3.9 7.3 %collective-permute-start.2 = (bf16[64,1024]{1,0:T(8,128)(2,1)}, bf16[64,1024]{1,0:T(8,128)(2,1)S(1)}, u32[]{:S(2)}, u32[]{:S(2)}) collective-permute-start(bf16[64,1024]{1,0:T(8,128)(2,1)} %refs_0_.3), channel_id=1, source_target_pairs={{0,4},{1,5},{2,6},{3,7},{4,0},{5,1},{6,2},{7,3},{8,12},{9,13},{10,... | collective-permute-start | bytes 393224 | tf_op jit(solution)/shard_map/ppermute | solution.py:278
  4.4 6.9 %collective-permute-start.1 = (bf16[64,1024]{1,0:T(8,128)(2,1)}, bf16[64,1024]{1,0:T(8,128)(2,1)S(1)}, u32[]{:S(2)}, u32[]{:S(2)}) collective-permute-start(bf16[64,1024]{1,0:T(8,128)(2,1)} %refs_0_.3), channel_id=1, source_target_pairs={{0,2},{1,3},{2,0},{3,1},{4,6},{5,7},{6,4},{7,5},{8,10},{9,11},{10,... | collective-permute-start | bytes 393224 | tf_op jit(solution)/shard_map/ppermute | solution.py:278
  4.5 7.9 %collective-permute-start = (bf16[64,1024]{1,0:T(8,128)(2,1)}, bf16[64,1024]{1,0:T(8,128)(2,1)S(1)}, u32[]{:S(2)}, u32[]{:S(2)}) collective-permute-start(bf16[64,1024]{1,0:T(8,128)(2,1)} %refs_0_.3), channel_id=1, source_target_pairs={{0,1},{1,0},{2,3},{3,2},{4,5},{5,4},{6,7},{7,6},{8,9},{9,8},{10,11... | collective-permute-start | bytes 393224 | tf_op jit(solution)/shard_map/ppermute | solution.py:278
  11.2 2.2 %copy-start = (bf16[64,1024]{1,0:T(8,128)(2,1)}, bf16[64,1024]{1,0:T(8,128)(2,1)S(1)}, u32[]{:S(2)}) copy-start(bf16[64,1024]{1,0:T(8,128)(2,1)S(1)} %collective-permute-done.3.refs_6_) | copy-start | bytes 393220
  11.2 2.1 %copy-start.1 = (bf16[64,1024]{1,0:T(8,128)(2,1)}, bf16[64,1024]{1,0:T(8,128)(2,1)S(1)}, u32[]{:S(2)}) copy-start(bf16[64,1024]{1,0:T(8,128)(2,1)S(1)} %collective-permute-done.2.refs_4_) | copy-start | bytes 393220
  11.3 2.1 %copy-start.2 = (bf16[64,1024]{1,0:T(8,128)(2,1)}, bf16[64,1024]{1,0:T(8,128)(2,1)S(1)}, u32[]{:S(2)}) copy-start(bf16[64,1024]{1,0:T(8,128)(2,1)S(1)} %collective-permute-done.1.refs_2_) | copy-start | bytes 393220
  11.3 1.6 %collective-permute-start.4 = (bf16[64,1024]{1,0:T(8,128)(2,1)S(1)}, bf16[64,1024]{1,0:T(8,128)(2,1)S(1)}, u32[]{:S(2)}, u32[]{:S(2)}) collective-permute-start(bf16[64,1024]{1,0:T(8,128)(2,1)S(1)} %collective-permute-done.1.refs_2_), channel_id=1, source_target_pairs={{0,1},{1,0},{2,3},{3,2},{4,5},{5,4},{6,7},{7,6},{8,9},{9,8},{10,11... | collective-permute-start | bytes 393224 | tf_op jit(solution)/shard_map/ppermute | solution.py:278
  11.8 1.3 %collective-permute-start.5 = (bf16[64,1024]{1,0:T(8,128)(2,1)S(1)}, bf16[64,1024]{1,0:T(8,128)(2,1)S(1)}, u32[]{:S(2)}, u32[]{:S(2)}) collective-permute-start(bf16[64,1024]{1,0:T(8,128)(2,1)S(1)} %collective-permute-done.2.refs_4_), channel_id=1, source_target_pairs={{0,1},{1,0},{2,3},{3,2},{4,5},{5,4},{6,7},{7,6},{8,9},{9,8},{10,11... | collective-permute-start | bytes 393224 | tf_op jit(solution)/shard_map/ppermute | solution.py:278
  11.9 1.5 %collective-permute-start.6 = (bf16[64,1024]{1,0:T(8,128)(2,1)S(1)}, bf16[64,1024]{1,0:T(8,128)(2,1)S(1)}, u32[]{:S(2)}, u32[]{:S(2)}) collective-permute-start(bf16[64,1024]{1,0:T(8,128)(2,1)S(1)} %collective-permute-done.3.refs_6_), channel_id=1, source_target_pairs={{0,1},{1,0},{2,3},{3,2},{4,5},{5,4},{6,7},{7,6},{8,9},{9,8},{10,11... | collective-permute-start | bytes 393224 | tf_op jit(solution)/shard_map/ppermute | solution.py:278
  12.4 1.0 %copy-start.3 = (bf16[64,1024]{1,0:T(8,128)(2,1)}, bf16[64,1024]{1,0:T(8,128)(2,1)S(1)}, u32[]{:S(2)}) copy-start(bf16[64,1024]{1,0:T(8,128)(2,1)S(1)} %collective-permute-done.refs_1_) | copy-start | bytes 393220
  12.8 0.7 copy-start.4
  13.2 0.6 copy-start.5
  13.4 0.6 copy-start.6
  44.4 8.3 %collective-permute-start.7 = (f32[64,256]{1,0:T(8,128)}, f32[64,256]{1,0:T(8,128)S(1)}, u32[]{:S(2)}, u32[]{:S(2)}) collective-permute-start(f32[64,256]{1,0:T(8,128)} %get-tuple-element.27), channel_id=1, source_target_pairs={{0,8},{1,17},{2,10},{3,19},{4,12},{5,21},{6,14},{7,23},{8,0},{9,25... | collective-permute-start | bytes 196616 | tf_op jit(solution)/shard_map/ppermute | solution.py:286
  46.5 8.4 %collective-permute-start.8 = (f32[64,256]{1,0:T(8,128)}, f32[64,256]{1,0:T(8,128)S(1)}, u32[]{:S(2)}, u32[]{:S(2)}) collective-permute-start(f32[64,256]{1,0:T(8,128)} %get-tuple-element.28), channel_id=1, source_target_pairs={{0,9},{1,16},{2,11},{3,18},{4,13},{5,20},{6,15},{7,22},{8,1},{9,24... | collective-permute-start | bytes 196616 | tf_op jit(solution)/shard_map/ppermute | solution.py:286
  48.8 8.5 %collective-permute-start.9 = (f32[64,256]{1,0:T(8,128)}, f32[64,256]{1,0:T(8,128)S(1)}, u32[]{:S(2)}, u32[]{:S(2)}) collective-permute-start(f32[64,256]{1,0:T(8,128)} %get-tuple-element.29), channel_id=1, source_target_pairs={{0,10},{1,19},{2,8},{3,17},{4,14},{5,23},{6,12},{7,21},{8,2},{9,27... | collective-permute-start | bytes 196616 | tf_op jit(solution)/shard_map/ppermute | solution.py:286
  50.1 10.7 %collective-permute-start.10 = (f32[64,256]{1,0:T(8,128)}, f32[64,256]{1,0:T(8,128)S(1)}, u32[]{:S(2)}, u32[]{:S(2)}) collective-permute-start(f32[64,256]{1,0:T(8,128)} %get-tuple-element.30), channel_id=1, source_target_pairs={{0,11},{1,18},{2,9},{3,16},{4,15},{5,22},{6,13},{7,20},{8,3},{9,26... | collective-permute-start | bytes 196616 | tf_op jit(solution)/shard_map/ppermute | solution.py:286
  50.2 10.7 %collective-permute-start.11 = (f32[64,256]{1,0:T(8,128)}, f32[64,256]{1,0:T(8,128)S(1)}, u32[]{:S(2)}, u32[]{:S(2)}) collective-permute-start(f32[64,256]{1,0:T(8,128)} %get-tuple-element.31), channel_id=1, source_target_pairs={{0,12},{1,21},{2,14},{3,23},{4,8},{5,17},{6,10},{7,19},{8,4},{9,29... | collective-permute-start | bytes 196616 | tf_op jit(solution)/shard_map/ppermute | solution.py:286
  52.7 11.2 %copy-start.7 = (f32[64,256]{1,0:T(8,128)}, f32[64,256]{1,0:T(8,128)S(1)}, u32[]{:S(2)}) copy-start(f32[64,256]{1,0:T(8,128)S(1)} %collective-permute-done.7.refs_0_) | copy-start | bytes 196612
  52.7 8.1 %collective-permute-start.12 = (f32[64,256]{1,0:T(8,128)}, f32[64,256]{1,0:T(8,128)S(1)}, u32[]{:S(2)}, u32[]{:S(2)}) collective-permute-start(f32[64,256]{1,0:T(8,128)} %get-tuple-element.32), channel_id=1, source_target_pairs={{0,13},{1,20},{2,15},{3,22},{4,9},{5,16},{6,11},{7,18},{8,5},{9,28... | collective-permute-start | bytes 196616 | tf_op jit(solution)/shard_map/ppermute | solution.py:286
  55.0 9.0 %copy-start.8 = (f32[64,256]{1,0:T(8,128)}, f32[64,256]{1,0:T(8,128)S(1)}, u32[]{:S(2)}) copy-start(f32[64,256]{1,0:T(8,128)S(1)} %collective-permute-done.8.refs_1_) | copy-start | bytes 196612
  55.0 6.5 %collective-permute-start.13 = (f32[64,256]{1,0:T(8,128)}, f32[64,256]{1,0:T(8,128)S(1)}, u32[]{:S(2)}, u32[]{:S(2)}) collective-permute-start(f32[64,256]{1,0:T(8,128)} %get-tuple-element.33), channel_id=1, source_target_pairs={{0,14},{1,23},{2,12},{3,21},{4,10},{5,19},{6,8},{7,17},{8,6},{9,31... | collective-permute-start | bytes 196616 | tf_op jit(solution)/shard_map/ppermute | solution.py:286
  57.3 6.7 %copy-start.9 = (f32[64,256]{1,0:T(8,128)}, f32[64,256]{1,0:T(8,128)S(1)}, u32[]{:S(2)}) copy-start(f32[64,256]{1,0:T(8,128)S(1)} %collective-permute-done.9.refs_2_) | copy-start | bytes 196612
  57.3 6.6 %collective-permute-start.14 = (f32[64,256]{1,0:T(8,128)}, f32[64,256]{1,0:T(8,128)S(1)}, u32[]{:S(2)}, u32[]{:S(2)}) collective-permute-start(f32[64,256]{1,0:T(8,128)} %get-tuple-element.34), channel_id=1, source_target_pairs={{0,15},{1,22},{2,13},{3,20},{4,11},{5,18},{6,9},{7,16},{8,7},{9,30... | collective-permute-start | bytes 196616 | tf_op jit(solution)/shard_map/ppermute | solution.py:286
  60.9 3.1 %copy-start.10 = (f32[64,256]{1,0:T(8,128)}, f32[64,256]{1,0:T(8,128)S(1)}, u32[]{:S(2)}) copy-start(f32[64,256]{1,0:T(8,128)S(1)} %collective-permute-done.10.refs_3_) | copy-start | bytes 196612
  60.9 3.1 %copy-start.11 = (f32[64,256]{1,0:T(8,128)}, f32[64,256]{1,0:T(8,128)S(1)}, u32[]{:S(2)}) copy-start(f32[64,256]{1,0:T(8,128)S(1)} %collective-permute-done.11.refs_4_) | copy-start | bytes 196612
  60.9 3.0 %copy-start.12 = (f32[64,256]{1,0:T(8,128)}, f32[64,256]{1,0:T(8,128)S(1)}, u32[]{:S(2)}) copy-start(f32[64,256]{1,0:T(8,128)S(1)} %collective-permute-done.12.refs_5_) | copy-start | bytes 196612
  61.5 2.5 %copy-start.13 = (f32[64,256]{1,0:T(8,128)}, f32[64,256]{1,0:T(8,128)S(1)}, u32[]{:S(2)}) copy-start(f32[64,256]{1,0:T(8,128)S(1)} %collective-permute-done.13.refs_6_) | copy-start | bytes 196612
  64.0 0.6 copy-start.14

commit v4 on v2

v4 whole, which is shorter than its diff:
```python
import functools

import jax
import jax.numpy as jnp
from jax import lax
from jax.experimental import pallas as pl
from jax.experimental.pallas import tpu as pltpu
from jax.sharding import PartitionSpec as P

QUAD = 4
VMEM_LIMIT = 46 * 1024 * 1024


def whole():
    return pl.BlockSpec(memory_space=pltpu.VMEM)


def any_place():
    return pl.BlockSpec(memory_space=pl.ANY)


def in_hbm():
    return pl.BlockSpec(memory_space=pltpu.HBM)


def prepare_kernel(code_ref, integral_ref, rows_ref, out_ref, kron_ref, copied_ref, arrived):
    pairs, window = code_ref.shape
    quads = window // QUAD
    size = pairs * QUAD
    copy = pltpu.make_async_copy(rows_ref, copied_ref, arrived)
    copy.start()
    codes = code_ref[...]
    for part in range(QUAD):
        out_ref[pl.ds(part, pairs, QUAD), :quads] = codes[:, part * quads : (part + 1) * quads]
    spread = (
        lax.broadcasted_iota(jnp.int32, (size, pairs), 0) // QUAD
        == lax.broadcasted_iota(jnp.int32, (size, pairs), 1)
    ).astype(jnp.bfloat16)
    tall = jnp.dot(spread, integral_ref[...], preferred_element_type=jnp.float32)
    wide = lax.dot_general(
        tall.astype(jnp.bfloat16),
        spread,
        (((1,), (1,)), ((), ())),
        preferred_element_type=jnp.float32,
    )
    row = lax.broadcasted_iota(jnp.int32, (size, size), 0)
    column = lax.broadcasted_iota(jnp.int32, (size, size), 1)
    kron_ref[...] = jnp.where(row % QUAD == column % QUAD, wide, 0.0).astype(jnp.bfloat16)
    copy.wait()


def prepare(codes, integrals, rows):
    pairs = codes.shape[0]
    size = pairs * QUAD
    return pl.pallas_call(
        prepare_kernel,
        out_shape=[
            jax.ShapeDtypeStruct((size, 128), jnp.int32),
            jax.ShapeDtypeStruct((size, size), jnp.bfloat16),
            jax.ShapeDtypeStruct(rows.shape, rows.dtype),
        ],
        in_specs=[whole(), whole(), any_place()],
        out_specs=[whole(), whole(), any_place()],
        scratch_shapes=[pltpu.SemaphoreType.DMA],
        compiler_params=pltpu.CompilerParams(vmem_limit_bytes=VMEM_LIMIT),
        cost_estimate=pl.CostEstimate(
            flops=0, bytes_accessed=4 * 1024 * 1024, transcendentals=0
        ),
        name="prepare",
    )(codes, integrals, rows)


def pair_images(step, quads, code_ref, kron_ref, turned):
    beta_count, rows = turned.shape
    size = kron_ref.shape[0]
    halves = size // (2 * QUAD)
    own = pltpu.roll(code_ref[...], 128 - step * quads, 1)
    codes = jnp.concatenate(
        [jnp.broadcast_to(own[:, quad : quad + 1], (size, 128)) for quad in range(quads)], axis=0
    )
    target = jnp.right_shift(codes, 2)
    value = ((codes & 3) - 1).astype(jnp.float32)
    lane = lax.broadcasted_iota(jnp.int32, codes.shape, 1)
    onehot = jnp.concatenate(
        [
            jnp.where(lane == target - start, value, 0.0).astype(jnp.bfloat16)
            for start in range(0, beta_count, 128)
        ],
        axis=1,
    )
    coupled = jnp.dot(onehot, turned[...], preferred_element_type=jnp.float32)
    coupled = coupled.astype(jnp.bfloat16)
    low = lax.broadcasted_iota(jnp.int32, (halves, 8, rows), 1) < QUAD
    evens, odds = [], []
    for pair in range(quads // 2):
        first, second = [
            jnp.dot(
                kron_ref[...],
                coupled[at * size : (at + 1) * size],
                preferred_element_type=jnp.float32,
            ).reshape(halves, 8, rows)
            for at in (2 * pair, 2 * pair + 1)
        ]
        evens.append(jnp.where(low, first, pltpu.roll(second, QUAD, 1)))
        odds.append(jnp.where(low, pltpu.roll(first, QUAD, 1), second))
    return [jnp.concatenate(side, axis=1).astype(jnp.bfloat16) for side in (evens, odds)]


def mixed_kernel(count, quads, bundle, place_ref, *refs):
    pieces = refs[:count]
    code_ref, kron_ref, alpha_ref = refs[count : count + 3]
    outs = refs[count + 3 : count + 3 + count // 2]
    rest = refs[count + 3 + count // 2 :]
    held, turned, images, total, lanes, ordered, indices, signs, arrived = rest
    step = pl.program_id(0)
    local_rows = pieces[0].shape[0]
    halves, _, window, block_rows = images.shape
    columns = quads * QUAD

    @pl.when(step == 0)
    def _():
        copies = [
            pltpu.make_async_copy(
                pieces[at], held.at[pl.ds(at * local_rows, local_rows)], arrived.at[at]
            )
            for at in range(count)
        ]
        for copy in copies:
            copy.start()
        for copy in copies:
            copy.wait()
        for start in range(0, block_rows, 128):
            turned[:, start : start + 128] = held[start : start + 128, :].T

    place = pl.ds(pl.multiple_of(step * columns, columns), columns)
    even, odd = pair_images(step, quads, code_ref, kron_ref, turned)
    images[:, 0, place, :] = even
    images[:, 1, place, :] = odd

    @pl.when(step == pl.num_programs(0) - 1)
    def _():
        total[...] = jnp.zeros_like(total)
        indices[...] = jnp.right_shift(alpha_ref[...], 2)
        signs[...] = ((alpha_ref[...] & 3) - 1).astype(jnp.float32)
        position = lax.broadcasted_iota(jnp.int32, (block_rows, block_rows), 0)
        position = jnp.bitwise_xor(position, place_ref[0] * local_rows)

        def body(at, carry):
            term = None
            for offset in range(bundle):
                pair = bundle * at + offset
                selector = jnp.where(
                    position == indices[pl.ds(pair, 1), :], signs[pl.ds(pair, 1), :], 0.0
                ).astype(jnp.bfloat16)
                part = jnp.dot(
                    images[lax.div(pair, 2), lax.rem(pair, 2)],
                    selector,
                    preferred_element_type=jnp.float32,
                )
                term = part if term is None else term + part
            total[...] += term
            return carry

        lax.fori_loop(0, 2 * halves // bundle, body, 0)
        quad_count = window // QUAD
        for at in range(block_rows // 128):
            rows = slice(at * 128, (at + 1) * 128)
            lanes[at] = total[:, rows]
            ordered[rows, :] = jnp.concatenate(
                [lanes[at, pl.ds(part, quad_count, QUAD), :] for part in range(QUAD)], axis=0
            ).T
        for at in range(count):
            start = pl.multiple_of((place_ref[0] ^ at) * local_rows, local_rows)
            rows = slice(at % 2 * local_rows, (at % 2 + 1) * local_rows)
            outs[at // 2][rows, :] = ordered[pl.ds(start, local_rows), :]


def mixed_pieces(place, pieces, codes, kron, alpha_codes, window):
    count = len(pieces)
    local_rows, beta_count = pieces[0].shape
    pairs, block_rows = alpha_codes.shape
    columns = min(128, window, 128 * 512 // block_rows)
    bundle = next(size for size in (25, 10, 5, 2, 1) if pairs % size == 0)
    flops = 2 * window * pairs * block_rows * (beta_count + pairs * QUAD + block_rows)
    return pl.pallas_call(
        functools.partial(mixed_kernel, count, columns // QUAD, bundle),
        out_shape=[jax.ShapeDtypeStruct((2 * local_rows, window), jnp.float32)] * (count // 2),
        grid_spec=pltpu.PrefetchScalarGridSpec(
            num_scalar_prefetch=1,
            grid=(window // columns,),
            in_specs=[any_place()] * count
            + [whole()] * 3,
            out_specs=[whole()] * (count // 2),
            scratch_shapes=[
                pltpu.VMEM((block_rows, beta_count), jnp.bfloat16),
                pltpu.VMEM((beta_count, block_rows), jnp.bfloat16),
                pltpu.VMEM((pairs // 2, 2, window, block_rows), jnp.bfloat16),
                pltpu.VMEM((window, block_rows), jnp.float32),
                pltpu.VMEM((block_rows // 128, window, 128), jnp.float32),
                pltpu.VMEM((block_rows, window), jnp.float32),
                pltpu.VMEM((pairs, block_rows), jnp.int32),
                pltpu.VMEM((pairs, block_rows), jnp.float32),
                pltpu.SemaphoreType.DMA((count,)),
            ],
        ),
        compiler_params=pltpu.CompilerParams(
            dimension_semantics=("arbitrary",), vmem_limit_bytes=VMEM_LIMIT
        ),
        cost_estimate=pl.CostEstimate(flops=flops, bytes_accessed=1 << 20, transcendentals=0),
        name="mixed",
    )(place, *pieces, codes, kron, alpha_codes)


def plain_kernel(count, place_ref, *refs):
    pieces = refs[:count]
    alpha_source, beta_source, out_ref, block, alpha_ref, beta_ref, arrived = refs[count:]
    local_rows = pieces[0].shape[0]
    copies = [
        pltpu.make_async_copy(alpha_source, alpha_ref, arrived.at[count]),
        pltpu.make_async_copy(beta_source, beta_ref, arrived.at[count + 1]),
    ]
    for at in range(count):
        start = pl.multiple_of((place_ref[0] ^ at) * local_rows, local_rows)
        copies.append(
            pltpu.make_async_copy(
                pieces[at], block.at[pl.ds(start, local_rows)], arrived.at[at]
            )
        )
    for copy in copies:
        copy.start()
    for copy in copies:
        copy.wait()
    start = pl.multiple_of(place_ref[0] * local_rows, local_rows)
    out_ref[...] = jnp.dot(
        alpha_ref[...], block[...], preferred_element_type=jnp.float32
    ) + jnp.dot(
        block[pl.ds(start, local_rows), :], beta_ref[...], preferred_element_type=jnp.float32
    )


def plain_terms(place, pieces, alpha_operator, beta_operator):
    count = len(pieces)
    local_rows, beta_count = pieces[0].shape
    block_rows = alpha_operator.shape[1]
    return pl.pallas_call(
        functools.partial(plain_kernel, count),
        out_shape=jax.ShapeDtypeStruct((local_rows, beta_count), jnp.float32),
        in_specs=[pl.BlockSpec(memory_space=pltpu.SMEM)]
        + [any_place()] * count
        + [in_hbm(), in_hbm()],
        out_specs=whole(),
        scratch_shapes=[
            pltpu.VMEM((block_rows, beta_count), jnp.bfloat16),
            pltpu.VMEM(alpha_operator.shape, jnp.bfloat16),
            pltpu.VMEM(beta_operator.shape, jnp.bfloat16),
            pltpu.SemaphoreType.DMA((count + 2,)),
        ],
        compiler_params=pltpu.CompilerParams(vmem_limit_bytes=VMEM_LIMIT),
        cost_estimate=pl.CostEstimate(
            flops=2 * local_rows * beta_count * (beta_count + block_rows),
            bytes_accessed=2 * beta_count * (beta_count + block_rows),
            transcendentals=0,
        ),
        name="plain",
    )(place, *pieces, alpha_operator, beta_operator)


def add_kernel(count, classes, place_ref, base_ref, *refs):
    own, passed = refs[:count], refs[count : 2 * count]
    out_ref, held, arrived = refs[2 * count :]
    local_rows, window = held.shape[1:]
    copies = []
    for at in range(count):
        for side, source in enumerate((own[at], passed[at])):
            slot = 2 * at + side
            rows = source.at[pl.ds(side * local_rows, local_rows)]
            copies.append(pltpu.make_async_copy(rows, held.at[slot], arrived.at[slot]))
    for copy in copies:
        copy.start()
    chunk = place_ref[0] // classes
    for at in range(count):
        copies[2 * at].wait()
        copies[2 * at + 1].wait()
        columns = pl.ds(pl.multiple_of((chunk ^ at) * window, window), window)
        out_ref[:, columns] = base_ref[:, columns] + (held[2 * at] + held[2 * at + 1])


def add_terms(place, base, own, passed, classes):
    count = len(own)
    rows, window = own[0].shape
    return pl.pallas_call(
        functools.partial(add_kernel, count, classes),
        out_shape=jax.ShapeDtypeStruct(base.shape, jnp.float32),
        in_specs=[pl.BlockSpec(memory_space=pltpu.SMEM), whole()] + [any_place()] * (2 * count),
        out_specs=whole(),
        scratch_shapes=[
            pltpu.VMEM((2 * count, rows // 2, window), jnp.float32),
            pltpu.SemaphoreType.DMA((2 * count,)),
        ],
        compiler_params=pltpu.CompilerParams(vmem_limit_bytes=VMEM_LIMIT),
        name="add",
    )(place, base, *own, *passed)


def local(
    civec, beta_index, beta_sign, alpha_index, alpha_sign, integrals, beta_operator, alpha_operator
):
    classes, pair_count = integrals.shape[:2]
    local_rows, beta_count = civec.shape
    count = lax.axis_size("str")
    blocks = lax.axis_size("blk")
    block_rows = local_rows * count
    window = beta_count * classes // count
    block_at, place = lax.axis_index("blk"), lax.axis_index("str")
    symmetry = place % classes
    partner = jnp.bitwise_xor(block_at, 1 << symmetry)

    def near(array, distance):
        route = [
            (blk * count + at, blk * count + (at ^ distance))
            for blk in range(blocks)
            for at in range(count)
        ]
        return lax.ppermute(array, ("blk", "str"), route)

    def far(array, distance):
        route = [
            (blk * count + at, (blk ^ (1 << at % classes)) * count + (at ^ distance))
            for blk in range(blocks)
            for at in range(count)
        ]
        return lax.ppermute(array, ("blk", "str"), route)

    def one_class(array, start, width):
        return lax.dynamic_slice(array, (symmetry, 0, start), (1, array.shape[1], width))[0]

    def row_codes(index, sign, start, width):
        return one_class(index, start, width) * 4 + one_class(sign, start, width) + 1

    beta_codes = row_codes(beta_index, beta_sign, place // classes * window, window)
    alpha_codes = row_codes(alpha_index, alpha_sign, partner * block_rows, block_rows)
    own_integrals = one_class(integrals, 0, pair_count)
    arrived = [near(civec, at) for at in range(2, count, 2)]
    place = place.astype(jnp.int32).reshape(1)
    codes, kron, rows = prepare(beta_codes, own_integrals, civec)
    codes, alpha_codes, *arrived = lax.optimization_barrier((codes, alpha_codes, *arrived))
    straight = [rows] + arrived
    crossed = [near(piece, 1) for piece in [civec] + arrived]
    pieces = [piece for two in zip(straight, crossed) for piece in two]

    sent = mixed_pieces(place, pieces, codes, kron, alpha_codes, window)
    own = [far(sent[at], 2 * at) for at in range(count // 2)]
    base = plain_terms(place, pieces, alpha_operator, beta_operator)
    own[-1], base = lax.optimization_barrier((own[-1], base))
    passed = [near(rows, 1) for rows in own]
    return add_terms(place, base, own, passed, classes)


def solution(mesh):
    placed = (P(("blk", "str"), None), P(), P(), P(), P(), P(), P(), P(("blk", "str"), None))
    return jax.shard_map(
        local, mesh=mesh, in_specs=placed, out_specs=P(("blk", "str"), None), check_vma=False
    )
```

time: 80.4 us -> 62.9 us (0.78)
  Pallas kernels: 41.6 us -> 33 us
  local copies, waits for them, and re-layouts: 11.8 us -> 3.71 us
  waiting for transfers between devices: 8.36 us -> 14 us
  starting transfers between devices: 17.4 us -> 11.9 us
    unnamed x35 -> x9, local copies, waits for them, and re-layouts: 11.8 us -> 0.92 us
    pallas_call x2, Pallas kernels: 36.3 us -> 29.1 us  [the longest x1 28.6 us: mixed_pieces(): pl.pallas_call(functools.partial(mixed_kernel, count, columns // QUAD, bu...]
    ppermute x8 -> x4, starting transfers between devices: 12.4 us -> 5.91 us  [far(): return lax.ppermute(array, ('blk', 'str'), route)]
    ppermute x8 -> x4, waiting for transfers between devices: 1.89 us -> 7.2 us  [far(): return lax.ppermute(array, ('blk', 'str'), route)]
    dynamic_slice x0 -> x3, local copies, waits for them, and re-layouts: none -> 2.8 us  [one_class(): lax.dynamic_slice(array, (symmetry, 0, start), (1, array.shape[1], width))]
    pallas_call x1, Pallas kernels: 3.46 us -> 2.4 us  [plain_terms(): pl.pallas_call(functools.partial(plain_kernel, count), out_shape=jax.Shap...]
    ppermute x7 -> x11, starting transfers between devices: 4.97 us -> 6 us  [near(): return lax.ppermute(array, ('blk', 'str'), route)]
    ppermute x7 -> x11, waiting for transfers between devices: 6.47 us -> 6.79 us  [near(): return lax.ppermute(array, ('blk', 'str'), route)]
  transfers between devices with their start and end apart: 15 -> 15, of which waited for: 3 -> 9; matrix products, arithmetic and copies ran while one was open for 14% -> 5% of each run, Pallas kernels for 12% -> 5%
where the time goes in v4:
time: 62.9 us; the launch traced here: 62.7 us
  Pallas kernels  33 us (52%)
  waiting for transfers between devices  14 us (22%)
  starting transfers between devices  11.9 us (19%)
  local copies, waits for them, and re-layouts  3.71 us (6%)
    pallas_call x1, Pallas kernels, mixed_pieces(): pl.pallas_call(functools.partial(mixed_kernel, count, columns // QUAD, bu...  28.6 us
    ppermute x4, waiting for transfers between devices, far(): return lax.ppermute(array, ('blk', 'str'), route)  7.2 us
    ppermute x11, waiting for transfers between devices, near(): return lax.ppermute(array, ('blk', 'str'), route)  6.79 us
    ppermute x11, starting transfers between devices, near(): return lax.ppermute(array, ('blk', 'str'), route)  6 us
    ppermute x4, starting transfers between devices, far(): return lax.ppermute(array, ('blk', 'str'), route)  5.91 us
    dynamic_slice x3, local copies, waits for them, and re-layouts, one_class(): lax.dynamic_slice(array, (symmetry, 0, start), (1, array.shape[1], width))  2.8 us
    pallas_call x1, Pallas kernels, plain_terms(): pl.pallas_call(functools.partial(plain_kernel, count), out_shape=jax.Shap...  2.4 us
    pallas_call x1, Pallas kernels, add_terms(): pl.pallas_call(functools.partial(add_kernel, count, classes), out_shape=j...  1.49 us
  transfers between devices with their start and end apart: 15, of which 9 were waited for; matrix products, arithmetic and copies ran while one was open for 5% of the time, Pallas kernels for 5%

profile of v4, /device:TPU:0, one launch (start us, length us, event | category | flops | bytes accessed | tf_op | source)
XLA Modules:
  0.0 62.7 jit_solution(6752321562988047194)
XLA Ops:
  0.0 0.0 copy-start
  0.0 2.9 %collective-permute-start.1 = (bf16[64,1024]{1,0:T(8,128)(2,1)}, bf16[64,1024]{1,0:T(8,128)(2,1)S(1)}, u32[]{:S(2)}, u32[]{:S(2)}) collective-permute-start(bf16[64,1024]{1,0:T(8,128)(2,1)} %rows_ref.1), channel_id=1, source_target_pairs={{0,2},{1,3},{2,0},{3,1},{4,6},{5,7},{6,4},{7,5},{8,10},{9,11},{10,... | collective-permute-start | bytes 393224 | tf_op jit(solution)/shard_map/ppermute | solution.py:324
  2.9 0.0 collective-permute-start
  2.9 1.5 %collective-permute-start.3 = (bf16[64,1024]{1,0:T(8,128)(2,1)}, bf16[64,1024]{1,0:T(8,128)(2,1)S(1)}, u32[]{:S(2)}, u32[]{:S(2)}) collective-permute-start(bf16[64,1024]{1,0:T(8,128)(2,1)} %rows_ref.1), channel_id=1, source_target_pairs={{0,6},{1,7},{2,4},{3,5},{4,2},{5,3},{6,0},{7,1},{8,14},{9,15},{10,... | collective-permute-start | bytes 393224 | tf_op jit(solution)/shard_map/ppermute | solution.py:324
  4.4 0.1 collective-permute-start.2
  4.6 0.0 copy-done
  4.6 1.2 %constant_dynamic-slice_fusion.3 = (s32[1,50,256]{2,0,1:T(1,128)S(1)}, s32[1,50,256]{2,0,1:T(1,128)S(1)}) fusion(s32[2,50,1024]{2,0,1:T(2,128)} %param.10, s32[]{:T(128)S(6)} %select_n.27, s32[]{:T(128)S(6)} %select_n.29, s32[2,50,1024]{2,0,1:T(2,128)} %param.9), kind=kLoop, calls=%fused_computation.12 | loop fusion | bytes 204808 | tf_op jit(solution)/shard_map/dynamic_slice | solution.py:335
  5.9 0.0 copy-start.2
  5.9 0.9 %copy-done.2 = bf16[64,1024]{1,0:T(8,128)(2,1)S(1)} copy-done((bf16[64,1024]{1,0:T(8,128)(2,1)S(1)}, bf16[64,1024]{1,0:T(8,128)(2,1)}, u32[]{:S(2)}) %copy-start.2) | copy-done | bytes 131096
  6.8 0.4 prepare.1
  7.2 1.5 %constant_dynamic-slice_fusion = (s32[1,50,512]{2,0,1:T(1,128)S(1)}, s32[1,50,512]{2,0,1:T(1,128)S(1)}) fusion(s32[2,50,2048]{2,0,1:T(2,128)} %param.12, s32[]{:T(128)S(6)} %select_n.27, s32[]{:T(128)S(6)} %select_n.30, s32[2,50,2048]{2,0,1:T(2,128)} %param.11), kind=kLoop, calls=%fused_computation.9 | loop fusion | bytes 409608 | tf_op jit(solution)/shard_map/dynamic_slice | solution.py:335
  8.8 0.0 collective-permute-done.1.refs_2_
  8.8 2.0 %collective-permute-done.3.refs_6_ = bf16[64,1024]{1,0:T(8,128)(2,1)S(1)} collective-permute-done((bf16[64,1024]{1,0:T(8,128)(2,1)}, bf16[64,1024]{1,0:T(8,128)(2,1)S(1)}, u32[]{:S(2)}, u32[]{:S(2)}) %collective-permute-start.3) | collective-permute-done | bytes 131104 | tf_op jit(solution)/shard_map/ppermute | solution.py:324
  10.8 2.2 %collective-permute-done.2.refs_4_ = bf16[64,1024]{1,0:T(8,128)(2,1)S(1)} collective-permute-done((bf16[64,1024]{1,0:T(8,128)(2,1)}, bf16[64,1024]{1,0:T(8,128)(2,1)S(1)}, u32[]{:S(2)}, u32[]{:S(2)}) %collective-permute-start.2) | collective-permute-done | bytes 131104 | tf_op jit(solution)/shard_map/ppermute | solution.py:324
  12.9 0.0 collective-permute-start.4
  12.9 0.5 collective-permute-start.5
  13.4 0.0 collective-permute-start.6
  13.4 0.0 collective-permute-done.refs_1_
  13.4 0.8 %collective-permute-done.4.refs_3_ = bf16[64,1024]{1,0:T(8,128)(2,1)S(1)} collective-permute-done((bf16[64,1024]{1,0:T(8,128)(2,1)S(1)}, bf16[64,1024]{1,0:T(8,128)(2,1)S(1)}, u32[]{:S(2)}, u32[]{:S(2)}) %collective-permute-start.4) | collective-permute-done | bytes 131104 | tf_op jit(solution)/shard_map/ppermute | solution.py:324
  14.3 0.2 collective-permute-done.5.refs_5_
  14.5 0.3 collective-permute-done.6.refs_7_
  14.8 0.0 copy-start.1
  14.8 0.0 copy-start.3
  14.8 28.6 %mixed.1 = (f32[128,256]{1,0:T(8,128)S(1)}, f32[128,256]{1,0:T(8,128)S(1)}, f32[128,256]{1,0:T(8,128)S(1)}, f32[128,256]{1,0:T(8,128)S(1)}) custom-call(s32[1]{0:T(128)} %bitcast.place_ref, bf16[64,1024]{1,0:T(8,128)(2,1)S(1)} %get-tuple-element.19.refs_0_, bf16[64,1024]{1,0:T(8,128)(2,1)S(1)} %collective-permute-done.refs_1_, ...), custom_call_target="tpu_custom_call" | custom-call | flops 22754099200 | bytes 1048576 | tf_op jit(solution)/shard_map/mixed/pallas_call | solution.py:185
  43.4 2.5 %collective-permute-start.7 = (f32[128,256]{1,0:T(8,128)S(1)}, f32[128,256]{1,0:T(8,128)S(1)}, u32[]{:S(2)}, u32[]{:S(2)}) collective-permute-start(f32[128,256]{1,0:T(8,128)S(1)} %get-tuple-element.27), channel_id=1, source_target_pairs={{0,14},{1,23},{2,12},{3,21},{4,10},{5,19},{6,8},{7,17},{8,6},{9,31... | collective-permute-start | bytes 393224 | tf_op jit(solution)/shard_map/ppermute | solution.py:332
  46.0 0.4 collective-permute-start.8
  46.4 1.7 %collective-permute-start.9 = (f32[128,256]{1,0:T(8,128)S(1)}, f32[128,256]{1,0:T(8,128)S(1)}, u32[]{:S(2)}, u32[]{:S(2)}) collective-permute-start(f32[128,256]{1,0:T(8,128)S(1)} %get-tuple-element.30), channel_id=1, source_target_pairs={{0,10},{1,19},{2,8},{3,17},{4,14},{5,23},{6,12},{7,21},{8,2},{9,27... | collective-permute-start | bytes 393224 | tf_op jit(solution)/shard_map/ppermute | solution.py:332
  48.1 1.3 %collective-permute-start.10 = (f32[128,256]{1,0:T(8,128)S(1)}, f32[128,256]{1,0:T(8,128)S(1)}, u32[]{:S(2)}, u32[]{:S(2)}) collective-permute-start(f32[128,256]{1,0:T(8,128)S(1)} %get-tuple-element.31), channel_id=1, source_target_pairs={{0,12},{1,21},{2,14},{3,23},{4,8},{5,17},{6,10},{7,19},{8,4},{9,29... | collective-permute-start | bytes 393224 | tf_op jit(solution)/shard_map/ppermute | solution.py:332
  49.3 0.0 copy-done.1
  49.3 0.0 copy-done.3
  49.3 2.4 %plain.1.base_ref = f32[64,1024]{1,0:T(8,128)S(1)} custom-call(s32[1]{0:T(128)} %bitcast.place_ref, bf16[64,1024]{1,0:T(8,128)(2,1)S(1)} %get-tuple-element.19.refs_0_, bf16[64,1024]{1,0:T(8,128)(2,1)S(1)} %collective-permute-done.refs_1_, bf16[64,1024]{1,0:T(8,128)(2,1)S(1)} %collective-permute-done.1.refs_2_, ...), custom_call_target="tpu_custom_call" | custom-call | flops 201326592 | bytes 3145728 | tf_op jit(solution)/shard_map/plain/pallas_call | solution.py:245
  51.8 0.0 collective-permute-done.7.refs_3_
  51.8 0.9 %collective-permute-start.14 = (f32[128,256]{1,0:T(8,128)S(1)}, f32[128,256]{1,0:T(8,128)S(1)}, u32[]{:S(2)}, u32[]{:S(2)}) collective-permute-start(f32[128,256]{1,0:T(8,128)S(1)} %collective-permute-done.7.refs_3_), channel_id=1, source_target_pairs={{0,1},{1,0},{2,3},{3,2},{4,5},{5,4},{6,7},{7,6},{8,9},{9,8},{10,11... | collective-permute-start | bytes 393224 | tf_op jit(solution)/shard_map/ppermute | solution.py:324
  52.7 1.2 %collective-permute-done.8.refs_0_ = f32[128,256]{1,0:T(8,128)S(1)} collective-permute-done((f32[128,256]{1,0:T(8,128)S(1)}, f32[128,256]{1,0:T(8,128)S(1)}, u32[]{:S(2)}, u32[]{:S(2)}) %collective-permute-start.8) | collective-permute-done | bytes 131104 | tf_op jit(solution)/shard_map/ppermute | solution.py:332
  53.9 0.0 collective-permute-start.11
  53.9 2.9 %collective-permute-done.9.refs_1_ = f32[128,256]{1,0:T(8,128)S(1)} collective-permute-done((f32[128,256]{1,0:T(8,128)S(1)}, f32[128,256]{1,0:T(8,128)S(1)}, u32[]{:S(2)}, u32[]{:S(2)}) %collective-permute-start.9) | collective-permute-done | bytes 131104 | tf_op jit(solution)/shard_map/ppermute | solution.py:332
  56.8 0.0 collective-permute-start.12
  56.8 3.1 %collective-permute-done.10.refs_2_ = f32[128,256]{1,0:T(8,128)S(1)} collective-permute-done((f32[128,256]{1,0:T(8,128)S(1)}, f32[128,256]{1,0:T(8,128)S(1)}, u32[]{:S(2)}, u32[]{:S(2)}) %collective-permute-start.10) | collective-permute-done | bytes 131104 | tf_op jit(solution)/shard_map/ppermute | solution.py:332
  59.9 0.0 collective-permute-start.13
  59.9 0.0 collective-permute-done.14.refs_7_
  59.9 0.0 collective-permute-done.11.refs_4_
  59.9 0.0 collective-permute-done.12.refs_5_
  59.9 1.3 %collective-permute-done.13.refs_6_ = f32[128,256]{1,0:T(8,128)S(1)} collective-permute-done((f32[128,256]{1,0:T(8,128)S(1)}, f32[128,256]{1,0:T(8,128)S(1)}, u32[]{:S(2)}, u32[]{:S(2)}) %collective-permute-start.13) | collective-permute-done | bytes 131104 | tf_op jit(solution)/shard_map/ppermute | solution.py:324
  61.2 1.5 %add.76 = f32[64,1024]{1,0:T(8,128)} custom-call(s32[1]{0:T(128)} %bitcast.place_ref, f32[64,1024]{1,0:T(8,128)S(1)} %plain.1.base_ref, f32[128,256]{1,0:T(8,128)S(1)} %collective-permute-done.8.refs_0_, f32[128,256]{1,0:T(8,128)S(1)} %collective-permute-done.9.refs_1_, f32[128,256]{1,0:T(8,128)S(1)} %collective-permute-done.10.refs_2_, ...), custom_call_target="tpu_custom_call" | custom-call | tf_op jit(solution)/shard_map/add/pallas_call | solution.py:291
  (4 shorter events, 0.1 us)
Async XLA Ops:
  0.0 4.6 %copy-start = (bf16[2,50,50]{2,0,1:T(2,128)(2,1)S(1)}, bf16[2,50,50]{2,0,1:T(2,128)(2,1)}, u32[]{:S(2)}) copy-start(bf16[2,50,50]{2,0,1:T(2,128)(2,1)} %param.13) | copy-start | bytes 30004
  0.0 8.8 %collective-permute-start.1 = (bf16[64,1024]{1,0:T(8,128)(2,1)}, bf16[64,1024]{1,0:T(8,128)(2,1)S(1)}, u32[]{:S(2)}, u32[]{:S(2)}) collective-permute-start(bf16[64,1024]{1,0:T(8,128)(2,1)} %rows_ref.1), channel_id=1, source_target_pairs={{0,2},{1,3},{2,0},{3,1},{4,6},{5,7},{6,4},{7,5},{8,10},{9,11},{10,... | collective-permute-start | bytes 393224 | tf_op jit(solution)/shard_map/ppermute | solution.py:324
  2.9 10.5 %collective-permute-start = (bf16[64,1024]{1,0:T(8,128)(2,1)}, bf16[64,1024]{1,0:T(8,128)(2,1)S(1)}, u32[]{:S(2)}, u32[]{:S(2)}) collective-permute-start(bf16[64,1024]{1,0:T(8,128)(2,1)} %rows_ref.1), channel_id=1, source_target_pairs={{0,1},{1,0},{2,3},{3,2},{4,5},{5,4},{6,7},{7,6},{8,9},{9,8},{10,11... | collective-permute-start | bytes 393224 | tf_op jit(solution)/shard_map/ppermute | solution.py:324
  2.9 7.8 %collective-permute-start.3 = (bf16[64,1024]{1,0:T(8,128)(2,1)}, bf16[64,1024]{1,0:T(8,128)(2,1)S(1)}, u32[]{:S(2)}, u32[]{:S(2)}) collective-permute-start(bf16[64,1024]{1,0:T(8,128)(2,1)} %rows_ref.1), channel_id=1, source_target_pairs={{0,6},{1,7},{2,4},{3,5},{4,2},{5,3},{6,0},{7,1},{8,14},{9,15},{10,... | collective-permute-start | bytes 393224 | tf_op jit(solution)/shard_map/ppermute | solution.py:324
  4.4 8.5 %collective-permute-start.2 = (bf16[64,1024]{1,0:T(8,128)(2,1)}, bf16[64,1024]{1,0:T(8,128)(2,1)S(1)}, u32[]{:S(2)}, u32[]{:S(2)}) collective-permute-start(bf16[64,1024]{1,0:T(8,128)(2,1)} %rows_ref.1), channel_id=1, source_target_pairs={{0,4},{1,5},{2,6},{3,7},{4,0},{5,1},{6,2},{7,3},{8,12},{9,13},{10,... | collective-permute-start | bytes 393224 | tf_op jit(solution)/shard_map/ppermute | solution.py:324
  5.9 0.9 %copy-start.2 = (bf16[64,1024]{1,0:T(8,128)(2,1)S(1)}, bf16[64,1024]{1,0:T(8,128)(2,1)}, u32[]{:S(2)}) copy-start(bf16[64,1024]{1,0:T(8,128)(2,1)} %rows_ref.1) | copy-start | bytes 393220
  12.9 1.3 %collective-permute-start.4 = (bf16[64,1024]{1,0:T(8,128)(2,1)S(1)}, bf16[64,1024]{1,0:T(8,128)(2,1)S(1)}, u32[]{:S(2)}, u32[]{:S(2)}) collective-permute-start(bf16[64,1024]{1,0:T(8,128)(2,1)S(1)} %collective-permute-done.1.refs_2_), channel_id=1, source_target_pairs={{0,1},{1,0},{2,3},{3,2},{4,5},{5,4},{6,7},{7,6},{8,9},{9,8},{10,11... | collective-permute-start | bytes 393224 | tf_op jit(solution)/shard_map/ppermute | solution.py:324
  12.9 1.5 %collective-permute-start.5 = (bf16[64,1024]{1,0:T(8,128)(2,1)S(1)}, bf16[64,1024]{1,0:T(8,128)(2,1)S(1)}, u32[]{:S(2)}, u32[]{:S(2)}) collective-permute-start(bf16[64,1024]{1,0:T(8,128)(2,1)S(1)} %collective-permute-done.2.refs_4_), channel_id=1, source_target_pairs={{0,1},{1,0},{2,3},{3,2},{4,5},{5,4},{6,7},{7,6},{8,9},{9,8},{10,11... | collective-permute-start | bytes 393224 | tf_op jit(solution)/shard_map/ppermute | solution.py:324
  13.4 1.3 %collective-permute-start.6 = (bf16[64,1024]{1,0:T(8,128)(2,1)S(1)}, bf16[64,1024]{1,0:T(8,128)(2,1)S(1)}, u32[]{:S(2)}, u32[]{:S(2)}) collective-permute-start(bf16[64,1024]{1,0:T(8,128)(2,1)S(1)} %collective-permute-done.3.refs_6_), channel_id=1, source_target_pairs={{0,1},{1,0},{2,3},{3,2},{4,5},{5,4},{6,7},{7,6},{8,9},{9,8},{10,11... | collective-permute-start | bytes 393224 | tf_op jit(solution)/shard_map/ppermute | solution.py:324
  14.8 34.6 %copy-start.1 = (bf16[1024,1024]{1,0:T(8,128)(2,1)S(1)}, bf16[1024,1024]{1,0:T(8,128)(2,1)}, u32[]{:S(2)}) copy-start(bf16[1024,1024]{1,0:T(8,128)(2,1)} %refs_9_.1) | copy-start | bytes 6291460
  14.8 34.6 %copy-start.3 = (bf16[64,512]{1,0:T(8,128)(2,1)S(1)}, bf16[64,512]{1,0:T(8,128)(2,1)}, u32[]{:S(2)}) copy-start(bf16[64,512]{1,0:T(8,128)(2,1)} %refs_8_.1) | copy-start | bytes 196612
  43.4 8.3 %collective-permute-start.7 = (f32[128,256]{1,0:T(8,128)S(1)}, f32[128,256]{1,0:T(8,128)S(1)}, u32[]{:S(2)}, u32[]{:S(2)}) collective-permute-start(f32[128,256]{1,0:T(8,128)S(1)} %get-tuple-element.27), channel_id=1, source_target_pairs={{0,14},{1,23},{2,12},{3,21},{4,10},{5,19},{6,8},{7,17},{8,6},{9,31... | collective-permute-start | bytes 393224 | tf_op jit(solution)/shard_map/ppermute | solution.py:332
  46.0 8.0 %collective-permute-start.8 = (f32[128,256]{1,0:T(8,128)S(1)}, f32[128,256]{1,0:T(8,128)S(1)}, u32[]{:S(2)}, u32[]{:S(2)}) collective-permute-start(f32[128,256]{1,0:T(8,128)S(1)} %get-tuple-element.29), channel_id=1, source_target_pairs={{0,8},{1,17},{2,10},{3,19},{4,12},{5,21},{6,14},{7,23},{8,0},{9,25... | collective-permute-start | bytes 393224 | tf_op jit(solution)/shard_map/ppermute | solution.py:332
  46.4 10.4 %collective-permute-start.9 = (f32[128,256]{1,0:T(8,128)S(1)}, f32[128,256]{1,0:T(8,128)S(1)}, u32[]{:S(2)}, u32[]{:S(2)}) collective-permute-start(f32[128,256]{1,0:T(8,128)S(1)} %get-tuple-element.30), channel_id=1, source_target_pairs={{0,10},{1,19},{2,8},{3,17},{4,14},{5,23},{6,12},{7,21},{8,2},{9,27... | collective-permute-start | bytes 393224 | tf_op jit(solution)/shard_map/ppermute | solution.py:332
  48.1 11.8 %collective-permute-start.10 = (f32[128,256]{1,0:T(8,128)S(1)}, f32[128,256]{1,0:T(8,128)S(1)}, u32[]{:S(2)}, u32[]{:S(2)}) collective-permute-start(f32[128,256]{1,0:T(8,128)S(1)} %get-tuple-element.31), channel_id=1, source_target_pairs={{0,12},{1,21},{2,14},{3,23},{4,8},{5,17},{6,10},{7,19},{8,4},{9,29... | collective-permute-start | bytes 393224 | tf_op jit(solution)/shard_map/ppermute | solution.py:332
  51.8 8.1 %collective-permute-start.14 = (f32[128,256]{1,0:T(8,128)S(1)}, f32[128,256]{1,0:T(8,128)S(1)}, u32[]{:S(2)}, u32[]{:S(2)}) collective-permute-start(f32[128,256]{1,0:T(8,128)S(1)} %collective-permute-done.7.refs_3_), channel_id=1, source_target_pairs={{0,1},{1,0},{2,3},{3,2},{4,5},{5,4},{6,7},{7,6},{8,9},{9,8},{10,11... | collective-permute-start | bytes 393224 | tf_op jit(solution)/shard_map/ppermute | solution.py:324
  53.9 6.0 %collective-permute-start.11 = (f32[128,256]{1,0:T(8,128)S(1)}, f32[128,256]{1,0:T(8,128)S(1)}, u32[]{:S(2)}, u32[]{:S(2)}) collective-permute-start(f32[128,256]{1,0:T(8,128)S(1)} %collective-permute-done.8.refs_0_), channel_id=1, source_target_pairs={{0,1},{1,0},{2,3},{3,2},{4,5},{5,4},{6,7},{7,6},{8,9},{9,8},{10,11... | collective-permute-start | bytes 393224 | tf_op jit(solution)/shard_map/ppermute | solution.py:324
  56.8 3.1 %collective-permute-start.12 = (f32[128,256]{1,0:T(8,128)S(1)}, f32[128,256]{1,0:T(8,128)S(1)}, u32[]{:S(2)}, u32[]{:S(2)}) collective-permute-start(f32[128,256]{1,0:T(8,128)S(1)} %collective-permute-done.9.refs_1_), channel_id=1, source_target_pairs={{0,1},{1,0},{2,3},{3,2},{4,5},{5,4},{6,7},{7,6},{8,9},{9,8},{10,11... | collective-permute-start | bytes 393224 | tf_op jit(solution)/shard_map/ppermute | solution.py:324
  59.9 1.3 %collective-permute-start.13 = (f32[128,256]{1,0:T(8,128)S(1)}, f32[128,256]{1,0:T(8,128)S(1)}, u32[]{:S(2)}, u32[]{:S(2)}) collective-permute-start(f32[128,256]{1,0:T(8,128)S(1)} %collective-permute-done.10.refs_2_), channel_id=1, source_target_pairs={{0,1},{1,0},{2,3},{3,2},{4,5},{5,4},{6,7},{7,6},{8,9},{9,8},{10,11... | collective-permute-start | bytes 393224 | tf_op jit(solution)/shard_map/ppermute | solution.py:324

commit v5 on v4

--- a/solution.py
+++ b/solution.py
@@ -78,12 +78,12 @@
     codes = jnp.concatenate(
         [jnp.broadcast_to(own[:, quad : quad + 1], (size, 128)) for quad in range(quads)], axis=0
     )
-    target = jnp.right_shift(codes, 2)
-    value = ((codes & 3) - 1).astype(jnp.float32)
-    lane = lax.broadcasted_iota(jnp.int32, codes.shape, 1)
+    target = jnp.right_shift(codes, 2).astype(jnp.int16)
+    value = ((codes & 3) - 1).astype(jnp.float32).astype(jnp.bfloat16)
+    lane = lax.broadcasted_iota(jnp.int32, codes.shape, 1).astype(jnp.int16)
     onehot = jnp.concatenate(
         [
-            jnp.where(lane == target - start, value, 0.0).astype(jnp.bfloat16)
+            jnp.where(lane == target - jnp.int16(start), value, jnp.zeros((), jnp.bfloat16))
             for start in range(0, beta_count, 128)
         ],
         axis=1,
@@ -340,18 +340,18 @@
     beta_codes = row_codes(beta_index, beta_sign, place // classes * window, window)
     alpha_codes = row_codes(alpha_index, alpha_sign, partner * block_rows, block_rows)
     own_integrals = one_class(integrals, 0, pair_count)
-    arrived = [near(civec, at) for at in range(2, count, 2)]
     place = place.astype(jnp.int32).reshape(1)
     codes, kron, rows = prepare(beta_codes, own_integrals, civec)
-    codes, alpha_codes, *arrived = lax.optimization_barrier((codes, alpha_codes, *arrived))
-    straight = [rows] + arrived
+    later, place = lax.optimization_barrier((civec, place))
+    arrived = [near(later if at == 2 else civec, at) for at in range(2, count, 2)]
+    codes, alpha_codes, arrived[0] = lax.optimization_barrier((codes, alpha_codes, arrived[0]))
     crossed = [near(piece, 1) for piece in [civec] + arrived]
-    pieces = [piece for two in zip(straight, crossed) for piece in two]
+    pieces = [piece for two in zip([rows] + arrived, crossed) for piece in two]
 
     sent = mixed_pieces(place, pieces, codes, kron, alpha_codes, window)
-    own = [far(sent[at], 2 * at) for at in range(count // 2)]
+    own = [far(sent[at], 2 * at) for at in reversed(range(count // 2))][::-1]
     base = plain_terms(place, pieces, alpha_operator, beta_operator)
-    own[-1], base = lax.optimization_barrier((own[-1], base))
+    own[0], base = lax.optimization_barrier((own[0], base))
     passed = [near(rows, 1) for rows in own]
     return add_terms(place, base, own, passed, classes)
 

time: 62.9 us -> 60.1 us (0.955)
  waiting for transfers between devices: 14 us -> 11.6 us
    ppermute x11, waiting for transfers between devices: 6.79 us -> 5.13 us  [near(): return lax.ppermute(array, ('blk', 'str'), route)]
    ppermute x4, waiting for transfers between devices: 7.2 us -> 6.43 us  [far(): return lax.ppermute(array, ('blk', 'str'), route)]
  transfers between devices with their start and end apart: 15 -> 15, of which waited for: 9 -> 8; matrix products, arithmetic and copies ran while one was open for 5% -> 5% of each run, Pallas kernels for 5% -> 5%
where the time goes in v5:
time: 60.1 us; the launch traced here: 60 us
  Pallas kernels  32.4 us (54%)
  starting transfers between devices  12.1 us (20%)
  waiting for transfers between devices  11.6 us (19%)
  local copies, waits for them, and re-layouts  3.71 us (6%)
    pallas_call x1, Pallas kernels, mixed_pieces(): pl.pallas_call(functools.partial(mixed_kernel, count, columns // QUAD, bu...  28.1 us
    ppermute x4, waiting for transfers between devices, far(): return lax.ppermute(array, ('blk', 'str'), route)  6.43 us
    ppermute x11, starting transfers between devices, near(): return lax.ppermute(array, ('blk', 'str'), route)  6.17 us
    ppermute x4, starting transfers between devices, far(): return lax.ppermute(array, ('blk', 'str'), route)  5.91 us
    ppermute x11, waiting for transfers between devices, near(): return lax.ppermute(array, ('blk', 'str'), route)  5.13 us
    dynamic_slice x3, local copies, waits for them, and re-layouts, one_class(): lax.dynamic_slice(array, (symmetry, 0, start), (1, array.shape[1], width))  2.8 us
    pallas_call x1, Pallas kernels, plain_terms(): pl.pallas_call(functools.partial(plain_kernel, count), out_shape=jax.Shap...  2.4 us
    pallas_call x1, Pallas kernels, add_terms(): pl.pallas_call(functools.partial(add_kernel, count, classes), out_shape=j...  1.49 us
  transfers between devices with their start and end apart: 15, of which 8 were waited for; matrix products, arithmetic and copies ran while one was open for 5% of the time, Pallas kernels for 5%

profile of v5, /device:TPU:0, one launch (start us, length us, event | category | flops | bytes accessed | tf_op | source)
XLA Modules:
  0.0 60.0 jit_solution(10566886677624269198)
XLA Ops:
  0.0 0.0 copy-start
  0.0 0.5 collective-permute-start
  0.5 3.5 %collective-permute-start.5 = (bf16[64,1024]{1,0:T(8,128)(2,1)}, bf16[64,1024]{1,0:T(8,128)(2,1)S(1)}, u32[]{:S(2)}, u32[]{:S(2)}) collective-permute-start(bf16[64,1024]{1,0:T(8,128)(2,1)} %rows_ref.1), channel_id=1, source_target_pairs={{0,6},{1,7},{2,4},{3,5},{4,2},{5,3},{6,0},{7,1},{8,14},{9,15},{10,... | collective-permute-start | bytes 393224 | tf_op jit(solution)/shard_map/ppermute | solution.py:324
  4.0 0.5 collective-permute-start.3
  4.5 0.2 collective-permute-start.1
  4.6 0.0 copy-done
  4.7 1.2 %constant_dynamic-slice_fusion.3 = (s32[1,50,256]{2,0,1:T(1,128)S(1)}, s32[1,50,256]{2,0,1:T(1,128)S(1)}) fusion(s32[2,50,1024]{2,0,1:T(2,128)} %param.10, s32[]{:T(128)S(6)} %select_n.27, s32[]{:T(128)S(6)} %select_n.29, s32[2,50,1024]{2,0,1:T(2,128)} %param.9), kind=kLoop, calls=%fused_computation.12 | loop fusion | bytes 204808 | tf_op jit(solution)/shard_map/dynamic_slice | solution.py:335
  6.0 0.0 copy-start.2
  6.0 0.9 %copy-done.2 = bf16[64,1024]{1,0:T(8,128)(2,1)S(1)} copy-done((bf16[64,1024]{1,0:T(8,128)(2,1)S(1)}, bf16[64,1024]{1,0:T(8,128)(2,1)}, u32[]{:S(2)}) %copy-start.2) | copy-done | bytes 131096
  6.9 0.4 prepare.1
  7.3 1.5 %constant_dynamic-slice_fusion = (s32[1,50,512]{2,0,1:T(1,128)S(1)}, s32[1,50,512]{2,0,1:T(1,128)S(1)}) fusion(s32[2,50,2048]{2,0,1:T(2,128)} %param.12, s32[]{:T(128)S(6)} %select_n.27, s32[]{:T(128)S(6)} %select_n.30, s32[2,50,2048]{2,0,1:T(2,128)} %param.11), kind=kLoop, calls=%fused_computation.9 | loop fusion | bytes 409608 | tf_op jit(solution)/shard_map/dynamic_slice | solution.py:335
  8.9 2.5 %collective-permute-done.1.refs_2_ = bf16[64,1024]{1,0:T(8,128)(2,1)S(1)} collective-permute-done((bf16[64,1024]{1,0:T(8,128)(2,1)}, bf16[64,1024]{1,0:T(8,128)(2,1)S(1)}, u32[]{:S(2)}, u32[]{:S(2)}) %collective-permute-start.1) | collective-permute-done | bytes 131104 | tf_op jit(solution)/shard_map/ppermute | solution.py:324
  11.4 0.0 collective-permute-done.5.refs_6_
  11.4 0.0 collective-permute-start.6
  11.4 0.0 collective-permute-done.3.refs_4_
  11.4 0.5 collective-permute-start.4
  11.9 0.1 collective-permute-start.2
  12.0 0.0 collective-permute-done.refs_1_
  12.0 0.8 %collective-permute-done.6.refs_7_ = bf16[64,1024]{1,0:T(8,128)(2,1)S(1)} collective-permute-done((bf16[64,1024]{1,0:T(8,128)(2,1)S(1)}, bf16[64,1024]{1,0:T(8,128)(2,1)S(1)}, u32[]{:S(2)}, u32[]{:S(2)}) %collective-permute-start.6) | collective-permute-done | bytes 131104 | tf_op jit(solution)/shard_map/ppermute | solution.py:324
  12.7 0.2 collective-permute-done.4.refs_5_
  12.9 0.3 collective-permute-done.2.refs_3_
  13.3 0.0 copy-start.1
  13.3 0.0 copy-start.3
  13.3 28.1 %mixed.1 = (f32[128,256]{1,0:T(8,128)S(1)}, f32[128,256]{1,0:T(8,128)S(1)}, f32[128,256]{1,0:T(8,128)S(1)}, f32[128,256]{1,0:T(8,128)S(1)}) custom-call(s32[1]{0:T(128)} %bitcast.place_ref, bf16[64,1024]{1,0:T(8,128)(2,1)S(1)} %get-tuple-element.20.refs_0_, bf16[64,1024]{1,0:T(8,128)(2,1)S(1)} %collective-permute-done.refs_1_, ...), custom_call_target="tpu_custom_call" | custom-call | flops 22754099200 | bytes 1048576 | tf_op jit(solution)/shard_map/mixed/pallas_call | solution.py:185
  41.4 1.6 %collective-permute-start.7 = (f32[128,256]{1,0:T(8,128)S(1)}, f32[128,256]{1,0:T(8,128)S(1)}, u32[]{:S(2)}, u32[]{:S(2)}) collective-permute-start(f32[128,256]{1,0:T(8,128)S(1)} %get-tuple-element.27), channel_id=1, source_target_pairs={{0,8},{1,17},{2,10},{3,19},{4,12},{5,21},{6,14},{7,23},{8,0},{9,25... | collective-permute-start | bytes 393224 | tf_op jit(solution)/shard_map/ppermute | solution.py:332
  43.0 1.4 %collective-permute-start.8 = (f32[128,256]{1,0:T(8,128)S(1)}, f32[128,256]{1,0:T(8,128)S(1)}, u32[]{:S(2)}, u32[]{:S(2)}) collective-permute-start(f32[128,256]{1,0:T(8,128)S(1)} %get-tuple-element.30), channel_id=1, source_target_pairs={{0,10},{1,19},{2,8},{3,17},{4,14},{5,23},{6,12},{7,21},{8,2},{9,27... | collective-permute-start | bytes 393224 | tf_op jit(solution)/shard_map/ppermute | solution.py:332
  44.4 1.5 %collective-permute-start.9 = (f32[128,256]{1,0:T(8,128)S(1)}, f32[128,256]{1,0:T(8,128)S(1)}, u32[]{:S(2)}, u32[]{:S(2)}) collective-permute-start(f32[128,256]{1,0:T(8,128)S(1)} %get-tuple-element.31), channel_id=1, source_target_pairs={{0,12},{1,21},{2,14},{3,23},{4,8},{5,17},{6,10},{7,19},{8,4},{9,29... | collective-permute-start | bytes 393224 | tf_op jit(solution)/shard_map/ppermute | solution.py:332
  45.9 1.4 %collective-permute-start.10 = (f32[128,256]{1,0:T(8,128)S(1)}, f32[128,256]{1,0:T(8,128)S(1)}, u32[]{:S(2)}, u32[]{:S(2)}) collective-permute-start(f32[128,256]{1,0:T(8,128)S(1)} %get-tuple-element.32), channel_id=1, source_target_pairs={{0,14},{1,23},{2,12},{3,21},{4,10},{5,19},{6,8},{7,17},{8,6},{9,31... | collective-permute-start | bytes 393224 | tf_op jit(solution)/shard_map/ppermute | solution.py:332
  47.3 0.0 copy-done.1
  47.3 0.0 copy-done.3
  47.3 2.4 %plain.1.base_ref = f32[64,1024]{1,0:T(8,128)S(1)} custom-call(s32[1]{0:T(128)} %bitcast.place_ref, bf16[64,1024]{1,0:T(8,128)(2,1)S(1)} %get-tuple-element.20.refs_0_, bf16[64,1024]{1,0:T(8,128)(2,1)S(1)} %collective-permute-done.refs_1_, bf16[64,1024]{1,0:T(8,128)(2,1)S(1)} %collective-permute-done.1.refs_2_, ...), custom_call_target="tpu_custom_call" | custom-call | flops 201326592 | bytes 3145728 | tf_op jit(solution)/shard_map/plain/pallas_call | solution.py:245
  49.7 0.0 collective-permute-done.7.refs_0_
  49.7 1.0 %collective-permute-start.11 = (f32[128,256]{1,0:T(8,128)S(1)}, f32[128,256]{1,0:T(8,128)S(1)}, u32[]{:S(2)}, u32[]{:S(2)}) collective-permute-start(f32[128,256]{1,0:T(8,128)S(1)} %collective-permute-done.7.refs_0_), channel_id=1, source_target_pairs={{0,1},{1,0},{2,3},{3,2},{4,5},{5,4},{6,7},{7,6},{8,9},{9,8},{10,11... | collective-permute-start | bytes 393224 | tf_op jit(solution)/shard_map/ppermute | solution.py:324
  50.7 1.2 %collective-permute-done.8.refs_1_ = f32[128,256]{1,0:T(8,128)S(1)} collective-permute-done((f32[128,256]{1,0:T(8,128)S(1)}, f32[128,256]{1,0:T(8,128)S(1)}, u32[]{:S(2)}, u32[]{:S(2)}) %collective-permute-start.8) | collective-permute-done | bytes 131104 | tf_op jit(solution)/shard_map/ppermute | solution.py:332
  51.9 0.0 collective-permute-start.12
  51.9 2.5 %collective-permute-done.9.refs_2_ = f32[128,256]{1,0:T(8,128)S(1)} collective-permute-done((f32[128,256]{1,0:T(8,128)S(1)}, f32[128,256]{1,0:T(8,128)S(1)}, u32[]{:S(2)}, u32[]{:S(2)}) %collective-permute-start.9) | collective-permute-done | bytes 131104 | tf_op jit(solution)/shard_map/ppermute | solution.py:332
  54.4 0.0 collective-permute-start.13
  54.4 2.7 %collective-permute-done.10.refs_3_ = f32[128,256]{1,0:T(8,128)S(1)} collective-permute-done((f32[128,256]{1,0:T(8,128)S(1)}, f32[128,256]{1,0:T(8,128)S(1)}, u32[]{:S(2)}, u32[]{:S(2)}) %collective-permute-start.10) | collective-permute-done | bytes 131104 | tf_op jit(solution)/shard_map/ppermute | solution.py:332
  57.1 0.0 collective-permute-start.14
  57.1 0.0 collective-permute-done.11.refs_4_
  57.1 0.0 collective-permute-done.12.refs_5_
  57.1 0.0 collective-permute-done.13.refs_6_
  57.1 1.3 %collective-permute-done.14.refs_7_ = f32[128,256]{1,0:T(8,128)S(1)} collective-permute-done((f32[128,256]{1,0:T(8,128)S(1)}, f32[128,256]{1,0:T(8,128)S(1)}, u32[]{:S(2)}, u32[]{:S(2)}) %collective-permute-start.14) | collective-permute-done | bytes 131104 | tf_op jit(solution)/shard_map/ppermute | solution.py:324
  58.5 1.5 %add.76 = f32[64,1024]{1,0:T(8,128)} custom-call(s32[1]{0:T(128)} %bitcast.place_ref, f32[64,1024]{1,0:T(8,128)S(1)} %plain.1.base_ref, f32[128,256]{1,0:T(8,128)S(1)} %collective-permute-done.7.refs_0_, f32[128,256]{1,0:T(8,128)S(1)} %collective-permute-done.8.refs_1_, f32[128,256]{1,0:T(8,128)S(1)} %collective-permute-done.9.refs_2_, ...), custom_call_target="tpu_custom_call" | custom-call | tf_op jit(solution)/shard_map/add/pallas_call | solution.py:291
  (4 shorter events, 0.1 us)
Async XLA Ops:
  0.0 4.6 %copy-start = (bf16[2,50,50]{2,0,1:T(2,128)(2,1)S(1)}, bf16[2,50,50]{2,0,1:T(2,128)(2,1)}, u32[]{:S(2)}) copy-start(bf16[2,50,50]{2,0,1:T(2,128)(2,1)} %param.13) | copy-start | bytes 30004
  0.0 12.0 %collective-permute-start = (bf16[64,1024]{1,0:T(8,128)(2,1)}, bf16[64,1024]{1,0:T(8,128)(2,1)S(1)}, u32[]{:S(2)}, u32[]{:S(2)}) collective-permute-start(bf16[64,1024]{1,0:T(8,128)(2,1)} %rows_ref.1), channel_id=1, source_target_pairs={{0,1},{1,0},{2,3},{3,2},{4,5},{5,4},{6,7},{7,6},{8,9},{9,8},{10,11... | collective-permute-start | bytes 393224 | tf_op jit(solution)/shard_map/ppermute | solution.py:324
  0.5 10.9 %collective-permute-start.5 = (bf16[64,1024]{1,0:T(8,128)(2,1)}, bf16[64,1024]{1,0:T(8,128)(2,1)S(1)}, u32[]{:S(2)}, u32[]{:S(2)}) collective-permute-start(bf16[64,1024]{1,0:T(8,128)(2,1)} %rows_ref.1), channel_id=1, source_target_pairs={{0,6},{1,7},{2,4},{3,5},{4,2},{5,3},{6,0},{7,1},{8,14},{9,15},{10,... | collective-permute-start | bytes 393224 | tf_op jit(solution)/shard_map/ppermute | solution.py:324
  4.0 7.4 %collective-permute-start.3 = (bf16[64,1024]{1,0:T(8,128)(2,1)}, bf16[64,1024]{1,0:T(8,128)(2,1)S(1)}, u32[]{:S(2)}, u32[]{:S(2)}) collective-permute-start(bf16[64,1024]{1,0:T(8,128)(2,1)} %rows_ref.1), channel_id=1, source_target_pairs={{0,4},{1,5},{2,6},{3,7},{4,0},{5,1},{6,2},{7,3},{8,12},{9,13},{10,... | collective-permute-start | bytes 393224 | tf_op jit(solution)/shard_map/ppermute | solution.py:324
  4.5 6.9 %collective-permute-start.1 = (bf16[64,1024]{1,0:T(8,128)(2,1)}, bf16[64,1024]{1,0:T(8,128)(2,1)S(1)}, u32[]{:S(2)}, u32[]{:S(2)}) collective-permute-start(bf16[64,1024]{1,0:T(8,128)(2,1)} %rows_ref.1), channel_id=1, source_target_pairs={{0,2},{1,3},{2,0},{3,1},{4,6},{5,7},{6,4},{7,5},{8,10},{9,11},{10,... | collective-permute-start | bytes 393224 | tf_op jit(solution)/shard_map/ppermute | solution.py:324
  6.0 0.9 %copy-start.2 = (bf16[64,1024]{1,0:T(8,128)(2,1)S(1)}, bf16[64,1024]{1,0:T(8,128)(2,1)}, u32[]{:S(2)}) copy-start(bf16[64,1024]{1,0:T(8,128)(2,1)} %rows_ref.1) | copy-start | bytes 393220
  11.4 1.3 %collective-permute-start.6 = (bf16[64,1024]{1,0:T(8,128)(2,1)S(1)}, bf16[64,1024]{1,0:T(8,128)(2,1)S(1)}, u32[]{:S(2)}, u32[]{:S(2)}) collective-permute-start(bf16[64,1024]{1,0:T(8,128)(2,1)S(1)} %collective-permute-done.5.refs_6_), channel_id=1, source_target_pairs={{0,1},{1,0},{2,3},{3,2},{4,5},{5,4},{6,7},{7,6},{8,9},{9,8},{10,11... | collective-permute-start | bytes 393224 | tf_op jit(solution)/shard_map/ppermute | solution.py:324
  11.4 1.5 %collective-permute-start.4 = (bf16[64,1024]{1,0:T(8,128)(2,1)S(1)}, bf16[64,1024]{1,0:T(8,128)(2,1)S(1)}, u32[]{:S(2)}, u32[]{:S(2)}) collective-permute-start(bf16[64,1024]{1,0:T(8,128)(2,1)S(1)} %collective-permute-done.3.refs_4_), channel_id=1, source_target_pairs={{0,1},{1,0},{2,3},{3,2},{4,5},{5,4},{6,7},{7,6},{8,9},{9,8},{10,11... | collective-permute-start | bytes 393224 | tf_op jit(solution)/shard_map/ppermute | solution.py:324
  11.9 1.3 %collective-permute-start.2 = (bf16[64,1024]{1,0:T(8,128)(2,1)S(1)}, bf16[64,1024]{1,0:T(8,128)(2,1)S(1)}, u32[]{:S(2)}, u32[]{:S(2)}) collective-permute-start(bf16[64,1024]{1,0:T(8,128)(2,1)S(1)} %collective-permute-done.1.refs_2_), channel_id=1, source_target_pairs={{0,1},{1,0},{2,3},{3,2},{4,5},{5,4},{6,7},{7,6},{8,9},{9,8},{10,11... | collective-permute-start | bytes 393224 | tf_op jit(solution)/shard_map/ppermute | solution.py:324
  13.3 34.0 %copy-start.1 = (bf16[1024,1024]{1,0:T(8,128)(2,1)S(1)}, bf16[1024,1024]{1,0:T(8,128)(2,1)}, u32[]{:S(2)}) copy-start(bf16[1024,1024]{1,0:T(8,128)(2,1)} %refs_9_.1) | copy-start | bytes 6291460
  13.3 34.0 %copy-start.3 = (bf16[64,512]{1,0:T(8,128)(2,1)S(1)}, bf16[64,512]{1,0:T(8,128)(2,1)}, u32[]{:S(2)}) copy-start(bf16[64,512]{1,0:T(8,128)(2,1)} %refs_8_.1) | copy-start | bytes 196612
  41.4 8.3 %collective-permute-start.7 = (f32[128,256]{1,0:T(8,128)S(1)}, f32[128,256]{1,0:T(8,128)S(1)}, u32[]{:S(2)}, u32[]{:S(2)}) collective-permute-start(f32[128,256]{1,0:T(8,128)S(1)} %get-tuple-element.27), channel_id=1, source_target_pairs={{0,8},{1,17},{2,10},{3,19},{4,12},{5,21},{6,14},{7,23},{8,0},{9,25... | collective-permute-start | bytes 393224 | tf_op jit(solution)/shard_map/ppermute | solution.py:332
  43.0 8.9 %collective-permute-start.8 = (f32[128,256]{1,0:T(8,128)S(1)}, f32[128,256]{1,0:T(8,128)S(1)}, u32[]{:S(2)}, u32[]{:S(2)}) collective-permute-start(f32[128,256]{1,0:T(8,128)S(1)} %get-tuple-element.30), channel_id=1, source_target_pairs={{0,10},{1,19},{2,8},{3,17},{4,14},{5,23},{6,12},{7,21},{8,2},{9,27... | collective-permute-start | bytes 393224 | tf_op jit(solution)/shard_map/ppermute | solution.py:332
  44.4 10.0 %collective-permute-start.9 = (f32[128,256]{1,0:T(8,128)S(1)}, f32[128,256]{1,0:T(8,128)S(1)}, u32[]{:S(2)}, u32[]{:S(2)}) collective-permute-start(f32[128,256]{1,0:T(8,128)S(1)} %get-tuple-element.31), channel_id=1, source_target_pairs={{0,12},{1,21},{2,14},{3,23},{4,8},{5,17},{6,10},{7,19},{8,4},{9,29... | collective-permute-start | bytes 393224 | tf_op jit(solution)/shard_map/ppermute | solution.py:332
  45.9 11.2 %collective-permute-start.10 = (f32[128,256]{1,0:T(8,128)S(1)}, f32[128,256]{1,0:T(8,128)S(1)}, u32[]{:S(2)}, u32[]{:S(2)}) collective-permute-start(f32[128,256]{1,0:T(8,128)S(1)} %get-tuple-element.32), channel_id=1, source_target_pairs={{0,14},{1,23},{2,12},{3,21},{4,10},{5,19},{6,8},{7,17},{8,6},{9,31... | collective-permute-start | bytes 393224 | tf_op jit(solution)/shard_map/ppermute | solution.py:332
  49.7 7.4 %collective-permute-start.11 = (f32[128,256]{1,0:T(8,128)S(1)}, f32[128,256]{1,0:T(8,128)S(1)}, u32[]{:S(2)}, u32[]{:S(2)}) collective-permute-start(f32[128,256]{1,0:T(8,128)S(1)} %collective-permute-done.7.refs_0_), channel_id=1, source_target_pairs={{0,1},{1,0},{2,3},{3,2},{4,5},{5,4},{6,7},{7,6},{8,9},{9,8},{10,11... | collective-permute-start | bytes 393224 | tf_op jit(solution)/shard_map/ppermute | solution.py:324
  51.9 5.2 %collective-permute-start.12 = (f32[128,256]{1,0:T(8,128)S(1)}, f32[128,256]{1,0:T(8,128)S(1)}, u32[]{:S(2)}, u32[]{:S(2)}) collective-permute-start(f32[128,256]{1,0:T(8,128)S(1)} %collective-permute-done.8.refs_1_), channel_id=1, source_target_pairs={{0,1},{1,0},{2,3},{3,2},{4,5},{5,4},{6,7},{7,6},{8,9},{9,8},{10,11... | collective-permute-start | bytes 393224 | tf_op jit(solution)/shard_map/ppermute | solution.py:324
  54.4 2.7 %collective-permute-start.13 = (f32[128,256]{1,0:T(8,128)S(1)}, f32[128,256]{1,0:T(8,128)S(1)}, u32[]{:S(2)}, u32[]{:S(2)}) collective-permute-start(f32[128,256]{1,0:T(8,128)S(1)} %collective-permute-done.9.refs_2_), channel_id=1, source_target_pairs={{0,1},{1,0},{2,3},{3,2},{4,5},{5,4},{6,7},{7,6},{8,9},{9,8},{10,11... | collective-permute-start | bytes 393224 | tf_op jit(solution)/shard_map/ppermute | solution.py:324
  57.1 1.3 %collective-permute-start.14 = (f32[128,256]{1,0:T(8,128)S(1)}, f32[128,256]{1,0:T(8,128)S(1)}, u32[]{:S(2)}, u32[]{:S(2)}) collective-permute-start(f32[128,256]{1,0:T(8,128)S(1)} %collective-permute-done.10.refs_3_), channel_id=1, source_target_pairs={{0,1},{1,0},{2,3},{3,2},{4,5},{5,4},{6,7},{7,6},{8,9},{9,8},{10,11... | collective-permute-start | bytes 393224 | tf_op jit(solution)/shard_map/ppermute | solution.py:324

commit v6 on v5

--- a/solution.py
+++ b/solution.py
@@ -8,11 +8,29 @@
 from jax.sharding import PartitionSpec as P
 
 QUAD = 4
+SPAN = 120.0
+SMALLEST = 2.0**-100
+SCALE_ROWS = 16
 VMEM_LIMIT = 46 * 1024 * 1024
 
 
 def whole():
     return pl.BlockSpec(memory_space=pltpu.VMEM)
+
+
+def coded(values):
+    largest = jnp.max(jnp.abs(values), axis=(0, 1), keepdims=True)
+    scale = (jnp.maximum(largest, SMALLEST) * 1.01).astype(jnp.bfloat16)
+    share = jnp.sqrt(jnp.abs(values) * (1.0 / scale.astype(jnp.float32)))
+    size = jnp.exp2((share * 2.0 - 1.0) * SPAN)
+    return jnp.where(values < 0.0, -size, size).astype(jnp.bfloat16), scale
+
+
+def decoded(codes, scale):
+    codes, scale = codes.astype(jnp.float32), scale.astype(jnp.float32)
+    share = jnp.log2(jnp.abs(codes)) * (0.5 / SPAN) + 0.5
+    value = share * share * scale
+    return jnp.where(codes < 0.0, -value, value)
 
 
 def any_place():
@@ -163,12 +181,16 @@
 
         lax.fori_loop(0, 2 * halves // bundle, body, 0)
         quad_count = window // QUAD
+        codes, scale = coded(total[...])
+        total[...] = codes.astype(jnp.float32)
         for at in range(block_rows // 128):
             rows = slice(at * 128, (at + 1) * 128)
             lanes[at] = total[:, rows]
             ordered[rows, :] = jnp.concatenate(
                 [lanes[at, pl.ds(part, quad_count, QUAD), :] for part in range(QUAD)], axis=0
-            ).T
+            ).T.astype(jnp.bfloat16)
+        for at in range(count // 2):
+            outs[at][2 * local_rows :, :] = jnp.broadcast_to(scale, (SCALE_ROWS, window))
         for at in range(count):
             start = pl.multiple_of((place_ref[0] ^ at) * local_rows, local_rows)
             rows = slice(at % 2 * local_rows, (at % 2 + 1) * local_rows)
@@ -184,7 +206,8 @@
     flops = 2 * window * pairs * block_rows * (beta_count + pairs * QUAD + block_rows)
     return pl.pallas_call(
         functools.partial(mixed_kernel, count, columns // QUAD, bundle),
-        out_shape=[jax.ShapeDtypeStruct((2 * local_rows, window), jnp.float32)] * (count // 2),
+        out_shape=[jax.ShapeDtypeStruct((2 * local_rows + SCALE_ROWS, window), jnp.bfloat16)]
+        * (count // 2),
         grid_spec=pltpu.PrefetchScalarGridSpec(
             num_scalar_prefetch=1,
             grid=(window // columns,),
@@ -197,7 +220,7 @@
                 pltpu.VMEM((pairs // 2, 2, window, block_rows), jnp.bfloat16),
                 pltpu.VMEM((window, block_rows), jnp.float32),
                 pltpu.VMEM((block_rows // 128, window, 128), jnp.float32),
-                pltpu.VMEM((block_rows, window), jnp.float32),
+                pltpu.VMEM((block_rows, window), jnp.bfloat16),
                 pltpu.VMEM((pairs, block_rows), jnp.int32),
                 pltpu.VMEM((pairs, block_rows), jnp.float32),
                 pltpu.SemaphoreType.DMA((count,)),
@@ -267,35 +290,42 @@
 
 def add_kernel(count, classes, place_ref, base_ref, *refs):
     own, passed = refs[:count], refs[count : 2 * count]
-    out_ref, held, arrived = refs[2 * count :]
+    out_ref, held, scales, arrived = refs[2 * count :]
     local_rows, window = held.shape[1:]
     copies = []
     for at in range(count):
         for side, source in enumerate((own[at], passed[at])):
             slot = 2 * at + side
             rows = source.at[pl.ds(side * local_rows, local_rows)]
-            copies.append(pltpu.make_async_copy(rows, held.at[slot], arrived.at[slot]))
+            scale = source.at[pl.ds(2 * local_rows, SCALE_ROWS)]
+            copies.append(pltpu.make_async_copy(rows, held.at[slot], arrived.at[slot, 0]))
+            copies.append(pltpu.make_async_copy(scale, scales.at[slot], arrived.at[slot, 1]))
     for copy in copies:
         copy.start()
     chunk = place_ref[0] // classes
     for at in range(count):
-        copies[2 * at].wait()
-        copies[2 * at + 1].wait()
+        for copy in copies[4 * at : 4 * at + 4]:
+            copy.wait()
         columns = pl.ds(pl.multiple_of((chunk ^ at) * window, window), window)
-        out_ref[:, columns] = base_ref[:, columns] + (held[2 * at] + held[2 * at + 1])
+        out_ref[:, columns] = base_ref[:, columns] + (
+            decoded(held[2 * at], scales[2 * at, :1, :1])
+            + decoded(held[2 * at + 1], scales[2 * at + 1, :1, :1])
+        )
 
 
 def add_terms(place, base, own, passed, classes):
     count = len(own)
     rows, window = own[0].shape
+    local_rows = (rows - SCALE_ROWS) // 2
     return pl.pallas_call(
         functools.partial(add_kernel, count, classes),
         out_shape=jax.ShapeDtypeStruct(base.shape, jnp.float32),
         in_specs=[pl.BlockSpec(memory_space=pltpu.SMEM), whole()] + [any_place()] * (2 * count),
         out_specs=whole(),
         scratch_shapes=[
-            pltpu.VMEM((2 * count, rows // 2, window), jnp.float32),
-            pltpu.SemaphoreType.DMA((2 * count,)),
+            pltpu.VMEM((2 * count, local_rows, window), jnp.bfloat16),
+            pltpu.VMEM((2 * count, SCALE_ROWS, window), jnp.bfloat16),
+            pltpu.SemaphoreType.DMA((2 * count, 2)),
         ],
         compiler_params=pltpu.CompilerParams(vmem_limit_bytes=VMEM_LIMIT),
         name="add",

time: 60.1 us -> 56.5 us (0.940)
  waiting for transfers between devices: 11.6 us -> 5.58 us
  starting transfers between devices: 12.1 us -> 14 us
    ppermute x4, waiting for transfers between devices: 6.43 us -> 0.88 us  [far(): return lax.ppermute(array, ('blk', 'str'), route)]
    ppermute x11, starting transfers between devices: 6.17 us -> 8.11 us  [near(): return lax.ppermute(array, ('blk', 'str'), route)]
  transfers between devices with their start and end apart: 15 -> 15, of which waited for: 8 -> 6; matrix products, arithmetic and copies ran while one was open for 5% -> 5% of each run, Pallas kernels for 5% -> 5%
where the time goes in v6:
time: 56.5 us; the launch traced here: 56.3 us
  Pallas kernels  32.8 us (58%)
  starting transfers between devices  14 us (25%)
  waiting for transfers between devices  5.58 us (10%)
  local copies, waits for them, and re-layouts  3.71 us (7%)
    pallas_call x1, Pallas kernels, mixed_pieces(): pl.pallas_call(functools.partial(mixed_kernel, count, columns // QUAD, bu...  28.5 us
    ppermute x11, starting transfers between devices, near(): return lax.ppermute(array, ('blk', 'str'), route)  8.11 us
    ppermute x4, starting transfers between devices, far(): return lax.ppermute(array, ('blk', 'str'), route)  5.91 us
    ppermute x11, waiting for transfers between devices, near(): return lax.ppermute(array, ('blk', 'str'), route)  4.7 us
    dynamic_slice x3, local copies, waits for them, and re-layouts, one_class(): lax.dynamic_slice(array, (symmetry, 0, start), (1, array.shape[1], width))  2.8 us
    pallas_call x1, Pallas kernels, plain_terms(): pl.pallas_call(functools.partial(plain_kernel, count), out_shape=jax.Shap...  2.4 us
    pallas_call x1, Pallas kernels, add_terms(): pl.pallas_call(functools.partial(add_kernel, count, classes), out_shape=j...  1.51 us
  transfers between devices with their start and end apart: 15, of which 6 were waited for; matrix products, arithmetic and copies ran while one was open for 5% of the time, Pallas kernels for 5%

profile of v6, /device:TPU:0, one launch (start us, length us, event | category | flops | bytes accessed | tf_op | source)
XLA Modules:
  0.0 56.3 jit_solution(15370763225993258839)
XLA Ops:
  0.0 0.0 copy-start
  0.0 0.5 collective-permute-start
  0.5 3.5 %collective-permute-start.5 = (bf16[64,1024]{1,0:T(8,128)(2,1)}, bf16[64,1024]{1,0:T(8,128)(2,1)S(1)}, u32[]{:S(2)}, u32[]{:S(2)}) collective-permute-start(bf16[64,1024]{1,0:T(8,128)(2,1)} %rows_ref.1), channel_id=1, source_target_pairs={{0,6},{1,7},{2,4},{3,5},{4,2},{5,3},{6,0},{7,1},{8,14},{9,15},{10,... | collective-permute-start | bytes 393224 | tf_op jit(solution)/shard_map/ppermute | solution.py:354
  4.0 0.5 collective-permute-start.3
  4.5 0.2 collective-permute-start.1
  4.6 0.0 copy-done
  4.7 1.2 %constant_dynamic-slice_fusion.3 = (s32[1,50,256]{2,0,1:T(1,128)S(1)}, s32[1,50,256]{2,0,1:T(1,128)S(1)}) fusion(s32[2,50,1024]{2,0,1:T(2,128)} %param.10, s32[]{:T(128)S(6)} %select_n.27, s32[]{:T(128)S(6)} %select_n.29, s32[2,50,1024]{2,0,1:T(2,128)} %param.9), kind=kLoop, calls=%fused_computation.12 | loop fusion | bytes 204808 | tf_op jit(solution)/shard_map/dynamic_slice | solution.py:365
  6.0 0.0 copy-start.2
  6.0 0.9 %copy-done.2 = bf16[64,1024]{1,0:T(8,128)(2,1)S(1)} copy-done((bf16[64,1024]{1,0:T(8,128)(2,1)S(1)}, bf16[64,1024]{1,0:T(8,128)(2,1)}, u32[]{:S(2)}) %copy-start.2) | copy-done | bytes 131096
  6.9 0.4 prepare.1
  7.3 1.5 %constant_dynamic-slice_fusion = (s32[1,50,512]{2,0,1:T(1,128)S(1)}, s32[1,50,512]{2,0,1:T(1,128)S(1)}) fusion(s32[2,50,2048]{2,0,1:T(2,128)} %param.12, s32[]{:T(128)S(6)} %select_n.27, s32[]{:T(128)S(6)} %select_n.30, s32[2,50,2048]{2,0,1:T(2,128)} %param.11), kind=kLoop, calls=%fused_computation.9 | loop fusion | bytes 409608 | tf_op jit(solution)/shard_map/dynamic_slice | solution.py:365
  8.9 2.5 %collective-permute-done.1.refs_2_ = bf16[64,1024]{1,0:T(8,128)(2,1)S(1)} collective-permute-done((bf16[64,1024]{1,0:T(8,128)(2,1)}, bf16[64,1024]{1,0:T(8,128)(2,1)S(1)}, u32[]{:S(2)}, u32[]{:S(2)}) %collective-permute-start.1) | collective-permute-done | bytes 131104 | tf_op jit(solution)/shard_map/ppermute | solution.py:354
  11.4 0.0 collective-permute-done.5.refs_6_
  11.4 0.0 collective-permute-start.6
  11.4 0.0 collective-permute-done.3.refs_4_
  11.4 0.5 collective-permute-start.4
  11.9 0.1 collective-permute-start.2
  12.0 0.0 collective-permute-done.refs_1_
  12.0 0.8 %collective-permute-done.6.refs_7_ = bf16[64,1024]{1,0:T(8,128)(2,1)S(1)} collective-permute-done((bf16[64,1024]{1,0:T(8,128)(2,1)S(1)}, bf16[64,1024]{1,0:T(8,128)(2,1)S(1)}, u32[]{:S(2)}, u32[]{:S(2)}) %collective-permute-start.6) | collective-permute-done | bytes 131104 | tf_op jit(solution)/shard_map/ppermute | solution.py:354
  12.7 0.2 collective-permute-done.4.refs_5_
  12.9 0.3 collective-permute-done.2.refs_3_
  13.3 0.0 copy-start.1
  13.3 0.0 copy-start.3
  13.3 28.5 %mixed.1 = (bf16[144,256]{1,0:T(8,128)(2,1)S(1)}, bf16[144,256]{1,0:T(8,128)(2,1)S(1)}, bf16[144,256]{1,0:T(8,128)(2,1)S(1)}, bf16[144,256]{1,0:T(8,128)(2,1)S(1)}) custom-call(s32[1]{0:T(128)} %bitcast.place_ref, bf16[64,1024]{1,0:T(8,128)(2,1)S(1)} %get-tuple-element.20.refs_0_, bf16[64,1024]{1,0:T(8,128)(2,1)S(1)} %collective-permute-done.refs_1_, ...), custom_call_target="tpu_custom_call" | custom-call | flops 22754099200 | bytes 1048576 | tf_op jit(solution)/shard_map/mixed/pallas_call | solution.py:207
  41.7 1.6 %collective-permute-start.7 = (bf16[144,256]{1,0:T(8,128)(2,1)S(1)}, bf16[144,256]{1,0:T(8,128)(2,1)S(1)}, u32[]{:S(2)}, u32[]{:S(2)}) collective-permute-start(bf16[144,256]{1,0:T(8,128)(2,1)S(1)} %get-tuple-element.27), channel_id=1, source_target_pairs={{0,8},{1,17},{2,10},{3,19},{4,12},{5,21},{6,14},{7,23},{8,0},{9,25... | collective-permute-start | bytes 221192 | tf_op jit(solution)/shard_map/ppermute | solution.py:362
  43.4 1.4 %collective-permute-start.8 = (bf16[144,256]{1,0:T(8,128)(2,1)S(1)}, bf16[144,256]{1,0:T(8,128)(2,1)S(1)}, u32[]{:S(2)}, u32[]{:S(2)}) collective-permute-start(bf16[144,256]{1,0:T(8,128)(2,1)S(1)} %get-tuple-element.30), channel_id=1, source_target_pairs={{0,10},{1,19},{2,8},{3,17},{4,14},{5,23},{6,12},{7,21},{8,2},{9,27... | collective-permute-start | bytes 221192 | tf_op jit(solution)/shard_map/ppermute | solution.py:362
  44.8 1.5 %collective-permute-start.9 = (bf16[144,256]{1,0:T(8,128)(2,1)S(1)}, bf16[144,256]{1,0:T(8,128)(2,1)S(1)}, u32[]{:S(2)}, u32[]{:S(2)}) collective-permute-start(bf16[144,256]{1,0:T(8,128)(2,1)S(1)} %get-tuple-element.31), channel_id=1, source_target_pairs={{0,12},{1,21},{2,14},{3,23},{4,8},{5,17},{6,10},{7,19},{8,4},{9,29... | collective-permute-start | bytes 221192 | tf_op jit(solution)/shard_map/ppermute | solution.py:362
  46.3 1.4 %collective-permute-start.10 = (bf16[144,256]{1,0:T(8,128)(2,1)S(1)}, bf16[144,256]{1,0:T(8,128)(2,1)S(1)}, u32[]{:S(2)}, u32[]{:S(2)}) collective-permute-start(bf16[144,256]{1,0:T(8,128)(2,1)S(1)} %get-tuple-element.32), channel_id=1, source_target_pairs={{0,14},{1,23},{2,12},{3,21},{4,10},{5,19},{6,8},{7,17},{8,6},{9,31... | collective-permute-start | bytes 221192 | tf_op jit(solution)/shard_map/ppermute | solution.py:362
  47.7 0.0 copy-done.1
  47.7 0.0 copy-done.3
  47.7 2.4 %plain.1.base_ref = f32[64,1024]{1,0:T(8,128)S(1)} custom-call(s32[1]{0:T(128)} %bitcast.place_ref, bf16[64,1024]{1,0:T(8,128)(2,1)S(1)} %get-tuple-element.20.refs_0_, bf16[64,1024]{1,0:T(8,128)(2,1)S(1)} %collective-permute-done.refs_1_, bf16[64,1024]{1,0:T(8,128)(2,1)S(1)} %collective-permute-done.1.refs_2_, ...), custom_call_target="tpu_custom_call" | custom-call | flops 201326592 | bytes 3145728 | tf_op jit(solution)/shard_map/plain/pallas_call | solution.py:268
  50.1 0.0 collective-permute-done.7.refs_0_
  50.1 1.0 %collective-permute-start.11 = (bf16[144,256]{1,0:T(8,128)(2,1)S(1)}, bf16[144,256]{1,0:T(8,128)(2,1)S(1)}, u32[]{:S(2)}, u32[]{:S(2)}) collective-permute-start(bf16[144,256]{1,0:T(8,128)(2,1)S(1)} %collective-permute-done.7.refs_0_), channel_id=1, source_target_pairs={{0,1},{1,0},{2,3},{3,2},{4,5},{5,4},{6,7},{7,6},{8,9},{9,8},{10,11... | collective-permute-start | bytes 221192 | tf_op jit(solution)/shard_map/ppermute | solution.py:354
  51.0 0.0 collective-permute-done.8.refs_1_
  51.0 0.1 collective-permute-start.12
  51.1 0.0 collective-permute-done.9.refs_2_
  51.1 0.4 collective-permute-start.13
  51.6 0.9 %collective-permute-done.10.refs_3_ = bf16[144,256]{1,0:T(8,128)(2,1)S(1)} collective-permute-done((bf16[144,256]{1,0:T(8,128)(2,1)S(1)}, bf16[144,256]{1,0:T(8,128)(2,1)S(1)}, u32[]{:S(2)}, u32[]{:S(2)}) %collective-permute-start.10) | collective-permute-done | bytes 73760 | tf_op jit(solution)/shard_map/ppermute | solution.py:362
  52.4 1.4 %collective-permute-start.14 = (bf16[144,256]{1,0:T(8,128)(2,1)S(1)}, bf16[144,256]{1,0:T(8,128)(2,1)S(1)}, u32[]{:S(2)}, u32[]{:S(2)}) collective-permute-start(bf16[144,256]{1,0:T(8,128)(2,1)S(1)} %collective-permute-done.10.refs_3_), channel_id=1, source_target_pairs={{0,1},{1,0},{2,3},{3,2},{4,5},{5,4},{6,7},{7,6},{8,9},{9,8},{10,11... | collective-permute-start | bytes 221192 | tf_op jit(solution)/shard_map/ppermute | solution.py:354
  53.9 0.0 collective-permute-done.11.refs_4_
  53.9 0.0 collective-permute-done.12.refs_5_
  53.9 0.0 collective-permute-done.13.refs_6_
  53.9 0.9 %collective-permute-done.14.refs_7_ = bf16[144,256]{1,0:T(8,128)(2,1)S(1)} collective-permute-done((bf16[144,256]{1,0:T(8,128)(2,1)S(1)}, bf16[144,256]{1,0:T(8,128)(2,1)S(1)}, u32[]{:S(2)}, u32[]{:S(2)}) %collective-permute-start.14) | collective-permute-done | bytes 73760 | tf_op jit(solution)/shard_map/ppermute | solution.py:354
  54.8 1.5 %add.76 = f32[64,1024]{1,0:T(8,128)} custom-call(s32[1]{0:T(128)} %bitcast.place_ref, f32[64,1024]{1,0:T(8,128)S(1)} %plain.1.base_ref, bf16[144,256]{1,0:T(8,128)(2,1)S(1)} %collective-permute-done.7.refs_0_, bf16[144,256]{1,0:T(8,128)(2,1)S(1)} %collective-permute-done.8.refs_1_, bf16[144,256]{1,0:T(8,128)(2,1)S(1)} %collective-permute-done.9.refs_2_, ...), custom_call_target="tpu_custom_call" | custom-call | tf_op jit(solution)/shard_map/add/pallas_call | solution.py:320
  (4 shorter events, 0.1 us)
Async XLA Ops:
  0.0 4.6 %copy-start = (bf16[2,50,50]{2,0,1:T(2,128)(2,1)S(1)}, bf16[2,50,50]{2,0,1:T(2,128)(2,1)}, u32[]{:S(2)}) copy-start(bf16[2,50,50]{2,0,1:T(2,128)(2,1)} %param.13) | copy-start | bytes 30004
  0.0 12.0 %collective-permute-start = (bf16[64,1024]{1,0:T(8,128)(2,1)}, bf16[64,1024]{1,0:T(8,128)(2,1)S(1)}, u32[]{:S(2)}, u32[]{:S(2)}) collective-permute-start(bf16[64,1024]{1,0:T(8,128)(2,1)} %rows_ref.1), channel_id=1, source_target_pairs={{0,1},{1,0},{2,3},{3,2},{4,5},{5,4},{6,7},{7,6},{8,9},{9,8},{10,11... | collective-permute-start | bytes 393224 | tf_op jit(solution)/shard_map/ppermute | solution.py:354
  0.5 10.9 %collective-permute-start.5 = (bf16[64,1024]{1,0:T(8,128)(2,1)}, bf16[64,1024]{1,0:T(8,128)(2,1)S(1)}, u32[]{:S(2)}, u32[]{:S(2)}) collective-permute-start(bf16[64,1024]{1,0:T(8,128)(2,1)} %rows_ref.1), channel_id=1, source_target_pairs={{0,6},{1,7},{2,4},{3,5},{4,2},{5,3},{6,0},{7,1},{8,14},{9,15},{10,... | collective-permute-start | bytes 393224 | tf_op jit(solution)/shard_map/ppermute | solution.py:354
  4.0 7.4 %collective-permute-start.3 = (bf16[64,1024]{1,0:T(8,128)(2,1)}, bf16[64,1024]{1,0:T(8,128)(2,1)S(1)}, u32[]{:S(2)}, u32[]{:S(2)}) collective-permute-start(bf16[64,1024]{1,0:T(8,128)(2,1)} %rows_ref.1), channel_id=1, source_target_pairs={{0,4},{1,5},{2,6},{3,7},{4,0},{5,1},{6,2},{7,3},{8,12},{9,13},{10,... | collective-permute-start | bytes 393224 | tf_op jit(solution)/shard_map/ppermute | solution.py:354
  4.5 6.9 %collective-permute-start.1 = (bf16[64,1024]{1,0:T(8,128)(2,1)}, bf16[64,1024]{1,0:T(8,128)(2,1)S(1)}, u32[]{:S(2)}, u32[]{:S(2)}) collective-permute-start(bf16[64,1024]{1,0:T(8,128)(2,1)} %rows_ref.1), channel_id=1, source_target_pairs={{0,2},{1,3},{2,0},{3,1},{4,6},{5,7},{6,4},{7,5},{8,10},{9,11},{10,... | collective-permute-start | bytes 393224 | tf_op jit(solution)/shard_map/ppermute | solution.py:354
  6.0 0.9 %copy-start.2 = (bf16[64,1024]{1,0:T(8,128)(2,1)S(1)}, bf16[64,1024]{1,0:T(8,128)(2,1)}, u32[]{:S(2)}) copy-start(bf16[64,1024]{1,0:T(8,128)(2,1)} %rows_ref.1) | copy-start | bytes 393220
  11.4 1.3 %collective-permute-start.6 = (bf16[64,1024]{1,0:T(8,128)(2,1)S(1)}, bf16[64,1024]{1,0:T(8,128)(2,1)S(1)}, u32[]{:S(2)}, u32[]{:S(2)}) collective-permute-start(bf16[64,1024]{1,0:T(8,128)(2,1)S(1)} %collective-permute-done.5.refs_6_), channel_id=1, source_target_pairs={{0,1},{1,0},{2,3},{3,2},{4,5},{5,4},{6,7},{7,6},{8,9},{9,8},{10,11... | collective-permute-start | bytes 393224 | tf_op jit(solution)/shard_map/ppermute | solution.py:354
  11.4 1.5 %collective-permute-start.4 = (bf16[64,1024]{1,0:T(8,128)(2,1)S(1)}, bf16[64,1024]{1,0:T(8,128)(2,1)S(1)}, u32[]{:S(2)}, u32[]{:S(2)}) collective-permute-start(bf16[64,1024]{1,0:T(8,128)(2,1)S(1)} %collective-permute-done.3.refs_4_), channel_id=1, source_target_pairs={{0,1},{1,0},{2,3},{3,2},{4,5},{5,4},{6,7},{7,6},{8,9},{9,8},{10,11... | collective-permute-start | bytes 393224 | tf_op jit(solution)/shard_map/ppermute | solution.py:354
  11.9 1.3 %collective-permute-start.2 = (bf16[64,1024]{1,0:T(8,128)(2,1)S(1)}, bf16[64,1024]{1,0:T(8,128)(2,1)S(1)}, u32[]{:S(2)}, u32[]{:S(2)}) collective-permute-start(bf16[64,1024]{1,0:T(8,128)(2,1)S(1)} %collective-permute-done.1.refs_2_), channel_id=1, source_target_pairs={{0,1},{1,0},{2,3},{3,2},{4,5},{5,4},{6,7},{7,6},{8,9},{9,8},{10,11... | collective-permute-start | bytes 393224 | tf_op jit(solution)/shard_map/ppermute | solution.py:354
  13.3 34.4 %copy-start.1 = (bf16[1024,1024]{1,0:T(8,128)(2,1)S(1)}, bf16[1024,1024]{1,0:T(8,128)(2,1)}, u32[]{:S(2)}) copy-start(bf16[1024,1024]{1,0:T(8,128)(2,1)} %refs_9_.1) | copy-start | bytes 6291460
  13.3 34.4 %copy-start.3 = (bf16[64,512]{1,0:T(8,128)(2,1)S(1)}, bf16[64,512]{1,0:T(8,128)(2,1)}, u32[]{:S(2)}) copy-start(bf16[64,512]{1,0:T(8,128)(2,1)} %refs_8_.1) | copy-start | bytes 196612
  41.7 8.3 %collective-permute-start.7 = (bf16[144,256]{1,0:T(8,128)(2,1)S(1)}, bf16[144,256]{1,0:T(8,128)(2,1)S(1)}, u32[]{:S(2)}, u32[]{:S(2)}) collective-permute-start(bf16[144,256]{1,0:T(8,128)(2,1)S(1)} %get-tuple-element.27), channel_id=1, source_target_pairs={{0,8},{1,17},{2,10},{3,19},{4,12},{5,21},{6,14},{7,23},{8,0},{9,25... | collective-permute-start | bytes 221192 | tf_op jit(solution)/shard_map/ppermute | solution.py:362
  43.4 7.7 %collective-permute-start.8 = (bf16[144,256]{1,0:T(8,128)(2,1)S(1)}, bf16[144,256]{1,0:T(8,128)(2,1)S(1)}, u32[]{:S(2)}, u32[]{:S(2)}) collective-permute-start(bf16[144,256]{1,0:T(8,128)(2,1)S(1)} %get-tuple-element.30), channel_id=1, source_target_pairs={{0,10},{1,19},{2,8},{3,17},{4,14},{5,23},{6,12},{7,21},{8,2},{9,27... | collective-permute-start | bytes 221192 | tf_op jit(solution)/shard_map/ppermute | solution.py:362
  44.8 6.4 %collective-permute-start.9 = (bf16[144,256]{1,0:T(8,128)(2,1)S(1)}, bf16[144,256]{1,0:T(8,128)(2,1)S(1)}, u32[]{:S(2)}, u32[]{:S(2)}) collective-permute-start(bf16[144,256]{1,0:T(8,128)(2,1)S(1)} %get-tuple-element.31), channel_id=1, source_target_pairs={{0,12},{1,21},{2,14},{3,23},{4,8},{5,17},{6,10},{7,19},{8,4},{9,29... | collective-permute-start | bytes 221192 | tf_op jit(solution)/shard_map/ppermute | solution.py:362
  46.3 6.2 %collective-permute-start.10 = (bf16[144,256]{1,0:T(8,128)(2,1)S(1)}, bf16[144,256]{1,0:T(8,128)(2,1)S(1)}, u32[]{:S(2)}, u32[]{:S(2)}) collective-permute-start(bf16[144,256]{1,0:T(8,128)(2,1)S(1)} %get-tuple-element.32), channel_id=1, source_target_pairs={{0,14},{1,23},{2,12},{3,21},{4,10},{5,19},{6,8},{7,17},{8,6},{9,31... | collective-permute-start | bytes 221192 | tf_op jit(solution)/shard_map/ppermute | solution.py:362
  50.1 3.8 %collective-permute-start.11 = (bf16[144,256]{1,0:T(8,128)(2,1)S(1)}, bf16[144,256]{1,0:T(8,128)(2,1)S(1)}, u32[]{:S(2)}, u32[]{:S(2)}) collective-permute-start(bf16[144,256]{1,0:T(8,128)(2,1)S(1)} %collective-permute-done.7.refs_0_), channel_id=1, source_target_pairs={{0,1},{1,0},{2,3},{3,2},{4,5},{5,4},{6,7},{7,6},{8,9},{9,8},{10,11... | collective-permute-start | bytes 221192 | tf_op jit(solution)/shard_map/ppermute | solution.py:354
  51.0 2.8 %collective-permute-start.12 = (bf16[144,256]{1,0:T(8,128)(2,1)S(1)}, bf16[144,256]{1,0:T(8,128)(2,1)S(1)}, u32[]{:S(2)}, u32[]{:S(2)}) collective-permute-start(bf16[144,256]{1,0:T(8,128)(2,1)S(1)} %collective-permute-done.8.refs_1_), channel_id=1, source_target_pairs={{0,1},{1,0},{2,3},{3,2},{4,5},{5,4},{6,7},{7,6},{8,9},{9,8},{10,11... | collective-permute-start | bytes 221192 | tf_op jit(solution)/shard_map/ppermute | solution.py:354
  51.1 2.8 %collective-permute-start.13 = (bf16[144,256]{1,0:T(8,128)(2,1)S(1)}, bf16[144,256]{1,0:T(8,128)(2,1)S(1)}, u32[]{:S(2)}, u32[]{:S(2)}) collective-permute-start(bf16[144,256]{1,0:T(8,128)(2,1)S(1)} %collective-permute-done.9.refs_2_), channel_id=1, source_target_pairs={{0,1},{1,0},{2,3},{3,2},{4,5},{5,4},{6,7},{7,6},{8,9},{9,8},{10,11... | collective-permute-start | bytes 221192 | tf_op jit(solution)/shard_map/ppermute | solution.py:354
  52.4 2.4 %collective-permute-start.14 = (bf16[144,256]{1,0:T(8,128)(2,1)S(1)}, bf16[144,256]{1,0:T(8,128)(2,1)S(1)}, u32[]{:S(2)}, u32[]{:S(2)}) collective-permute-start(bf16[144,256]{1,0:T(8,128)(2,1)S(1)} %collective-permute-done.10.refs_3_), channel_id=1, source_target_pairs={{0,1},{1,0},{2,3},{3,2},{4,5},{5,4},{6,7},{7,6},{8,9},{9,8},{10,11... | collective-permute-start | bytes 221192 | tf_op jit(solution)/shard_map/ppermute | solution.py:354

commit v7 on v6

--- a/solution.py
+++ b/solution.py
@@ -88,13 +88,16 @@
     )(codes, integrals, rows)
 
 
-def pair_images(step, quads, code_ref, kron_ref, turned):
+def pair_images(first_quad, quads, code_ref, kron_ref, turned):
     beta_count, rows = turned.shape
     size = kron_ref.shape[0]
     halves = size // (2 * QUAD)
-    own = pltpu.roll(code_ref[...], 128 - step * quads, 1)
     codes = jnp.concatenate(
-        [jnp.broadcast_to(own[:, quad : quad + 1], (size, 128)) for quad in range(quads)], axis=0
+        [
+            jnp.broadcast_to(code_ref[:, quad : quad + 1], (size, 128))
+            for quad in range(first_quad, first_quad + quads)
+        ],
+        axis=0,
     )
     target = jnp.right_shift(codes, 2).astype(jnp.int16)
     value = ((codes & 3) - 1).astype(jnp.float32).astype(jnp.bfloat16)
@@ -130,105 +133,97 @@
     outs = refs[count + 3 : count + 3 + count // 2]
     rest = refs[count + 3 + count // 2 :]
     held, turned, images, total, lanes, ordered, indices, signs, arrived = rest
-    step = pl.program_id(0)
     local_rows = pieces[0].shape[0]
     halves, _, window, block_rows = images.shape
     columns = quads * QUAD
 
-    @pl.when(step == 0)
-    def _():
-        copies = [
-            pltpu.make_async_copy(
-                pieces[at], held.at[pl.ds(at * local_rows, local_rows)], arrived.at[at]
+    copies = [
+        pltpu.make_async_copy(
+            pieces[at], held.at[pl.ds(at * local_rows, local_rows)], arrived.at[at]
+        )
+        for at in range(count)
+    ]
+    for copy in copies:
+        copy.start()
+    for start in range(0, block_rows, 128):
+        for copy in copies[start // local_rows : (start + 128) // local_rows]:
+            copy.wait()
+        turned[:, start : start + 128] = held[start : start + 128, :].T
+
+    for start in range(0, window, columns):
+        even, odd = pair_images(start // QUAD, quads, code_ref, kron_ref, turned)
+        images[:, 0, start : start + columns, :] = even
+        images[:, 1, start : start + columns, :] = odd
+
+    indices[...] = jnp.right_shift(alpha_ref[...], 2)
+    signs[...] = ((alpha_ref[...] & 3) - 1).astype(jnp.float32)
+    position = lax.broadcasted_iota(jnp.int32, (block_rows, block_rows), 0)
+    position = jnp.bitwise_xor(position, place_ref[0] * local_rows).astype(jnp.int16)
+    total[...] = jnp.zeros_like(total)
+
+    def body(at, carry):
+        term = None
+        for offset in range(bundle):
+            pair = bundle * at + offset
+            selector = jnp.where(
+                position == indices[pl.ds(pair, 1), :].astype(jnp.int16),
+                signs[pl.ds(pair, 1), :].astype(jnp.bfloat16),
+                jnp.zeros((), jnp.bfloat16),
             )
-            for at in range(count)
-        ]
-        for copy in copies:
-            copy.start()
-        for copy in copies:
-            copy.wait()
-        for start in range(0, block_rows, 128):
-            turned[:, start : start + 128] = held[start : start + 128, :].T
-
-    place = pl.ds(pl.multiple_of(step * columns, columns), columns)
-    even, odd = pair_images(step, quads, code_ref, kron_ref, turned)
-    images[:, 0, place, :] = even
-    images[:, 1, place, :] = odd
-
-    @pl.when(step == pl.num_programs(0) - 1)
-    def _():
-        total[...] = jnp.zeros_like(total)
-        indices[...] = jnp.right_shift(alpha_ref[...], 2)
-        signs[...] = ((alpha_ref[...] & 3) - 1).astype(jnp.float32)
-        position = lax.broadcasted_iota(jnp.int32, (block_rows, block_rows), 0)
-        position = jnp.bitwise_xor(position, place_ref[0] * local_rows)
-
-        def body(at, carry):
-            term = None
-            for offset in range(bundle):
-                pair = bundle * at + offset
-                selector = jnp.where(
-                    position == indices[pl.ds(pair, 1), :], signs[pl.ds(pair, 1), :], 0.0
-                ).astype(jnp.bfloat16)
-                part = jnp.dot(
-                    images[lax.div(pair, 2), lax.rem(pair, 2)],
-                    selector,
-                    preferred_element_type=jnp.float32,
-                )
-                term = part if term is None else term + part
-            total[...] += term
-            return carry
-
-        lax.fori_loop(0, 2 * halves // bundle, body, 0)
-        quad_count = window // QUAD
-        codes, scale = coded(total[...])
-        total[...] = codes.astype(jnp.float32)
-        for at in range(block_rows // 128):
-            rows = slice(at * 128, (at + 1) * 128)
-            lanes[at] = total[:, rows]
-            ordered[rows, :] = jnp.concatenate(
-                [lanes[at, pl.ds(part, quad_count, QUAD), :] for part in range(QUAD)], axis=0
-            ).T.astype(jnp.bfloat16)
-        for at in range(count // 2):
-            outs[at][2 * local_rows :, :] = jnp.broadcast_to(scale, (SCALE_ROWS, window))
-        for at in range(count):
-            start = pl.multiple_of((place_ref[0] ^ at) * local_rows, local_rows)
-            rows = slice(at % 2 * local_rows, (at % 2 + 1) * local_rows)
-            outs[at // 2][rows, :] = ordered[pl.ds(start, local_rows), :]
+            part = jnp.dot(
+                images[lax.div(pair, 2), lax.rem(pair, 2)],
+                selector,
+                preferred_element_type=jnp.float32,
+            )
+            term = part if term is None else term + part
+        total[...] += term
+        return carry
+
+    lax.fori_loop(0, 2 * halves // bundle, body, 0)
+    codes, scale = coded(total[...])
+    total[...] = codes.astype(jnp.float32)
+    quad_count = window // QUAD
+    for at in range(block_rows // 128):
+        rows = slice(at * 128, (at + 1) * 128)
+        lanes[at] = total[:, rows]
+        ordered[rows, :] = jnp.concatenate(
+            [lanes[at, pl.ds(part, quad_count, QUAD), :] for part in range(QUAD)], axis=0
+        ).T.astype(jnp.bfloat16)
+    for at in range(count // 2):
+        outs[at][2 * local_rows :, :] = jnp.broadcast_to(scale, (SCALE_ROWS, window))
+    for at in range(count):
+        start = pl.multiple_of((place_ref[0] ^ at) * local_rows, local_rows)
+        rows = slice(at % 2 * local_rows, (at % 2 + 1) * local_rows)
+        outs[at // 2][rows, :] = ordered[pl.ds(start, local_rows), :]
 
 
 def mixed_pieces(place, pieces, codes, kron, alpha_codes, window):
     count = len(pieces)
     local_rows, beta_count = pieces[0].shape
     pairs, block_rows = alpha_codes.shape
-    columns = min(128, window, 128 * 512 // block_rows)
     bundle = next(size for size in (25, 10, 5, 2, 1) if pairs % size == 0)
+    quads = min(8, window // QUAD, 8 * 512 // block_rows)
     flops = 2 * window * pairs * block_rows * (beta_count + pairs * QUAD + block_rows)
     return pl.pallas_call(
-        functools.partial(mixed_kernel, count, columns // QUAD, bundle),
+        functools.partial(mixed_kernel, count, quads, bundle),
         out_shape=[jax.ShapeDtypeStruct((2 * local_rows + SCALE_ROWS, window), jnp.bfloat16)]
         * (count // 2),
-        grid_spec=pltpu.PrefetchScalarGridSpec(
-            num_scalar_prefetch=1,
-            grid=(window // columns,),
-            in_specs=[any_place()] * count
-            + [whole()] * 3,
-            out_specs=[whole()] * (count // 2),
-            scratch_shapes=[
-                pltpu.VMEM((block_rows, beta_count), jnp.bfloat16),
-                pltpu.VMEM((beta_count, block_rows), jnp.bfloat16),
-                pltpu.VMEM((pairs // 2, 2, window, block_rows), jnp.bfloat16),
-                pltpu.VMEM((window, block_rows), jnp.float32),
-                pltpu.VMEM((block_rows // 128, window, 128), jnp.float32),
-                pltpu.VMEM((block_rows, window), jnp.bfloat16),
-                pltpu.VMEM((pairs, block_rows), jnp.int32),
-                pltpu.VMEM((pairs, block_rows), jnp.float32),
-                pltpu.SemaphoreType.DMA((count,)),
-            ],
-        ),
-        compiler_params=pltpu.CompilerParams(
-            dimension_semantics=("arbitrary",), vmem_limit_bytes=VMEM_LIMIT
-        ),
+        in_specs=[pl.BlockSpec(memory_space=pltpu.SMEM)]
+        + [any_place()] * count
+        + [whole()] * 3,
+        out_specs=[whole()] * (count // 2),
+        scratch_shapes=[
+            pltpu.VMEM((block_rows, beta_count), jnp.bfloat16),
+            pltpu.VMEM((beta_count, block_rows), jnp.bfloat16),
+            pltpu.VMEM((pairs // 2, 2, window, block_rows), jnp.bfloat16),
+            pltpu.VMEM((window, block_rows), jnp.float32),
+            pltpu.VMEM((block_rows // 128, window, 128), jnp.float32),
+            pltpu.VMEM((block_rows, window), jnp.bfloat16),
+            pltpu.VMEM((pairs, block_rows), jnp.int32),
+            pltpu.VMEM((pairs, block_rows), jnp.float32),
+            pltpu.SemaphoreType.DMA((count,)),
+        ],
+        compiler_params=pltpu.CompilerParams(vmem_limit_bytes=VMEM_LIMIT),
         cost_estimate=pl.CostEstimate(flops=flops, bytes_accessed=1 << 20, transcendentals=0),
         name="mixed",
     )(place, *pieces, codes, kron, alpha_codes)
@@ -306,7 +301,7 @@
     for at in range(count):
         for copy in copies[4 * at : 4 * at + 4]:
             copy.wait()
-        columns = pl.ds(pl.multiple_of((chunk ^ at) * window, window), window)
+        columns = pl.ds(pl.multiple_of((chunk ^ (count - 1 - at)) * window, window), window)
         out_ref[:, columns] = base_ref[:, columns] + (
             decoded(held[2 * at], scales[2 * at, :1, :1])
             + decoded(held[2 * at + 1], scales[2 * at + 1, :1, :1])
@@ -374,12 +369,12 @@
     codes, kron, rows = prepare(beta_codes, own_integrals, civec)
     later, place = lax.optimization_barrier((civec, place))
     arrived = [near(later if at == 2 else civec, at) for at in range(2, count, 2)]
-    codes, alpha_codes, arrived[0] = lax.optimization_barrier((codes, alpha_codes, arrived[0]))
+    codes, alpha_codes, arrived[-1] = lax.optimization_barrier((codes, alpha_codes, arrived[-1]))
     crossed = [near(piece, 1) for piece in [civec] + arrived]
     pieces = [piece for two in zip([rows] + arrived, crossed) for piece in two]
 
     sent = mixed_pieces(place, pieces, codes, kron, alpha_codes, window)
-    own = [far(sent[at], 2 * at) for at in reversed(range(count // 2))][::-1]
+    own = [far(sent[at], 2 * at) for at in reversed(range(count // 2))]
     base = plain_terms(place, pieces, alpha_operator, beta_operator)
     own[0], base = lax.optimization_barrier((own[0], base))
     passed = [near(rows, 1) for rows in own]

time: 56.5 us -> 56.1 us (level)
  starting transfers between devices: 14 us -> 12.6 us
  waiting for transfers between devices: 5.58 us -> 6.92 us
    ppermute x11, starting transfers between devices: 8.11 us -> 6.65 us  [near(): return lax.ppermute(array, ('blk', 'str'), route)]
    ppermute x4, waiting for transfers between devices: 0.88 us -> 1.83 us  [far(): return lax.ppermute(array, ('blk', 'str'), route)]
  transfers between devices with their start and end apart: 15 -> 15, of which waited for: 6 -> 7; matrix products, arithmetic and copies ran while one was open for 5% -> 5% of each run, Pallas kernels for 5% -> 5%
where the time goes in v7:
time: 56.1 us; the launch traced here: 55.9 us
  Pallas kernels  32.4 us (58%)
  starting transfers between devices  12.6 us (22%)
  waiting for transfers between devices  6.92 us (12%)
  local copies, waits for them, and re-layouts  3.71 us (7%)
    pallas_call x1, Pallas kernels, mixed_pieces(): pl.pallas_call(functools.partial(mixed_kernel, count, quads, bundle), out...  28.1 us
    ppermute x11, starting transfers between devices, near(): return lax.ppermute(array, ('blk', 'str'), route)  6.65 us
    ppermute x4, starting transfers between devices, far(): return lax.ppermute(array, ('blk', 'str'), route)  5.91 us
    ppermute x11, waiting for transfers between devices, near(): return lax.ppermute(array, ('blk', 'str'), route)  5.09 us
    dynamic_slice x3, local copies, waits for them, and re-layouts, one_class(): lax.dynamic_slice(array, (symmetry, 0, start), (1, array.shape[1], width))  2.8 us
    pallas_call x1, Pallas kernels, plain_terms(): pl.pallas_call(functools.partial(plain_kernel, count), out_shape=jax.Shap...  2.4 us
    ppermute x4, waiting for transfers between devices, far(): return lax.ppermute(array, ('blk', 'str'), route)  1.83 us
    pallas_call x1, Pallas kernels, add_terms(): pl.pallas_call(functools.partial(add_kernel, count, classes), out_shape=j...  1.51 us
  transfers between devices with their start and end apart: 15, of which 7 were waited for; matrix products, arithmetic and copies ran while one was open for 5% of the time, Pallas kernels for 5%

profile of v7, /device:TPU:0, one launch (start us, length us, event | category | flops | bytes accessed | tf_op | source)
XLA Modules:
  0.0 55.9 jit_solution(11324190062703899048)
XLA Ops:
  0.0 0.0 copy-start
  0.0 0.5 collective-permute-start
  0.5 3.5 %collective-permute-start.5 = (bf16[64,1024]{1,0:T(8,128)(2,1)}, bf16[64,1024]{1,0:T(8,128)(2,1)S(1)}, u32[]{:S(2)}, u32[]{:S(2)}) collective-permute-start(bf16[64,1024]{1,0:T(8,128)(2,1)} %rows_ref.1), channel_id=1, source_target_pairs={{0,6},{1,7},{2,4},{3,5},{4,2},{5,3},{6,0},{7,1},{8,14},{9,15},{10,... | collective-permute-start | bytes 393224 | tf_op jit(solution)/shard_map/ppermute | solution.py:349
  4.0 0.5 collective-permute-start.3
  4.5 0.2 collective-permute-start.1
  4.6 0.0 copy-done
  4.7 1.2 %constant_dynamic-slice_fusion.3 = (s32[1,50,256]{2,0,1:T(1,128)S(1)}, s32[1,50,256]{2,0,1:T(1,128)S(1)}) fusion(s32[2,50,1024]{2,0,1:T(2,128)} %param.10, s32[]{:T(128)S(6)} %select_n.27, s32[]{:T(128)S(6)} %select_n.29, s32[2,50,1024]{2,0,1:T(2,128)} %param.9), kind=kLoop, calls=%fused_computation.12 | loop fusion | bytes 204808 | tf_op jit(solution)/shard_map/dynamic_slice | solution.py:360
  6.0 0.0 copy-start.2
  6.0 0.9 %copy-done.2 = bf16[64,1024]{1,0:T(8,128)(2,1)S(1)} copy-done((bf16[64,1024]{1,0:T(8,128)(2,1)S(1)}, bf16[64,1024]{1,0:T(8,128)(2,1)}, u32[]{:S(2)}) %copy-start.2) | copy-done | bytes 131096
  6.9 0.4 prepare.1
  7.3 1.5 %constant_dynamic-slice_fusion = (s32[1,50,512]{2,0,1:T(1,128)S(1)}, s32[1,50,512]{2,0,1:T(1,128)S(1)}) fusion(s32[2,50,2048]{2,0,1:T(2,128)} %param.12, s32[]{:T(128)S(6)} %select_n.27, s32[]{:T(128)S(6)} %select_n.30, s32[2,50,2048]{2,0,1:T(2,128)} %param.11), kind=kLoop, calls=%fused_computation.9 | loop fusion | bytes 409608 | tf_op jit(solution)/shard_map/dynamic_slice | solution.py:360
  8.9 0.0 collective-permute-done.5.refs_6_
  8.9 2.5 %collective-permute-done.1.refs_2_ = bf16[64,1024]{1,0:T(8,128)(2,1)S(1)} collective-permute-done((bf16[64,1024]{1,0:T(8,128)(2,1)}, bf16[64,1024]{1,0:T(8,128)(2,1)S(1)}, u32[]{:S(2)}, u32[]{:S(2)}) %collective-permute-start.1) | collective-permute-done | bytes 131104 | tf_op jit(solution)/shard_map/ppermute | solution.py:349
  11.4 0.0 collective-permute-start.2
  11.4 0.0 collective-permute-done.3.refs_4_
  11.4 0.5 collective-permute-start.4
  11.9 0.0 collective-permute-start.6
  11.9 0.0 collective-permute-done.refs_1_
  11.9 0.8 %collective-permute-done.2.refs_3_ = bf16[64,1024]{1,0:T(8,128)(2,1)S(1)} collective-permute-done((bf16[64,1024]{1,0:T(8,128)(2,1)S(1)}, bf16[64,1024]{1,0:T(8,128)(2,1)S(1)}, u32[]{:S(2)}, u32[]{:S(2)}) %collective-permute-start.2) | collective-permute-done | bytes 131104 | tf_op jit(solution)/shard_map/ppermute | solution.py:349
  12.7 0.2 collective-permute-done.4.refs_5_
  12.9 0.3 collective-permute-done.6.refs_7_
  13.2 0.0 copy-start.1
  13.2 0.0 copy-start.3
  13.3 28.1 %mixed.1 = (bf16[144,256]{1,0:T(8,128)(2,1)S(1)}, bf16[144,256]{1,0:T(8,128)(2,1)S(1)}, bf16[144,256]{1,0:T(8,128)(2,1)S(1)}, bf16[144,256]{1,0:T(8,128)(2,1)S(1)}) custom-call(s32[1]{0:T(128)} %bitcast.place_ref, bf16[64,1024]{1,0:T(8,128)(2,1)S(1)} %get-tuple-element.20.refs_0_, bf16[64,1024]{1,0:T(8,128)(2,1)S(1)} %collective-permute-done.refs_1_, ...), custom_call_target="tpu_custom_call" | custom-call | flops 22754099200 | bytes 1048576 | tf_op jit(solution)/shard_map/mixed/pallas_call | solution.py:207
  41.3 2.5 %collective-permute-start.7 = (bf16[144,256]{1,0:T(8,128)(2,1)S(1)}, bf16[144,256]{1,0:T(8,128)(2,1)S(1)}, u32[]{:S(2)}, u32[]{:S(2)}) collective-permute-start(bf16[144,256]{1,0:T(8,128)(2,1)S(1)} %get-tuple-element.27), channel_id=1, source_target_pairs={{0,14},{1,23},{2,12},{3,21},{4,10},{5,19},{6,8},{7,17},{8,6},{9,31... | collective-permute-start | bytes 221192 | tf_op jit(solution)/shard_map/ppermute | solution.py:357
  43.8 1.4 %collective-permute-start.8 = (bf16[144,256]{1,0:T(8,128)(2,1)S(1)}, bf16[144,256]{1,0:T(8,128)(2,1)S(1)}, u32[]{:S(2)}, u32[]{:S(2)}) collective-permute-start(bf16[144,256]{1,0:T(8,128)(2,1)S(1)} %get-tuple-element.30), channel_id=1, source_target_pairs={{0,12},{1,21},{2,14},{3,23},{4,8},{5,17},{6,10},{7,19},{8,4},{9,29... | collective-permute-start | bytes 221192 | tf_op jit(solution)/shard_map/ppermute | solution.py:357
  45.3 1.6 %collective-permute-start.9 = (bf16[144,256]{1,0:T(8,128)(2,1)S(1)}, bf16[144,256]{1,0:T(8,128)(2,1)S(1)}, u32[]{:S(2)}, u32[]{:S(2)}) collective-permute-start(bf16[144,256]{1,0:T(8,128)(2,1)S(1)} %get-tuple-element.31), channel_id=1, source_target_pairs={{0,10},{1,19},{2,8},{3,17},{4,14},{5,23},{6,12},{7,21},{8,2},{9,27... | collective-permute-start | bytes 221192 | tf_op jit(solution)/shard_map/ppermute | solution.py:357
  46.8 0.4 collective-permute-start.10
  47.3 0.0 copy-done.1
  47.3 0.0 copy-done.3
  47.3 2.4 %plain.1.base_ref = f32[64,1024]{1,0:T(8,128)S(1)} custom-call(s32[1]{0:T(128)} %bitcast.place_ref, bf16[64,1024]{1,0:T(8,128)(2,1)S(1)} %get-tuple-element.20.refs_0_, bf16[64,1024]{1,0:T(8,128)(2,1)S(1)} %collective-permute-done.refs_1_, bf16[64,1024]{1,0:T(8,128)(2,1)S(1)} %collective-permute-done.1.refs_2_, ...), custom_call_target="tpu_custom_call" | custom-call | flops 201326592 | bytes 3145728 | tf_op jit(solution)/shard_map/plain/pallas_call | solution.py:263
  49.7 0.0 collective-permute-done.7.refs_0_
  49.7 0.9 %collective-permute-start.11 = (bf16[144,256]{1,0:T(8,128)(2,1)S(1)}, bf16[144,256]{1,0:T(8,128)(2,1)S(1)}, u32[]{:S(2)}, u32[]{:S(2)}) collective-permute-start(bf16[144,256]{1,0:T(8,128)(2,1)S(1)} %collective-permute-done.7.refs_0_), channel_id=1, source_target_pairs={{0,1},{1,0},{2,3},{3,2},{4,5},{5,4},{6,7},{7,6},{8,9},{9,8},{10,11... | collective-permute-start | bytes 221192 | tf_op jit(solution)/shard_map/ppermute | solution.py:349
  50.6 0.0 collective-permute-done.8.refs_1_
  50.6 0.1 collective-permute-start.12
  50.7 0.5 collective-permute-done.9.refs_2_
  51.2 0.5 collective-permute-start.13
  51.7 1.3 %collective-permute-done.10.refs_3_ = bf16[144,256]{1,0:T(8,128)(2,1)S(1)} collective-permute-done((bf16[144,256]{1,0:T(8,128)(2,1)S(1)}, bf16[144,256]{1,0:T(8,128)(2,1)S(1)}, u32[]{:S(2)}, u32[]{:S(2)}) %collective-permute-start.10) | collective-permute-done | bytes 73760 | tf_op jit(solution)/shard_map/ppermute | solution.py:357
  53.0 0.0 collective-permute-start.14
  53.0 0.0 collective-permute-done.11.refs_4_
  53.0 0.0 collective-permute-done.12.refs_5_
  53.0 0.0 collective-permute-done.13.refs_6_
  53.0 1.2 %collective-permute-done.14.refs_7_ = bf16[144,256]{1,0:T(8,128)(2,1)S(1)} collective-permute-done((bf16[144,256]{1,0:T(8,128)(2,1)S(1)}, bf16[144,256]{1,0:T(8,128)(2,1)S(1)}, u32[]{:S(2)}, u32[]{:S(2)}) %collective-permute-start.14) | collective-permute-done | bytes 73760 | tf_op jit(solution)/shard_map/ppermute | solution.py:349
  54.3 1.5 %add.76 = f32[64,1024]{1,0:T(8,128)} custom-call(s32[1]{0:T(128)} %bitcast.place_ref, f32[64,1024]{1,0:T(8,128)S(1)} %plain.1.base_ref, bf16[144,256]{1,0:T(8,128)(2,1)S(1)} %collective-permute-done.7.refs_0_, bf16[144,256]{1,0:T(8,128)(2,1)S(1)} %collective-permute-done.8.refs_1_, bf16[144,256]{1,0:T(8,128)(2,1)S(1)} %collective-permute-done.9.refs_2_, ...), custom_call_target="tpu_custom_call" | custom-call | tf_op jit(solution)/shard_map/add/pallas_call | solution.py:315
  (4 shorter events, 0.1 us)
Async XLA Ops:
  0.0 4.6 %copy-start = (bf16[2,50,50]{2,0,1:T(2,128)(2,1)S(1)}, bf16[2,50,50]{2,0,1:T(2,128)(2,1)}, u32[]{:S(2)}) copy-start(bf16[2,50,50]{2,0,1:T(2,128)(2,1)} %param.13) | copy-start | bytes 30004
  0.0 11.9 %collective-permute-start = (bf16[64,1024]{1,0:T(8,128)(2,1)}, bf16[64,1024]{1,0:T(8,128)(2,1)S(1)}, u32[]{:S(2)}, u32[]{:S(2)}) collective-permute-start(bf16[64,1024]{1,0:T(8,128)(2,1)} %rows_ref.1), channel_id=1, source_target_pairs={{0,1},{1,0},{2,3},{3,2},{4,5},{5,4},{6,7},{7,6},{8,9},{9,8},{10,11... | collective-permute-start | bytes 393224 | tf_op jit(solution)/shard_map/ppermute | solution.py:349
  0.5 8.4 %collective-permute-start.5 = (bf16[64,1024]{1,0:T(8,128)(2,1)}, bf16[64,1024]{1,0:T(8,128)(2,1)S(1)}, u32[]{:S(2)}, u32[]{:S(2)}) collective-permute-start(bf16[64,1024]{1,0:T(8,128)(2,1)} %rows_ref.1), channel_id=1, source_target_pairs={{0,6},{1,7},{2,4},{3,5},{4,2},{5,3},{6,0},{7,1},{8,14},{9,15},{10,... | collective-permute-start | bytes 393224 | tf_op jit(solution)/shard_map/ppermute | solution.py:349
  4.0 7.4 %collective-permute-start.3 = (bf16[64,1024]{1,0:T(8,128)(2,1)}, bf16[64,1024]{1,0:T(8,128)(2,1)S(1)}, u32[]{:S(2)}, u32[]{:S(2)}) collective-permute-start(bf16[64,1024]{1,0:T(8,128)(2,1)} %rows_ref.1), channel_id=1, source_target_pairs={{0,4},{1,5},{2,6},{3,7},{4,0},{5,1},{6,2},{7,3},{8,12},{9,13},{10,... | collective-permute-start | bytes 393224 | tf_op jit(solution)/shard_map/ppermute | solution.py:349
  4.5 6.9 %collective-permute-start.1 = (bf16[64,1024]{1,0:T(8,128)(2,1)}, bf16[64,1024]{1,0:T(8,128)(2,1)S(1)}, u32[]{:S(2)}, u32[]{:S(2)}) collective-permute-start(bf16[64,1024]{1,0:T(8,128)(2,1)} %rows_ref.1), channel_id=1, source_target_pairs={{0,2},{1,3},{2,0},{3,1},{4,6},{5,7},{6,4},{7,5},{8,10},{9,11},{10,... | collective-permute-start | bytes 393224 | tf_op jit(solution)/shard_map/ppermute | solution.py:349
  6.0 0.9 %copy-start.2 = (bf16[64,1024]{1,0:T(8,128)(2,1)S(1)}, bf16[64,1024]{1,0:T(8,128)(2,1)}, u32[]{:S(2)}) copy-start(bf16[64,1024]{1,0:T(8,128)(2,1)} %rows_ref.1) | copy-start | bytes 393220
  11.4 1.3 %collective-permute-start.2 = (bf16[64,1024]{1,0:T(8,128)(2,1)S(1)}, bf16[64,1024]{1,0:T(8,128)(2,1)S(1)}, u32[]{:S(2)}, u32[]{:S(2)}) collective-permute-start(bf16[64,1024]{1,0:T(8,128)(2,1)S(1)} %collective-permute-done.1.refs_2_), channel_id=1, source_target_pairs={{0,1},{1,0},{2,3},{3,2},{4,5},{5,4},{6,7},{7,6},{8,9},{9,8},{10,11... | collective-permute-start | bytes 393224 | tf_op jit(solution)/shard_map/ppermute | solution.py:349
  11.4 1.5 %collective-permute-start.4 = (bf16[64,1024]{1,0:T(8,128)(2,1)S(1)}, bf16[64,1024]{1,0:T(8,128)(2,1)S(1)}, u32[]{:S(2)}, u32[]{:S(2)}) collective-permute-start(bf16[64,1024]{1,0:T(8,128)(2,1)S(1)} %collective-permute-done.3.refs_4_), channel_id=1, source_target_pairs={{0,1},{1,0},{2,3},{3,2},{4,5},{5,4},{6,7},{7,6},{8,9},{9,8},{10,11... | collective-permute-start | bytes 393224 | tf_op jit(solution)/shard_map/ppermute | solution.py:349
  11.9 1.3 %collective-permute-start.6 = (bf16[64,1024]{1,0:T(8,128)(2,1)S(1)}, bf16[64,1024]{1,0:T(8,128)(2,1)S(1)}, u32[]{:S(2)}, u32[]{:S(2)}) collective-permute-start(bf16[64,1024]{1,0:T(8,128)(2,1)S(1)} %collective-permute-done.5.refs_6_), channel_id=1, source_target_pairs={{0,1},{1,0},{2,3},{3,2},{4,5},{5,4},{6,7},{7,6},{8,9},{9,8},{10,11... | collective-permute-start | bytes 393224 | tf_op jit(solution)/shard_map/ppermute | solution.py:349
  13.2 34.0 %copy-start.1 = (bf16[1024,1024]{1,0:T(8,128)(2,1)S(1)}, bf16[1024,1024]{1,0:T(8,128)(2,1)}, u32[]{:S(2)}) copy-start(bf16[1024,1024]{1,0:T(8,128)(2,1)} %refs_9_.1) | copy-start | bytes 6291460
  13.2 34.0 %copy-start.3 = (bf16[64,512]{1,0:T(8,128)(2,1)S(1)}, bf16[64,512]{1,0:T(8,128)(2,1)}, u32[]{:S(2)}) copy-start(bf16[64,512]{1,0:T(8,128)(2,1)} %refs_8_.1) | copy-start | bytes 196612
  41.3 8.3 %collective-permute-start.7 = (bf16[144,256]{1,0:T(8,128)(2,1)S(1)}, bf16[144,256]{1,0:T(8,128)(2,1)S(1)}, u32[]{:S(2)}, u32[]{:S(2)}) collective-permute-start(bf16[144,256]{1,0:T(8,128)(2,1)S(1)} %get-tuple-element.27), channel_id=1, source_target_pairs={{0,14},{1,23},{2,12},{3,21},{4,10},{5,19},{6,8},{7,17},{8,6},{9,31... | collective-permute-start | bytes 221192 | tf_op jit(solution)/shard_map/ppermute | solution.py:357
  43.8 6.8 %collective-permute-start.8 = (bf16[144,256]{1,0:T(8,128)(2,1)S(1)}, bf16[144,256]{1,0:T(8,128)(2,1)S(1)}, u32[]{:S(2)}, u32[]{:S(2)}) collective-permute-start(bf16[144,256]{1,0:T(8,128)(2,1)S(1)} %get-tuple-element.30), channel_id=1, source_target_pairs={{0,12},{1,21},{2,14},{3,23},{4,8},{5,17},{6,10},{7,19},{8,4},{9,29... | collective-permute-start | bytes 221192 | tf_op jit(solution)/shard_map/ppermute | solution.py:357
  45.3 6.0 %collective-permute-start.9 = (bf16[144,256]{1,0:T(8,128)(2,1)S(1)}, bf16[144,256]{1,0:T(8,128)(2,1)S(1)}, u32[]{:S(2)}, u32[]{:S(2)}) collective-permute-start(bf16[144,256]{1,0:T(8,128)(2,1)S(1)} %get-tuple-element.31), channel_id=1, source_target_pairs={{0,10},{1,19},{2,8},{3,17},{4,14},{5,23},{6,12},{7,21},{8,2},{9,27... | collective-permute-start | bytes 221192 | tf_op jit(solution)/shard_map/ppermute | solution.py:357
  46.8 6.2 %collective-permute-start.10 = (bf16[144,256]{1,0:T(8,128)(2,1)S(1)}, bf16[144,256]{1,0:T(8,128)(2,1)S(1)}, u32[]{:S(2)}, u32[]{:S(2)}) collective-permute-start(bf16[144,256]{1,0:T(8,128)(2,1)S(1)} %get-tuple-element.32), channel_id=1, source_target_pairs={{0,8},{1,17},{2,10},{3,19},{4,12},{5,21},{6,14},{7,23},{8,0},{9,25... | collective-permute-start | bytes 221192 | tf_op jit(solution)/shard_map/ppermute | solution.py:357
  49.7 3.3 %collective-permute-start.11 = (bf16[144,256]{1,0:T(8,128)(2,1)S(1)}, bf16[144,256]{1,0:T(8,128)(2,1)S(1)}, u32[]{:S(2)}, u32[]{:S(2)}) collective-permute-start(bf16[144,256]{1,0:T(8,128)(2,1)S(1)} %collective-permute-done.7.refs_0_), channel_id=1, source_target_pairs={{0,1},{1,0},{2,3},{3,2},{4,5},{5,4},{6,7},{7,6},{8,9},{9,8},{10,11... | collective-permute-start | bytes 221192 | tf_op jit(solution)/shard_map/ppermute | solution.py:349
  50.6 2.4 %collective-permute-start.12 = (bf16[144,256]{1,0:T(8,128)(2,1)S(1)}, bf16[144,256]{1,0:T(8,128)(2,1)S(1)}, u32[]{:S(2)}, u32[]{:S(2)}) collective-permute-start(bf16[144,256]{1,0:T(8,128)(2,1)S(1)} %collective-permute-done.8.refs_1_), channel_id=1, source_target_pairs={{0,1},{1,0},{2,3},{3,2},{4,5},{5,4},{6,7},{7,6},{8,9},{9,8},{10,11... | collective-permute-start | bytes 221192 | tf_op jit(solution)/shard_map/ppermute | solution.py:349
  51.2 1.8 %collective-permute-start.13 = (bf16[144,256]{1,0:T(8,128)(2,1)S(1)}, bf16[144,256]{1,0:T(8,128)(2,1)S(1)}, u32[]{:S(2)}, u32[]{:S(2)}) collective-permute-start(bf16[144,256]{1,0:T(8,128)(2,1)S(1)} %collective-permute-done.9.refs_2_), channel_id=1, source_target_pairs={{0,1},{1,0},{2,3},{3,2},{4,5},{5,4},{6,7},{7,6},{8,9},{9,8},{10,11... | collective-permute-start | bytes 221192 | tf_op jit(solution)/shard_map/ppermute | solution.py:349
  53.0 1.3 %collective-permute-start.14 = (bf16[144,256]{1,0:T(8,128)(2,1)S(1)}, bf16[144,256]{1,0:T(8,128)(2,1)S(1)}, u32[]{:S(2)}, u32[]{:S(2)}) collective-permute-start(bf16[144,256]{1,0:T(8,128)(2,1)S(1)} %collective-permute-done.10.refs_3_), channel_id=1, source_target_pairs={{0,1},{1,0},{2,3},{3,2},{4,5},{5,4},{6,7},{7,6},{8,9},{9,8},{10,11... | collective-permute-start | bytes 221192 | tf_op jit(solution)/shard_map/ppermute | solution.py:349

commit v8 on v7

--- a/solution.py
+++ b/solution.py
@@ -127,7 +127,7 @@
     return [jnp.concatenate(side, axis=1).astype(jnp.bfloat16) for side in (evens, odds)]
 
 
-def mixed_kernel(count, quads, bundle, place_ref, *refs):
+def mixed_kernel(count, quads, place_ref, *refs):
     pieces = refs[:count]
     code_ref, kron_ref, alpha_ref = refs[count : count + 3]
     outs = refs[count + 3 : count + 3 + count // 2]
@@ -159,28 +159,18 @@
     signs[...] = ((alpha_ref[...] & 3) - 1).astype(jnp.float32)
     position = lax.broadcasted_iota(jnp.int32, (block_rows, block_rows), 0)
     position = jnp.bitwise_xor(position, place_ref[0] * local_rows).astype(jnp.int16)
-    total[...] = jnp.zeros_like(total)
-
-    def body(at, carry):
-        term = None
-        for offset in range(bundle):
-            pair = bundle * at + offset
-            selector = jnp.where(
-                position == indices[pl.ds(pair, 1), :].astype(jnp.int16),
-                signs[pl.ds(pair, 1), :].astype(jnp.bfloat16),
-                jnp.zeros((), jnp.bfloat16),
-            )
-            part = jnp.dot(
-                images[lax.div(pair, 2), lax.rem(pair, 2)],
-                selector,
-                preferred_element_type=jnp.float32,
-            )
-            term = part if term is None else term + part
-        total[...] += term
-        return carry
-
-    lax.fori_loop(0, 2 * halves // bundle, body, 0)
-    codes, scale = coded(total[...])
+    term = None
+    for pair in range(2 * halves):
+        selector = jnp.where(
+            position == indices[pair : pair + 1, :].astype(jnp.int16),
+            signs[pair : pair + 1, :].astype(jnp.bfloat16),
+            jnp.zeros((), jnp.bfloat16),
+        )
+        part = jnp.dot(
+            images[pair // 2, pair % 2], selector, preferred_element_type=jnp.float32
+        )
+        term = part if term is None else term + part
+    codes, scale = coded(term)
     total[...] = codes.astype(jnp.float32)
     quad_count = window // QUAD
     for at in range(block_rows // 128):
@@ -201,11 +191,10 @@
     count = len(pieces)
     local_rows, beta_count = pieces[0].shape
     pairs, block_rows = alpha_codes.shape
-    bundle = next(size for size in (25, 10, 5, 2, 1) if pairs % size == 0)
     quads = min(8, window // QUAD, 8 * 512 // block_rows)
     flops = 2 * window * pairs * block_rows * (beta_count + pairs * QUAD + block_rows)
     return pl.pallas_call(
-        functools.partial(mixed_kernel, count, quads, bundle),
+        functools.partial(mixed_kernel, count, quads),
         out_shape=[jax.ShapeDtypeStruct((2 * local_rows + SCALE_ROWS, window), jnp.bfloat16)]
         * (count // 2),
         in_specs=[pl.BlockSpec(memory_space=pltpu.SMEM)]

time: 56.1 us -> 55.4 us (0.988)
  Pallas kernels: 32.4 us -> 31.7 us
    pallas_call x1, Pallas kernels: 28.1 us -> 27.3 us  [mixed_pieces(): pl.pallas_call(functools.partial(mixed_kernel, count, quads), out_shape=[...]
where the time goes in v8:
time: 55.4 us; the launch traced here: 55.2 us
  Pallas kernels  31.7 us (57%)
  starting transfers between devices  12.5 us (23%)
  waiting for transfers between devices  6.95 us (13%)
  local copies, waits for them, and re-layouts  3.71 us (7%)
    pallas_call x1, Pallas kernels, mixed_pieces(): pl.pallas_call(functools.partial(mixed_kernel, count, quads), out_shape=[...  27.3 us
    ppermute x11, starting transfers between devices, near(): return lax.ppermute(array, ('blk', 'str'), route)  6.62 us
    ppermute x4, starting transfers between devices, far(): return lax.ppermute(array, ('blk', 'str'), route)  5.91 us
    ppermute x11, waiting for transfers between devices, near(): return lax.ppermute(array, ('blk', 'str'), route)  5.09 us
    dynamic_slice x3, local copies, waits for them, and re-layouts, one_class(): lax.dynamic_slice(array, (symmetry, 0, start), (1, array.shape[1], width))  2.8 us
    pallas_call x1, Pallas kernels, plain_terms(): pl.pallas_call(functools.partial(plain_kernel, count), out_shape=jax.Shap...  2.4 us
    ppermute x4, waiting for transfers between devices, far(): return lax.ppermute(array, ('blk', 'str'), route)  1.86 us
    pallas_call x1, Pallas kernels, add_terms(): pl.pallas_call(functools.partial(add_kernel, count, classes), out_shape=j...  1.51 us
  transfers between devices with their start and end apart: 15, of which 7 were waited for; matrix products, arithmetic and copies ran while one was open for 5% of the time, Pallas kernels for 5%

profile of v8, /device:TPU:0, one launch (start us, length us, event | category | flops | bytes accessed | tf_op | source)
XLA Modules:
  0.0 55.2 jit_solution(4528527825304575747)
XLA Ops:
  0.0 0.0 copy-start
  0.0 0.5 collective-permute-start
  0.5 3.5 %collective-permute-start.5 = (bf16[64,1024]{1,0:T(8,128)(2,1)}, bf16[64,1024]{1,0:T(8,128)(2,1)S(1)}, u32[]{:S(2)}, u32[]{:S(2)}) collective-permute-start(bf16[64,1024]{1,0:T(8,128)(2,1)} %rows_ref.1), channel_id=1, source_target_pairs={{0,6},{1,7},{2,4},{3,5},{4,2},{5,3},{6,0},{7,1},{8,14},{9,15},{10,... | collective-permute-start | bytes 393224 | tf_op jit(solution)/shard_map/ppermute | solution.py:338
  4.0 0.5 collective-permute-start.3
  4.5 0.2 collective-permute-start.1
  4.6 0.0 copy-done
  4.7 1.2 %constant_dynamic-slice_fusion.3 = (s32[1,50,256]{2,0,1:T(1,128)S(1)}, s32[1,50,256]{2,0,1:T(1,128)S(1)}) fusion(s32[2,50,1024]{2,0,1:T(2,128)} %param.10, s32[]{:T(128)S(6)} %select_n.27, s32[]{:T(128)S(6)} %select_n.29, s32[2,50,1024]{2,0,1:T(2,128)} %param.9), kind=kLoop, calls=%fused_computation.12 | loop fusion | bytes 204808 | tf_op jit(solution)/shard_map/dynamic_slice | solution.py:349
  6.0 0.0 copy-start.2
  6.0 0.9 %copy-done.2 = bf16[64,1024]{1,0:T(8,128)(2,1)S(1)} copy-done((bf16[64,1024]{1,0:T(8,128)(2,1)S(1)}, bf16[64,1024]{1,0:T(8,128)(2,1)}, u32[]{:S(2)}) %copy-start.2) | copy-done | bytes 131096
  6.9 0.4 prepare.1
  7.3 1.5 %constant_dynamic-slice_fusion = (s32[1,50,512]{2,0,1:T(1,128)S(1)}, s32[1,50,512]{2,0,1:T(1,128)S(1)}) fusion(s32[2,50,2048]{2,0,1:T(2,128)} %param.12, s32[]{:T(128)S(6)} %select_n.27, s32[]{:T(128)S(6)} %select_n.30, s32[2,50,2048]{2,0,1:T(2,128)} %param.11), kind=kLoop, calls=%fused_computation.9 | loop fusion | bytes 409608 | tf_op jit(solution)/shard_map/dynamic_slice | solution.py:349
  8.9 0.0 collective-permute-done.5.refs_6_
  8.9 2.5 %collective-permute-done.1.refs_2_ = bf16[64,1024]{1,0:T(8,128)(2,1)S(1)} collective-permute-done((bf16[64,1024]{1,0:T(8,128)(2,1)}, bf16[64,1024]{1,0:T(8,128)(2,1)S(1)}, u32[]{:S(2)}, u32[]{:S(2)}) %collective-permute-start.1) | collective-permute-done | bytes 131104 | tf_op jit(solution)/shard_map/ppermute | solution.py:338
  11.4 0.0 collective-permute-start.2
  11.4 0.0 collective-permute-done.3.refs_4_
  11.4 0.5 collective-permute-start.4
  11.9 0.0 collective-permute-start.6
  11.9 0.0 collective-permute-done.refs_1_
  11.9 0.8 %collective-permute-done.2.refs_3_ = bf16[64,1024]{1,0:T(8,128)(2,1)S(1)} collective-permute-done((bf16[64,1024]{1,0:T(8,128)(2,1)S(1)}, bf16[64,1024]{1,0:T(8,128)(2,1)S(1)}, u32[]{:S(2)}, u32[]{:S(2)}) %collective-permute-start.2) | collective-permute-done | bytes 131104 | tf_op jit(solution)/shard_map/ppermute | solution.py:338
  12.7 0.2 collective-permute-done.4.refs_5_
  12.9 0.3 collective-permute-done.6.refs_7_
  13.2 0.0 copy-start.1
  13.2 0.0 copy-start.3
  13.3 27.3 %mixed.1 = (bf16[144,256]{1,0:T(8,128)(2,1)S(1)}, bf16[144,256]{1,0:T(8,128)(2,1)S(1)}, bf16[144,256]{1,0:T(8,128)(2,1)S(1)}, bf16[144,256]{1,0:T(8,128)(2,1)S(1)}) custom-call(s32[1]{0:T(128)} %bitcast.place_ref, bf16[64,1024]{1,0:T(8,128)(2,1)S(1)} %get-tuple-element.20.refs_0_, bf16[64,1024]{1,0:T(8,128)(2,1)S(1)} %collective-permute-done.refs_1_, ...), custom_call_target="tpu_custom_call" | custom-call | flops 22754099200 | bytes 1048576 | tf_op jit(solution)/shard_map/mixed/pallas_call | solution.py:196
  40.6 2.5 %collective-permute-start.7 = (bf16[144,256]{1,0:T(8,128)(2,1)S(1)}, bf16[144,256]{1,0:T(8,128)(2,1)S(1)}, u32[]{:S(2)}, u32[]{:S(2)}) collective-permute-start(bf16[144,256]{1,0:T(8,128)(2,1)S(1)} %get-tuple-element.27), channel_id=1, source_target_pairs={{0,14},{1,23},{2,12},{3,21},{4,10},{5,19},{6,8},{7,17},{8,6},{9,31... | collective-permute-start | bytes 221192 | tf_op jit(solution)/shard_map/ppermute | solution.py:346
  43.1 1.4 %collective-permute-start.8 = (bf16[144,256]{1,0:T(8,128)(2,1)S(1)}, bf16[144,256]{1,0:T(8,128)(2,1)S(1)}, u32[]{:S(2)}, u32[]{:S(2)}) collective-permute-start(bf16[144,256]{1,0:T(8,128)(2,1)S(1)} %get-tuple-element.30), channel_id=1, source_target_pairs={{0,12},{1,21},{2,14},{3,23},{4,8},{5,17},{6,10},{7,19},{8,4},{9,29... | collective-permute-start | bytes 221192 | tf_op jit(solution)/shard_map/ppermute | solution.py:346
  44.5 1.5 %collective-permute-start.9 = (bf16[144,256]{1,0:T(8,128)(2,1)S(1)}, bf16[144,256]{1,0:T(8,128)(2,1)S(1)}, u32[]{:S(2)}, u32[]{:S(2)}) collective-permute-start(bf16[144,256]{1,0:T(8,128)(2,1)S(1)} %get-tuple-element.31), channel_id=1, source_target_pairs={{0,10},{1,19},{2,8},{3,17},{4,14},{5,23},{6,12},{7,21},{8,2},{9,27... | collective-permute-start | bytes 221192 | tf_op jit(solution)/shard_map/ppermute | solution.py:346
  46.0 0.5 collective-permute-start.10
  46.5 0.0 copy-done.1
  46.5 0.0 copy-done.3
  46.5 2.4 %plain.1.base_ref = f32[64,1024]{1,0:T(8,128)S(1)} custom-call(s32[1]{0:T(128)} %bitcast.place_ref, bf16[64,1024]{1,0:T(8,128)(2,1)S(1)} %get-tuple-element.20.refs_0_, bf16[64,1024]{1,0:T(8,128)(2,1)S(1)} %collective-permute-done.refs_1_, bf16[64,1024]{1,0:T(8,128)(2,1)S(1)} %collective-permute-done.1.refs_2_, ...), custom_call_target="tpu_custom_call" | custom-call | flops 201326592 | bytes 3145728 | tf_op jit(solution)/shard_map/plain/pallas_call | solution.py:252
  48.9 0.0 collective-permute-done.7.refs_0_
  48.9 0.9 %collective-permute-start.11 = (bf16[144,256]{1,0:T(8,128)(2,1)S(1)}, bf16[144,256]{1,0:T(8,128)(2,1)S(1)}, u32[]{:S(2)}, u32[]{:S(2)}) collective-permute-start(bf16[144,256]{1,0:T(8,128)(2,1)S(1)} %collective-permute-done.7.refs_0_), channel_id=1, source_target_pairs={{0,1},{1,0},{2,3},{3,2},{4,5},{5,4},{6,7},{7,6},{8,9},{9,8},{10,11... | collective-permute-start | bytes 221192 | tf_op jit(solution)/shard_map/ppermute | solution.py:338
  49.8 0.0 collective-permute-done.8.refs_1_
  49.8 0.1 collective-permute-start.12
  49.9 0.5 collective-permute-done.9.refs_2_
  50.5 0.5 collective-permute-start.13
  50.9 1.3 %collective-permute-done.10.refs_3_ = bf16[144,256]{1,0:T(8,128)(2,1)S(1)} collective-permute-done((bf16[144,256]{1,0:T(8,128)(2,1)S(1)}, bf16[144,256]{1,0:T(8,128)(2,1)S(1)}, u32[]{:S(2)}, u32[]{:S(2)}) %collective-permute-start.10) | collective-permute-done | bytes 73760 | tf_op jit(solution)/shard_map/ppermute | solution.py:346
  52.2 0.0 collective-permute-start.14
  52.3 0.0 collective-permute-done.11.refs_4_
  52.3 0.0 collective-permute-done.12.refs_5_
  52.3 0.0 collective-permute-done.13.refs_6_
  52.3 1.2 %collective-permute-done.14.refs_7_ = bf16[144,256]{1,0:T(8,128)(2,1)S(1)} collective-permute-done((bf16[144,256]{1,0:T(8,128)(2,1)S(1)}, bf16[144,256]{1,0:T(8,128)(2,1)S(1)}, u32[]{:S(2)}, u32[]{:S(2)}) %collective-permute-start.14) | collective-permute-done | bytes 73760 | tf_op jit(solution)/shard_map/ppermute | solution.py:338
  53.5 1.5 %add.76 = f32[64,1024]{1,0:T(8,128)} custom-call(s32[1]{0:T(128)} %bitcast.place_ref, f32[64,1024]{1,0:T(8,128)S(1)} %plain.1.base_ref, bf16[144,256]{1,0:T(8,128)(2,1)S(1)} %collective-permute-done.7.refs_0_, bf16[144,256]{1,0:T(8,128)(2,1)S(1)} %collective-permute-done.8.refs_1_, bf16[144,256]{1,0:T(8,128)(2,1)S(1)} %collective-permute-done.9.refs_2_, ...), custom_call_target="tpu_custom_call" | custom-call | tf_op jit(solution)/shard_map/add/pallas_call | solution.py:304
  (4 shorter events, 0.1 us)
Async XLA Ops:
  0.0 4.6 %copy-start = (bf16[2,50,50]{2,0,1:T(2,128)(2,1)S(1)}, bf16[2,50,50]{2,0,1:T(2,128)(2,1)}, u32[]{:S(2)}) copy-start(bf16[2,50,50]{2,0,1:T(2,128)(2,1)} %param.13) | copy-start | bytes 30004
  0.0 11.9 %collective-permute-start = (bf16[64,1024]{1,0:T(8,128)(2,1)}, bf16[64,1024]{1,0:T(8,128)(2,1)S(1)}, u32[]{:S(2)}, u32[]{:S(2)}) collective-permute-start(bf16[64,1024]{1,0:T(8,128)(2,1)} %rows_ref.1), channel_id=1, source_target_pairs={{0,1},{1,0},{2,3},{3,2},{4,5},{5,4},{6,7},{7,6},{8,9},{9,8},{10,11... | collective-permute-start | bytes 393224 | tf_op jit(solution)/shard_map/ppermute | solution.py:338
  0.5 8.4 %collective-permute-start.5 = (bf16[64,1024]{1,0:T(8,128)(2,1)}, bf16[64,1024]{1,0:T(8,128)(2,1)S(1)}, u32[]{:S(2)}, u32[]{:S(2)}) collective-permute-start(bf16[64,1024]{1,0:T(8,128)(2,1)} %rows_ref.1), channel_id=1, source_target_pairs={{0,6},{1,7},{2,4},{3,5},{4,2},{5,3},{6,0},{7,1},{8,14},{9,15},{10,... | collective-permute-start | bytes 393224 | tf_op jit(solution)/shard_map/ppermute | solution.py:338
  4.0 7.4 %collective-permute-start.3 = (bf16[64,1024]{1,0:T(8,128)(2,1)}, bf16[64,1024]{1,0:T(8,128)(2,1)S(1)}, u32[]{:S(2)}, u32[]{:S(2)}) collective-permute-start(bf16[64,1024]{1,0:T(8,128)(2,1)} %rows_ref.1), channel_id=1, source_target_pairs={{0,4},{1,5},{2,6},{3,7},{4,0},{5,1},{6,2},{7,3},{8,12},{9,13},{10,... | collective-permute-start | bytes 393224 | tf_op jit(solution)/shard_map/ppermute | solution.py:338
  4.5 6.9 %collective-permute-start.1 = (bf16[64,1024]{1,0:T(8,128)(2,1)}, bf16[64,1024]{1,0:T(8,128)(2,1)S(1)}, u32[]{:S(2)}, u32[]{:S(2)}) collective-permute-start(bf16[64,1024]{1,0:T(8,128)(2,1)} %rows_ref.1), channel_id=1, source_target_pairs={{0,2},{1,3},{2,0},{3,1},{4,6},{5,7},{6,4},{7,5},{8,10},{9,11},{10,... | collective-permute-start | bytes 393224 | tf_op jit(solution)/shard_map/ppermute | solution.py:338
  6.0 0.9 %copy-start.2 = (bf16[64,1024]{1,0:T(8,128)(2,1)S(1)}, bf16[64,1024]{1,0:T(8,128)(2,1)}, u32[]{:S(2)}) copy-start(bf16[64,1024]{1,0:T(8,128)(2,1)} %rows_ref.1) | copy-start | bytes 393220
  11.4 1.3 %collective-permute-start.2 = (bf16[64,1024]{1,0:T(8,128)(2,1)S(1)}, bf16[64,1024]{1,0:T(8,128)(2,1)S(1)}, u32[]{:S(2)}, u32[]{:S(2)}) collective-permute-start(bf16[64,1024]{1,0:T(8,128)(2,1)S(1)} %collective-permute-done.1.refs_2_), channel_id=1, source_target_pairs={{0,1},{1,0},{2,3},{3,2},{4,5},{5,4},{6,7},{7,6},{8,9},{9,8},{10,11... | collective-permute-start | bytes 393224 | tf_op jit(solution)/shard_map/ppermute | solution.py:338
  11.4 1.5 %collective-permute-start.4 = (bf16[64,1024]{1,0:T(8,128)(2,1)S(1)}, bf16[64,1024]{1,0:T(8,128)(2,1)S(1)}, u32[]{:S(2)}, u32[]{:S(2)}) collective-permute-start(bf16[64,1024]{1,0:T(8,128)(2,1)S(1)} %collective-permute-done.3.refs_4_), channel_id=1, source_target_pairs={{0,1},{1,0},{2,3},{3,2},{4,5},{5,4},{6,7},{7,6},{8,9},{9,8},{10,11... | collective-permute-start | bytes 393224 | tf_op jit(solution)/shard_map/ppermute | solution.py:338
  11.9 1.3 %collective-permute-start.6 = (bf16[64,1024]{1,0:T(8,128)(2,1)S(1)}, bf16[64,1024]{1,0:T(8,128)(2,1)S(1)}, u32[]{:S(2)}, u32[]{:S(2)}) collective-permute-start(bf16[64,1024]{1,0:T(8,128)(2,1)S(1)} %collective-permute-done.5.refs_6_), channel_id=1, source_target_pairs={{0,1},{1,0},{2,3},{3,2},{4,5},{5,4},{6,7},{7,6},{8,9},{9,8},{10,11... | collective-permute-start | bytes 393224 | tf_op jit(solution)/shard_map/ppermute | solution.py:338
  13.2 33.2 %copy-start.1 = (bf16[1024,1024]{1,0:T(8,128)(2,1)S(1)}, bf16[1024,1024]{1,0:T(8,128)(2,1)}, u32[]{:S(2)}) copy-start(bf16[1024,1024]{1,0:T(8,128)(2,1)} %refs_9_.1) | copy-start | bytes 6291460
  13.2 33.2 %copy-start.3 = (bf16[64,512]{1,0:T(8,128)(2,1)S(1)}, bf16[64,512]{1,0:T(8,128)(2,1)}, u32[]{:S(2)}) copy-start(bf16[64,512]{1,0:T(8,128)(2,1)} %refs_8_.1) | copy-start | bytes 196612
  40.6 8.3 %collective-permute-start.7 = (bf16[144,256]{1,0:T(8,128)(2,1)S(1)}, bf16[144,256]{1,0:T(8,128)(2,1)S(1)}, u32[]{:S(2)}, u32[]{:S(2)}) collective-permute-start(bf16[144,256]{1,0:T(8,128)(2,1)S(1)} %get-tuple-element.27), channel_id=1, source_target_pairs={{0,14},{1,23},{2,12},{3,21},{4,10},{5,19},{6,8},{7,17},{8,6},{9,31... | collective-permute-start | bytes 221192 | tf_op jit(solution)/shard_map/ppermute | solution.py:346
  43.1 6.8 %collective-permute-start.8 = (bf16[144,256]{1,0:T(8,128)(2,1)S(1)}, bf16[144,256]{1,0:T(8,128)(2,1)S(1)}, u32[]{:S(2)}, u32[]{:S(2)}) collective-permute-start(bf16[144,256]{1,0:T(8,128)(2,1)S(1)} %get-tuple-element.30), channel_id=1, source_target_pairs={{0,12},{1,21},{2,14},{3,23},{4,8},{5,17},{6,10},{7,19},{8,4},{9,29... | collective-permute-start | bytes 221192 | tf_op jit(solution)/shard_map/ppermute | solution.py:346
  44.5 6.0 %collective-permute-start.9 = (bf16[144,256]{1,0:T(8,128)(2,1)S(1)}, bf16[144,256]{1,0:T(8,128)(2,1)S(1)}, u32[]{:S(2)}, u32[]{:S(2)}) collective-permute-start(bf16[144,256]{1,0:T(8,128)(2,1)S(1)} %get-tuple-element.31), channel_id=1, source_target_pairs={{0,10},{1,19},{2,8},{3,17},{4,14},{5,23},{6,12},{7,21},{8,2},{9,27... | collective-permute-start | bytes 221192 | tf_op jit(solution)/shard_map/ppermute | solution.py:346
  46.0 6.2 %collective-permute-start.10 = (bf16[144,256]{1,0:T(8,128)(2,1)S(1)}, bf16[144,256]{1,0:T(8,128)(2,1)S(1)}, u32[]{:S(2)}, u32[]{:S(2)}) collective-permute-start(bf16[144,256]{1,0:T(8,128)(2,1)S(1)} %get-tuple-element.32), channel_id=1, source_target_pairs={{0,8},{1,17},{2,10},{3,19},{4,12},{5,21},{6,14},{7,23},{8,0},{9,25... | collective-permute-start | bytes 221192 | tf_op jit(solution)/shard_map/ppermute | solution.py:346
  48.9 3.3 %collective-permute-start.11 = (bf16[144,256]{1,0:T(8,128)(2,1)S(1)}, bf16[144,256]{1,0:T(8,128)(2,1)S(1)}, u32[]{:S(2)}, u32[]{:S(2)}) collective-permute-start(bf16[144,256]{1,0:T(8,128)(2,1)S(1)} %collective-permute-done.7.refs_0_), channel_id=1, source_target_pairs={{0,1},{1,0},{2,3},{3,2},{4,5},{5,4},{6,7},{7,6},{8,9},{9,8},{10,11... | collective-permute-start | bytes 221192 | tf_op jit(solution)/shard_map/ppermute | solution.py:338
  49.8 2.4 %collective-permute-start.12 = (bf16[144,256]{1,0:T(8,128)(2,1)S(1)}, bf16[144,256]{1,0:T(8,128)(2,1)S(1)}, u32[]{:S(2)}, u32[]{:S(2)}) collective-permute-start(bf16[144,256]{1,0:T(8,128)(2,1)S(1)} %collective-permute-done.8.refs_1_), channel_id=1, source_target_pairs={{0,1},{1,0},{2,3},{3,2},{4,5},{5,4},{6,7},{7,6},{8,9},{9,8},{10,11... | collective-permute-start | bytes 221192 | tf_op jit(solution)/shard_map/ppermute | solution.py:338
  50.5 1.8 %collective-permute-start.13 = (bf16[144,256]{1,0:T(8,128)(2,1)S(1)}, bf16[144,256]{1,0:T(8,128)(2,1)S(1)}, u32[]{:S(2)}, u32[]{:S(2)}) collective-permute-start(bf16[144,256]{1,0:T(8,128)(2,1)S(1)} %collective-permute-done.9.refs_2_), channel_id=1, source_target_pairs={{0,1},{1,0},{2,3},{3,2},{4,5},{5,4},{6,7},{7,6},{8,9},{9,8},{10,11... | collective-permute-start | bytes 221192 | tf_op jit(solution)/shard_map/ppermute | solution.py:338
  52.2 1.3 %collective-permute-start.14 = (bf16[144,256]{1,0:T(8,128)(2,1)S(1)}, bf16[144,256]{1,0:T(8,128)(2,1)S(1)}, u32[]{:S(2)}, u32[]{:S(2)}) collective-permute-start(bf16[144,256]{1,0:T(8,128)(2,1)S(1)} %collective-permute-done.10.refs_3_), channel_id=1, source_target_pairs={{0,1},{1,0},{2,3},{3,2},{4,5},{5,4},{6,7},{7,6},{8,9},{9,8},{10,11... | collective-permute-start | bytes 221192 | tf_op jit(solution)/shard_map/ppermute | solution.py:338

commit v9 on v8

--- a/solution.py
+++ b/solution.py
@@ -365,7 +365,7 @@
     sent = mixed_pieces(place, pieces, codes, kron, alpha_codes, window)
     own = [far(sent[at], 2 * at) for at in reversed(range(count // 2))]
     base = plain_terms(place, pieces, alpha_operator, beta_operator)
-    own[0], base = lax.optimization_barrier((own[0], base))
+    own[-1], base = lax.optimization_barrier((own[-1], base))
     passed = [near(rows, 1) for rows in own]
     return add_terms(place, base, own, passed, classes)
 

time: 55.4 us -> 55.5 us (level)
  starting transfers between devices: 12.5 us -> 13.4 us
  waiting for transfers between devices: 6.95 us -> 6.21 us
    ppermute x11, starting transfers between devices: 6.62 us -> 7.49 us  [near(): return lax.ppermute(array, ('blk', 'str'), route)]
where the time goes in v9:
time: 55.5 us; the launch traced here: 55.3 us
  Pallas kernels  31.7 us (57%)
  starting transfers between devices  13.4 us (24%)
  waiting for transfers between devices  6.21 us (11%)
  local copies, waits for them, and re-layouts  3.71 us (7%)
    pallas_call x1, Pallas kernels, mixed_pieces(): pl.pallas_call(functools.partial(mixed_kernel, count, quads), out_shape=[...  27.3 us
    ppermute x11, starting transfers between devices, near(): return lax.ppermute(array, ('blk', 'str'), route)  7.49 us
    ppermute x4, starting transfers between devices, far(): return lax.ppermute(array, ('blk', 'str'), route)  5.91 us
    ppermute x11, waiting for transfers between devices, near(): return lax.ppermute(array, ('blk', 'str'), route)  4.76 us
    dynamic_slice x3, local copies, waits for them, and re-layouts, one_class(): lax.dynamic_slice(array, (symmetry, 0, start), (1, array.shape[1], width))  2.8 us
    pallas_call x1, Pallas kernels, plain_terms(): pl.pallas_call(functools.partial(plain_kernel, count), out_shape=jax.Shap...  2.4 us
    pallas_call x1, Pallas kernels, add_terms(): pl.pallas_call(functools.partial(add_kernel, count, classes), out_shape=j...  1.51 us
    ppermute x4, waiting for transfers between devices, far(): return lax.ppermute(array, ('blk', 'str'), route)  1.46 us
  transfers between devices with their start and end apart: 15, of which 7 were waited for; matrix products, arithmetic and copies ran while one was open for 5% of the time, Pallas kernels for 5%

profile of v9, /device:TPU:0, one launch (start us, length us, event | category | flops | bytes accessed | tf_op | source)
XLA Modules:
  0.0 55.3 jit_solution(5530834247045802844)
XLA Ops:
  0.0 0.0 copy-start
  0.0 0.5 collective-permute-start
  0.5 3.5 %collective-permute-start.5 = (bf16[64,1024]{1,0:T(8,128)(2,1)}, bf16[64,1024]{1,0:T(8,128)(2,1)S(1)}, u32[]{:S(2)}, u32[]{:S(2)}) collective-permute-start(bf16[64,1024]{1,0:T(8,128)(2,1)} %rows_ref.1), channel_id=1, source_target_pairs={{0,6},{1,7},{2,4},{3,5},{4,2},{5,3},{6,0},{7,1},{8,14},{9,15},{10,... | collective-permute-start | bytes 393224 | tf_op jit(solution)/shard_map/ppermute | solution.py:338
  4.0 0.5 collective-permute-start.3
  4.5 0.2 collective-permute-start.1
  4.6 0.0 copy-done
  4.7 1.2 %constant_dynamic-slice_fusion.3 = (s32[1,50,256]{2,0,1:T(1,128)S(1)}, s32[1,50,256]{2,0,1:T(1,128)S(1)}) fusion(s32[2,50,1024]{2,0,1:T(2,128)} %param.10, s32[]{:T(128)S(6)} %select_n.27, s32[]{:T(128)S(6)} %select_n.29, s32[2,50,1024]{2,0,1:T(2,128)} %param.9), kind=kLoop, calls=%fused_computation.12 | loop fusion | bytes 204808 | tf_op jit(solution)/shard_map/dynamic_slice | solution.py:349
  6.0 0.0 copy-start.2
  6.0 0.9 %copy-done.2 = bf16[64,1024]{1,0:T(8,128)(2,1)S(1)} copy-done((bf16[64,1024]{1,0:T(8,128)(2,1)S(1)}, bf16[64,1024]{1,0:T(8,128)(2,1)}, u32[]{:S(2)}) %copy-start.2) | copy-done | bytes 131096
  6.9 0.4 prepare.1
  7.3 1.5 %constant_dynamic-slice_fusion = (s32[1,50,512]{2,0,1:T(1,128)S(1)}, s32[1,50,512]{2,0,1:T(1,128)S(1)}) fusion(s32[2,50,2048]{2,0,1:T(2,128)} %param.12, s32[]{:T(128)S(6)} %select_n.27, s32[]{:T(128)S(6)} %select_n.30, s32[2,50,2048]{2,0,1:T(2,128)} %param.11), kind=kLoop, calls=%fused_computation.9 | loop fusion | bytes 409608 | tf_op jit(solution)/shard_map/dynamic_slice | solution.py:349
  8.9 0.0 collective-permute-done.5.refs_6_
  8.9 2.5 %collective-permute-done.1.refs_2_ = bf16[64,1024]{1,0:T(8,128)(2,1)S(1)} collective-permute-done((bf16[64,1024]{1,0:T(8,128)(2,1)}, bf16[64,1024]{1,0:T(8,128)(2,1)S(1)}, u32[]{:S(2)}, u32[]{:S(2)}) %collective-permute-start.1) | collective-permute-done | bytes 131104 | tf_op jit(solution)/shard_map/ppermute | solution.py:338
  11.4 0.0 collective-permute-start.2
  11.4 0.0 collective-permute-done.3.refs_4_
  11.4 0.5 collective-permute-start.4
  11.9 0.0 collective-permute-start.6
  11.9 0.0 collective-permute-done.refs_1_
  11.9 0.8 %collective-permute-done.2.refs_3_ = bf16[64,1024]{1,0:T(8,128)(2,1)S(1)} collective-permute-done((bf16[64,1024]{1,0:T(8,128)(2,1)S(1)}, bf16[64,1024]{1,0:T(8,128)(2,1)S(1)}, u32[]{:S(2)}, u32[]{:S(2)}) %collective-permute-start.2) | collective-permute-done | bytes 131104 | tf_op jit(solution)/shard_map/ppermute | solution.py:338
  12.7 0.2 collective-permute-done.4.refs_5_
  12.9 0.3 collective-permute-done.6.refs_7_
  13.2 0.0 copy-start.1
  13.2 0.0 copy-start.3
  13.3 27.3 %mixed.1 = (bf16[144,256]{1,0:T(8,128)(2,1)S(1)}, bf16[144,256]{1,0:T(8,128)(2,1)S(1)}, bf16[144,256]{1,0:T(8,128)(2,1)S(1)}, bf16[144,256]{1,0:T(8,128)(2,1)S(1)}) custom-call(s32[1]{0:T(128)} %bitcast.place_ref, bf16[64,1024]{1,0:T(8,128)(2,1)S(1)} %get-tuple-element.20.refs_0_, bf16[64,1024]{1,0:T(8,128)(2,1)S(1)} %collective-permute-done.refs_1_, ...), custom_call_target="tpu_custom_call" | custom-call | flops 22754099200 | bytes 1048576 | tf_op jit(solution)/shard_map/mixed/pallas_call | solution.py:196
  40.6 1.6 %collective-permute-start.7 = (bf16[144,256]{1,0:T(8,128)(2,1)S(1)}, bf16[144,256]{1,0:T(8,128)(2,1)S(1)}, u32[]{:S(2)}, u32[]{:S(2)}) collective-permute-start(bf16[144,256]{1,0:T(8,128)(2,1)S(1)} %get-tuple-element.27), channel_id=1, source_target_pairs={{0,8},{1,17},{2,10},{3,19},{4,12},{5,21},{6,14},{7,23},{8,0},{9,25... | collective-permute-start | bytes 221192 | tf_op jit(solution)/shard_map/ppermute | solution.py:346
  42.2 1.3 %collective-permute-start.8 = (bf16[144,256]{1,0:T(8,128)(2,1)S(1)}, bf16[144,256]{1,0:T(8,128)(2,1)S(1)}, u32[]{:S(2)}, u32[]{:S(2)}) collective-permute-start(bf16[144,256]{1,0:T(8,128)(2,1)S(1)} %get-tuple-element.29), channel_id=1, source_target_pairs={{0,14},{1,23},{2,12},{3,21},{4,10},{5,19},{6,8},{7,17},{8,6},{9,31... | collective-permute-start | bytes 221192 | tf_op jit(solution)/shard_map/ppermute | solution.py:346
  43.5 2.5 %collective-permute-start.9 = (bf16[144,256]{1,0:T(8,128)(2,1)S(1)}, bf16[144,256]{1,0:T(8,128)(2,1)S(1)}, u32[]{:S(2)}, u32[]{:S(2)}) collective-permute-start(bf16[144,256]{1,0:T(8,128)(2,1)S(1)} %get-tuple-element.30), channel_id=1, source_target_pairs={{0,12},{1,21},{2,14},{3,23},{4,8},{5,17},{6,10},{7,19},{8,4},{9,29... | collective-permute-start | bytes 221192 | tf_op jit(solution)/shard_map/ppermute | solution.py:346
  46.1 0.4 collective-permute-start.10
  46.5 0.0 copy-done.1
  46.5 0.0 copy-done.3
  46.5 2.4 %plain.1.base_ref = f32[64,1024]{1,0:T(8,128)S(1)} custom-call(s32[1]{0:T(128)} %bitcast.place_ref, bf16[64,1024]{1,0:T(8,128)(2,1)S(1)} %get-tuple-element.20.refs_0_, bf16[64,1024]{1,0:T(8,128)(2,1)S(1)} %collective-permute-done.refs_1_, bf16[64,1024]{1,0:T(8,128)(2,1)S(1)} %collective-permute-done.1.refs_2_, ...), custom_call_target="tpu_custom_call" | custom-call | flops 201326592 | bytes 3145728 | tf_op jit(solution)/shard_map/plain/pallas_call | solution.py:252
  48.9 0.0 collective-permute-done.7.refs_3_
  48.9 0.9 %collective-permute-start.14 = (bf16[144,256]{1,0:T(8,128)(2,1)S(1)}, bf16[144,256]{1,0:T(8,128)(2,1)S(1)}, u32[]{:S(2)}, u32[]{:S(2)}) collective-permute-start(bf16[144,256]{1,0:T(8,128)(2,1)S(1)} %collective-permute-done.7.refs_3_), channel_id=1, source_target_pairs={{0,1},{1,0},{2,3},{3,2},{4,5},{5,4},{6,7},{7,6},{8,9},{9,8},{10,11... | collective-permute-start | bytes 221192 | tf_op jit(solution)/shard_map/ppermute | solution.py:338
  49.9 0.0 collective-permute-done.8.refs_0_
  49.9 0.1 collective-permute-start.11
  50.0 0.7 %collective-permute-done.9.refs_1_ = bf16[144,256]{1,0:T(8,128)(2,1)S(1)} collective-permute-done((bf16[144,256]{1,0:T(8,128)(2,1)S(1)}, bf16[144,256]{1,0:T(8,128)(2,1)S(1)}, u32[]{:S(2)}, u32[]{:S(2)}) %collective-permute-start.9) | collective-permute-done | bytes 73760 | tf_op jit(solution)/shard_map/ppermute | solution.py:346
  50.7 0.0 collective-permute-start.12
  50.7 0.7 %collective-permute-done.10.refs_2_ = bf16[144,256]{1,0:T(8,128)(2,1)S(1)} collective-permute-done((bf16[144,256]{1,0:T(8,128)(2,1)S(1)}, bf16[144,256]{1,0:T(8,128)(2,1)S(1)}, u32[]{:S(2)}, u32[]{:S(2)}) %collective-permute-start.10) | collective-permute-done | bytes 73760 | tf_op jit(solution)/shard_map/ppermute | solution.py:346
  51.4 1.3 %collective-permute-start.13 = (bf16[144,256]{1,0:T(8,128)(2,1)S(1)}, bf16[144,256]{1,0:T(8,128)(2,1)S(1)}, u32[]{:S(2)}, u32[]{:S(2)}) collective-permute-start(bf16[144,256]{1,0:T(8,128)(2,1)S(1)} %collective-permute-done.10.refs_2_), channel_id=1, source_target_pairs={{0,1},{1,0},{2,3},{3,2},{4,5},{5,4},{6,7},{7,6},{8,9},{9,8},{10,11... | collective-permute-start | bytes 221192 | tf_op jit(solution)/shard_map/ppermute | solution.py:338
  52.7 0.0 collective-permute-done.14.refs_7_
  52.7 0.0 collective-permute-done.11.refs_4_
  52.7 0.0 collective-permute-done.12.refs_5_
  52.7 0.9 %collective-permute-done.13.refs_6_ = bf16[144,256]{1,0:T(8,128)(2,1)S(1)} collective-permute-done((bf16[144,256]{1,0:T(8,128)(2,1)S(1)}, bf16[144,256]{1,0:T(8,128)(2,1)S(1)}, u32[]{:S(2)}, u32[]{:S(2)}) %collective-permute-start.13) | collective-permute-done | bytes 73760 | tf_op jit(solution)/shard_map/ppermute | solution.py:338
  53.6 1.5 %add.76 = f32[64,1024]{1,0:T(8,128)} custom-call(s32[1]{0:T(128)} %bitcast.place_ref, f32[64,1024]{1,0:T(8,128)S(1)} %plain.1.base_ref, bf16[144,256]{1,0:T(8,128)(2,1)S(1)} %collective-permute-done.8.refs_0_, bf16[144,256]{1,0:T(8,128)(2,1)S(1)} %collective-permute-done.9.refs_1_, bf16[144,256]{1,0:T(8,128)(2,1)S(1)} %collective-permute-done.10.refs_2_, ...), custom_call_target="tpu_custom_call" | custom-call | tf_op jit(solution)/shard_map/add/pallas_call | solution.py:304
  (4 shorter events, 0.1 us)
Async XLA Ops:
  0.0 4.6 %copy-start = (bf16[2,50,50]{2,0,1:T(2,128)(2,1)S(1)}, bf16[2,50,50]{2,0,1:T(2,128)(2,1)}, u32[]{:S(2)}) copy-start(bf16[2,50,50]{2,0,1:T(2,128)(2,1)} %param.13) | copy-start | bytes 30004
  0.0 11.9 %collective-permute-start = (bf16[64,1024]{1,0:T(8,128)(2,1)}, bf16[64,1024]{1,0:T(8,128)(2,1)S(1)}, u32[]{:S(2)}, u32[]{:S(2)}) collective-permute-start(bf16[64,1024]{1,0:T(8,128)(2,1)} %rows_ref.1), channel_id=1, source_target_pairs={{0,1},{1,0},{2,3},{3,2},{4,5},{5,4},{6,7},{7,6},{8,9},{9,8},{10,11... | collective-permute-start | bytes 393224 | tf_op jit(solution)/shard_map/ppermute | solution.py:338
  0.5 8.4 %collective-permute-start.5 = (bf16[64,1024]{1,0:T(8,128)(2,1)}, bf16[64,1024]{1,0:T(8,128)(2,1)S(1)}, u32[]{:S(2)}, u32[]{:S(2)}) collective-permute-start(bf16[64,1024]{1,0:T(8,128)(2,1)} %rows_ref.1), channel_id=1, source_target_pairs={{0,6},{1,7},{2,4},{3,5},{4,2},{5,3},{6,0},{7,1},{8,14},{9,15},{10,... | collective-permute-start | bytes 393224 | tf_op jit(solution)/shard_map/ppermute | solution.py:338
  4.0 7.4 %collective-permute-start.3 = (bf16[64,1024]{1,0:T(8,128)(2,1)}, bf16[64,1024]{1,0:T(8,128)(2,1)S(1)}, u32[]{:S(2)}, u32[]{:S(2)}) collective-permute-start(bf16[64,1024]{1,0:T(8,128)(2,1)} %rows_ref.1), channel_id=1, source_target_pairs={{0,4},{1,5},{2,6},{3,7},{4,0},{5,1},{6,2},{7,3},{8,12},{9,13},{10,... | collective-permute-start | bytes 393224 | tf_op jit(solution)/shard_map/ppermute | solution.py:338
  4.5 6.9 %collective-permute-start.1 = (bf16[64,1024]{1,0:T(8,128)(2,1)}, bf16[64,1024]{1,0:T(8,128)(2,1)S(1)}, u32[]{:S(2)}, u32[]{:S(2)}) collective-permute-start(bf16[64,1024]{1,0:T(8,128)(2,1)} %rows_ref.1), channel_id=1, source_target_pairs={{0,2},{1,3},{2,0},{3,1},{4,6},{5,7},{6,4},{7,5},{8,10},{9,11},{10,... | collective-permute-start | bytes 393224 | tf_op jit(solution)/shard_map/ppermute | solution.py:338
  6.0 0.9 %copy-start.2 = (bf16[64,1024]{1,0:T(8,128)(2,1)S(1)}, bf16[64,1024]{1,0:T(8,128)(2,1)}, u32[]{:S(2)}) copy-start(bf16[64,1024]{1,0:T(8,128)(2,1)} %rows_ref.1) | copy-start | bytes 393220
  11.4 1.3 %collective-permute-start.2 = (bf16[64,1024]{1,0:T(8,128)(2,1)S(1)}, bf16[64,1024]{1,0:T(8,128)(2,1)S(1)}, u32[]{:S(2)}, u32[]{:S(2)}) collective-permute-start(bf16[64,1024]{1,0:T(8,128)(2,1)S(1)} %collective-permute-done.1.refs_2_), channel_id=1, source_target_pairs={{0,1},{1,0},{2,3},{3,2},{4,5},{5,4},{6,7},{7,6},{8,9},{9,8},{10,11... | collective-permute-start | bytes 393224 | tf_op jit(solution)/shard_map/ppermute | solution.py:338
  11.4 1.5 %collective-permute-start.4 = (bf16[64,1024]{1,0:T(8,128)(2,1)S(1)}, bf16[64,1024]{1,0:T(8,128)(2,1)S(1)}, u32[]{:S(2)}, u32[]{:S(2)}) collective-permute-start(bf16[64,1024]{1,0:T(8,128)(2,1)S(1)} %collective-permute-done.3.refs_4_), channel_id=1, source_target_pairs={{0,1},{1,0},{2,3},{3,2},{4,5},{5,4},{6,7},{7,6},{8,9},{9,8},{10,11... | collective-permute-start | bytes 393224 | tf_op jit(solution)/shard_map/ppermute | solution.py:338
  11.9 1.3 %collective-permute-start.6 = (bf16[64,1024]{1,0:T(8,128)(2,1)S(1)}, bf16[64,1024]{1,0:T(8,128)(2,1)S(1)}, u32[]{:S(2)}, u32[]{:S(2)}) collective-permute-start(bf16[64,1024]{1,0:T(8,128)(2,1)S(1)} %collective-permute-done.5.refs_6_), channel_id=1, source_target_pairs={{0,1},{1,0},{2,3},{3,2},{4,5},{5,4},{6,7},{7,6},{8,9},{9,8},{10,11... | collective-permute-start | bytes 393224 | tf_op jit(solution)/shard_map/ppermute | solution.py:338
  13.2 33.2 %copy-start.1 = (bf16[1024,1024]{1,0:T(8,128)(2,1)S(1)}, bf16[1024,1024]{1,0:T(8,128)(2,1)}, u32[]{:S(2)}) copy-start(bf16[1024,1024]{1,0:T(8,128)(2,1)} %refs_9_.1) | copy-start | bytes 6291460
  13.2 33.2 %copy-start.3 = (bf16[64,512]{1,0:T(8,128)(2,1)S(1)}, bf16[64,512]{1,0:T(8,128)(2,1)}, u32[]{:S(2)}) copy-start(bf16[64,512]{1,0:T(8,128)(2,1)} %refs_8_.1) | copy-start | bytes 196612
  40.6 8.3 %collective-permute-start.7 = (bf16[144,256]{1,0:T(8,128)(2,1)S(1)}, bf16[144,256]{1,0:T(8,128)(2,1)S(1)}, u32[]{:S(2)}, u32[]{:S(2)}) collective-permute-start(bf16[144,256]{1,0:T(8,128)(2,1)S(1)} %get-tuple-element.27), channel_id=1, source_target_pairs={{0,8},{1,17},{2,10},{3,19},{4,12},{5,21},{6,14},{7,23},{8,0},{9,25... | collective-permute-start | bytes 221192 | tf_op jit(solution)/shard_map/ppermute | solution.py:346
  42.2 7.7 %collective-permute-start.8 = (bf16[144,256]{1,0:T(8,128)(2,1)S(1)}, bf16[144,256]{1,0:T(8,128)(2,1)S(1)}, u32[]{:S(2)}, u32[]{:S(2)}) collective-permute-start(bf16[144,256]{1,0:T(8,128)(2,1)S(1)} %get-tuple-element.29), channel_id=1, source_target_pairs={{0,14},{1,23},{2,12},{3,21},{4,10},{5,19},{6,8},{7,17},{8,6},{9,31... | collective-permute-start | bytes 221192 | tf_op jit(solution)/shard_map/ppermute | solution.py:346
  43.5 7.1 %collective-permute-start.9 = (bf16[144,256]{1,0:T(8,128)(2,1)S(1)}, bf16[144,256]{1,0:T(8,128)(2,1)S(1)}, u32[]{:S(2)}, u32[]{:S(2)}) collective-permute-start(bf16[144,256]{1,0:T(8,128)(2,1)S(1)} %get-tuple-element.30), channel_id=1, source_target_pairs={{0,12},{1,21},{2,14},{3,23},{4,8},{5,17},{6,10},{7,19},{8,4},{9,29... | collective-permute-start | bytes 221192 | tf_op jit(solution)/shard_map/ppermute | solution.py:346
  46.1 5.4 %collective-permute-start.10 = (bf16[144,256]{1,0:T(8,128)(2,1)S(1)}, bf16[144,256]{1,0:T(8,128)(2,1)S(1)}, u32[]{:S(2)}, u32[]{:S(2)}) collective-permute-start(bf16[144,256]{1,0:T(8,128)(2,1)S(1)} %get-tuple-element.31), channel_id=1, source_target_pairs={{0,10},{1,19},{2,8},{3,17},{4,14},{5,23},{6,12},{7,21},{8,2},{9,27... | collective-permute-start | bytes 221192 | tf_op jit(solution)/shard_map/ppermute | solution.py:346
  48.9 3.8 %collective-permute-start.14 = (bf16[144,256]{1,0:T(8,128)(2,1)S(1)}, bf16[144,256]{1,0:T(8,128)(2,1)S(1)}, u32[]{:S(2)}, u32[]{:S(2)}) collective-permute-start(bf16[144,256]{1,0:T(8,128)(2,1)S(1)} %collective-permute-done.7.refs_3_), channel_id=1, source_target_pairs={{0,1},{1,0},{2,3},{3,2},{4,5},{5,4},{6,7},{7,6},{8,9},{9,8},{10,11... | collective-permute-start | bytes 221192 | tf_op jit(solution)/shard_map/ppermute | solution.py:338
  49.9 2.9 %collective-permute-start.11 = (bf16[144,256]{1,0:T(8,128)(2,1)S(1)}, bf16[144,256]{1,0:T(8,128)(2,1)S(1)}, u32[]{:S(2)}, u32[]{:S(2)}) collective-permute-start(bf16[144,256]{1,0:T(8,128)(2,1)S(1)} %collective-permute-done.8.refs_0_), channel_id=1, source_target_pairs={{0,1},{1,0},{2,3},{3,2},{4,5},{5,4},{6,7},{7,6},{8,9},{9,8},{10,11... | collective-permute-start | bytes 221192 | tf_op jit(solution)/shard_map/ppermute | solution.py:338
  50.7 2.1 %collective-permute-start.12 = (bf16[144,256]{1,0:T(8,128)(2,1)S(1)}, bf16[144,256]{1,0:T(8,128)(2,1)S(1)}, u32[]{:S(2)}, u32[]{:S(2)}) collective-permute-start(bf16[144,256]{1,0:T(8,128)(2,1)S(1)} %collective-permute-done.9.refs_1_), channel_id=1, source_target_pairs={{0,1},{1,0},{2,3},{3,2},{4,5},{5,4},{6,7},{7,6},{8,9},{9,8},{10,11... | collective-permute-start | bytes 221192 | tf_op jit(solution)/shard_map/ppermute | solution.py:338
  51.4 2.2 %collective-permute-start.13 = (bf16[144,256]{1,0:T(8,128)(2,1)S(1)}, bf16[144,256]{1,0:T(8,128)(2,1)S(1)}, u32[]{:S(2)}, u32[]{:S(2)}) collective-permute-start(bf16[144,256]{1,0:T(8,128)(2,1)S(1)} %collective-permute-done.10.refs_2_), channel_id=1, source_target_pairs={{0,1},{1,0},{2,3},{3,2},{4,5},{5,4},{6,7},{7,6},{8,9},{9,8},{10,11... | collective-permute-start | bytes 221192 | tf_op jit(solution)/shard_map/ppermute | solution.py:338
